TPU v7x, 1024 devices: a whole 4x4x32 slice. The times are simulated.
1024 devices in a mesh: section: 64 (over y, x, z_hi, core), dp: 16 (over z_lo).
Axes of the slice: x: 4, y: 4, z: 32 (z_hi: 2, z_lo: 16; z = z_hi * 16 + z_lo), core: 2. Of those that a mesh axis runs over, the one named last changes fastest.
Arguments:
- patches: bfloat16 [16, 4096, 3200], P('dp', 'section'), may hold values from -6 to 6
- live: int32 [16, 64], P('dp'), may hold values from 1 to 64, 1536 in all within a row
- rounds: int32 [16, 64], P('dp'), may hold values from 0 to 63, each once within a row
- ln_gain: float32 [3200], replicated, may hold values from 0.1 to 1.9
- fc1_weight: bfloat16 [3200, 10240], P(None, 'dp'), may hold values from -0.109375 to 0.109375
- fc1_bias: float32 [10240], P('dp'), may hold values from -3 to 3
- fc2_weight: bfloat16 [10240, 3200], P('dp'), may hold values from -0.0625 to 0.0625
- fc2_bias: float32 [3200], replicated, may hold values from -3 to 3
- layer_scale: float32 [3200], replicated, may hold values from 0.5 to 2
Outputs:
- encoded: bfloat16 [16, 1536, 3200], P('dp', 'section')
Inputs may be any that keep to these rules, and one draw needn't show every extreme that they name: In each row d the 64 counts sum to 1536, and some device holds exactly 64 live rows. Each rounds[d] lists every section index exactly once.
All inputs are finite; a program needn't handle non-finite values.
Results may differ from a plain program's by a relative error of at most 0.017.
Values may be sent and summed in bfloat16 or wider, within the bound.
No kernel may reach another device: no remote copies, remote signals or barrier semaphores. Data moves between devices by JAX's collectives and lax.ppermute only.
A program may use at most 32 MiB of HBM per device.

v0:
```python
import jax
import jax.numpy as jnp
from jax import lax
from jax.sharding import PartitionSpec as P


def per_device(
    patches, live, rounds, ln_gain, fc1_weight, fc1_bias, fc2_weight, fc2_bias, layer_scale
):
    section_count = lax.axis_size("section")
    my_section = lax.axis_index("section")
    slot_count = patches.shape[1]
    keep_rows = fc2_bias.shape[0] * 0 + 3 * section_count // 8
    width = patches.shape[2]
    live_row = live[0]
    order_row = rounds[0]
    section_ids = jnp.arange(section_count, dtype=jnp.int32)
    ends = jnp.cumsum(live_row)
    starts = ends - live_row
    is_mine = section_ids == my_section
    my_start = jnp.sum(jnp.where(is_mine, starts, 0))
    my_live = jnp.sum(jnp.where(is_mine, live_row, 0))
    slot_ids = jnp.arange(slot_count, dtype=jnp.int32)
    position = (my_start + slot_ids) % section_count
    target = jnp.sum(
        jnp.where(position[:, None] == section_ids[None, :], order_row[None, :], 0), axis=1
    )
    send_index = jnp.where(slot_ids < my_live, target, section_count)
    send_rows = (
        jnp.zeros((section_count, width), jnp.bfloat16).at[send_index].set(patches[0], mode="drop")
    )
    received = lax.all_to_all(send_rows, "section", split_axis=0, concat_axis=0, tiled=True)
    my_position = jnp.sum(jnp.where(order_row == my_section, section_ids, 0))
    keep_ids = jnp.arange(keep_rows, dtype=jnp.int32)
    row_global = keep_ids * section_count + my_position
    source_ids = jnp.sum((ends[None, :] <= row_global[:, None]).astype(jnp.int32), axis=1)
    routed = received[source_ids]
    rows32 = routed.astype(jnp.float32)
    mean = jnp.mean(rows32, axis=1, keepdims=True)
    centered = rows32 - mean
    var = jnp.mean(centered * centered, axis=1, keepdims=True)
    normed = (centered * lax.rsqrt(var + 1e-06) * ln_gain).astype(jnp.bfloat16)
    gathered = lax.all_gather(normed, "dp", axis=0, tiled=True)
    pre = jnp.dot(gathered, fc1_weight, preferred_element_type=jnp.float32) + fc1_bias
    hidden = jax.nn.gelu(pre, approximate=False).astype(jnp.bfloat16)
    summed = lax.psum_scatter(
        jnp.dot(hidden, fc2_weight, preferred_element_type=jnp.float32).astype(jnp.bfloat16),
        "dp",
        scatter_dimension=0,
        tiled=True,
    ).astype(jnp.float32)
    encoded = (rows32 + layer_scale * (summed + fc2_bias)).astype(jnp.bfloat16)
    return encoded[None]


def solution(mesh):
    placed = (
        P("dp", "section", None),
        P("dp", None),
        P("dp", None),
        P(),
        P(None, "dp"),
        P("dp"),
        P("dp", None),
        P(),
        P(),
    )
    return jax.shard_map(
        per_device, mesh=mesh, in_specs=placed, out_specs=P("dp", "section", None), check_vma=False
    )
```

profile of v0, /device:TPU:4, one launch (start us, length us, event | category | flops | bytes accessed | tf_op | source)
XLA Modules:
  0.0 518.3 jit_solution(7559957463068673175)
XLA Ops:
  6.5 0.0 copy-start
  6.5 0.0 copy-start.1
  6.5 0.0 copy-start.4
  6.5 0.8 copy.15
  7.3 0.1 reduce-window.8
  7.4 0.1 reduce
  7.5 1.4 fusion.51
  9.0 0.7 and_select_fusion
  9.7 0.8 select_reduce_fusion
  10.5 0.7 fusion.56
  11.2 0.0 copy-done
  11.2 1.3 scatter_custom_fusion
  12.5 0.5 broadcast.136
  13.0 0.9 reduce.1
  13.8 1.2 reshape.120
  15.1 34.5 %all-to-all-start = ((bf16[64,2,1600]{2,1,0:T(2,128)(2,1)}), bf16[64,2,1600]{2,1,0:T(2,128)(2,1)S(1)}, u32[]{:S(2)}, u32[]{:S(2)}) async-start(bf16[64,2,1600]{2,1,0:T(2,128)(2,1)} %reshape.120), calls=%async_computation | async-start | bytes 851968 | tf_op jit(solution)/shard_map/all_to_all | solution.py:32
  49.6 0.0 all-gather.2.cloned.1.call-start
  49.6 0.7 multiply_add_fusion
  50.3 0.2 convert_reduce_fusion.1
  50.5 27.6 %all-to-all-done = bf16[64,2,1600]{2,1,0:T(2,128)(2,1)S(1)} async-done(((bf16[64,2,1600]{2,1,0:T(2,128)(2,1)}), bf16[64,2,1600]{2,1,0:T(2,128)(2,1)S(1)}, u32[]{:S(2)}, u32[]{:S(2)}) %all-to-all-start) | async-done | bytes 409632 | tf_op jit(solution)/shard_map/all_to_all | solution.py:32
  78.1 0.6 reshape.121
  78.8 0.7 gather_fusion
  79.4 0.1 convert_reduce_fusion
  79.6 0.2 fusion.45
  79.8 0.0 copy-done.1
  79.8 0.8 fusion.47
  80.6 0.0 all-gather.2.cloned.1.call-update
  80.6 0.0 copy-start.2
  80.6 0.0 copy-start.3
  80.6 0.0 reduce-scatter.5.cloned.1.call-start
  80.7 207.8 %all-gather.2.cloned.1.call-done = bf16[384,3200]{1,0:T(8,128)(2,1)} async-done(((bf16[24,3200]{1,0:T(8,128)(2,1)}), bf16[384,3200]{1,0:T(8,128)(2,1)}) %all-gather.2.cloned.1.call-update) | async-done | bytes 2457616 | tf_op jit(solution)/shard_map/all_gather | solution.py:43
  288.5 0.0 copy-done.4
  288.5 12.4 %convolution_convert_fusion = bf16[384,3200]{1,0:T(8,128)(2,1)} fusion(bf16[640,3200]{1,0:T(8,128)(2,1)} %param.15, bf16[384,3200]{1,0:T(8,128)(2,1)} %all-gather.2.cloned.1.call-done, bf16[3200,640]{1,0:T(8,128)(2,1)} %param.13, f32[640]{0:T(1024)S(1)} %copy-done.4), kind=kOutput, calls=%fused_computation.2 | convolution fusion | flops 3163176960 | bytes 13109760 | tf_op jit(solution)/shard_map/dot_general | solution.py:47
  300.9 0.0 reduce-scatter.5.cloned.1.call-update
  300.9 208.9 %reduce-scatter.5.cloned.1.call-done = bf16[24,3200]{1,0:T(8,128)(2,1)} async-done(((bf16[384,3200]{1,0:T(8,128)(2,1)}), bf16[24,3200]{1,0:T(8,128)(2,1)}) %reduce-scatter.5.cloned.1.call-update) | async-done | bytes 153616
  509.8 0.0 copy-done.2
  509.8 0.0 copy-done.3
  509.8 1.6 fusion.50
  (5 shorter events, 0.1 us)
Async XLA Ops:
  6.5 4.7 copy-start
  6.5 73.3 %copy-start.1 = (f32[3200]{0:T(1024)S(1)}, f32[3200]{0:T(1024)}, u32[]{:S(2)}) copy-start(f32[3200]{0:T(1024)} %param.12) | copy-start | bytes 38404
  6.5 282.0 %copy-start.4 = (f32[640]{0:T(1024)S(1)}, f32[640]{0:T(1024)}, u32[]{:S(2)}) copy-start(f32[640]{0:T(1024)} %param.14) | copy-start | bytes 7684
  15.1 63.0 %all-to-all-start = ((bf16[64,2,1600]{2,1,0:T(2,128)(2,1)}), bf16[64,2,1600]{2,1,0:T(2,128)(2,1)S(1)}, u32[]{:S(2)}, u32[]{:S(2)}) async-start(bf16[64,2,1600]{2,1,0:T(2,128)(2,1)} %reshape.120), calls=%async_computation | async-start | bytes 851968 | tf_op jit(solution)/shard_map/all_to_all | solution.py:32
  49.6 238.9 %all-gather.2.cloned.1.call-start = ((), (), s32[]{:S(2)}) async-start(), calls=%async_computation.2 | async-start | bytes 2611200 | tf_op jit(solution)/shard_map/all_gather | solution.py:43
  80.6 429.2 %copy-start.2 = (f32[3200]{0:T(1024)S(1)}, f32[3200]{0:T(1024)}, u32[]{:S(2)}) copy-start(f32[3200]{0:T(1024)} %param.16) | copy-start | bytes 38404
  80.6 429.2 %copy-start.3 = (f32[3200]{0:T(1024)S(1)}, f32[3200]{0:T(1024)}, u32[]{:S(2)}) copy-start(f32[3200]{0:T(1024)} %param.17) | copy-start | bytes 38404
  80.6 429.2 %reduce-scatter.5.cloned.1.call-start = ((), (), s32[]{:S(2)}) async-start(), calls=%async_computation.3 | async-start | bytes 2611200
Sparse Core Ops, SparseCore 0:
  80.7 207.7 all-gather.1
  301.0 208.7 reduce-scatter.4
where the time goes:
time: 519 us; the launch traced here: 518 us
  waiting for transfers between devices  444 us (86%)
  starting transfers between devices  34.6 us (7%)
  between operations  13.5 us (3%)
  matrix products  12.4 us (2%)
  other arithmetic  8.36 us (2%)
    unnamed x3, waiting for transfers between devices  209 us
    all_gather x1, waiting for transfers between devices, per_device(): gathered = lax.all_gather(normed, 'dp', axis=0, tiled=True)  208 us
    all_to_all x1, starting transfers between devices, per_device(): lax.all_to_all(send_rows, 'section', split_axis=0, concat_axis=0, tiled=T...  34.5 us
    all_to_all x1, waiting for transfers between devices, per_device(): lax.all_to_all(send_rows, 'section', split_axis=0, concat_axis=0, tiled=T...  27.6 us
    dot_general x1, matrix products, per_device(): jnp.dot(hidden, fc2_weight, preferred_element_type=jnp.float32)  12.4 us
  transfers between devices with their start and end apart: 3, of which 3 were waited for; matrix products, arithmetic and copies ran while one was open for 0% of the time, Pallas kernels for 0%

commit v1 on v0

v1 whole, which is shorter than its diff:
```python
import jax
import jax.numpy as jnp
from jax import lax
from jax.sharding import PartitionSpec as P

AXES = ("section", "dp")


def coordinates(sections, dps):
    for section in range(sections):
        for dp in range(dps):
            yield section // 4, (section // 2 % 2) * dps + dp, section % 2, section * dps + dp


def shift_pairs(sections, dps, hops):
    ring = 2 * dps
    pairs = []
    for column, z, core, flat in coordinates(sections, dps):
        there = (z + (hops if core == 0 else -hops)) % ring
        section = (column * 2 + there // dps) * 2 + core
        pairs.append((flat, section * dps + there % dps))
    return pairs


def swap_pairs(sections, dps):
    return [(s * dps + d, (s ^ 1) * dps + d) for s in range(sections) for d in range(dps)]


def route(patches, live_row, order_row, my_section, section_count, keep_rows):
    slot_count = patches.shape[0]
    width = patches.shape[1]
    section_ids = jnp.arange(section_count, dtype=jnp.int32)
    ends = jnp.cumsum(live_row)
    starts = ends - live_row
    is_mine = section_ids == my_section
    my_start = jnp.sum(jnp.where(is_mine, starts, 0))
    my_live = jnp.sum(jnp.where(is_mine, live_row, 0))
    slot_ids = jnp.arange(slot_count, dtype=jnp.int32)
    position = (my_start + slot_ids) % section_count
    target = jnp.sum(
        jnp.where(position[:, None] == section_ids[None, :], order_row[None, :], 0), axis=1
    )
    send_index = jnp.where(slot_ids < my_live, target, section_count)
    send_rows = (
        jnp.zeros((section_count, width), jnp.bfloat16).at[send_index].set(patches, mode="drop")
    )
    received = lax.all_to_all(send_rows, "section", split_axis=0, concat_axis=0, tiled=True)
    my_position = jnp.sum(jnp.where(order_row == my_section, section_ids, 0))
    keep_ids = jnp.arange(keep_rows, dtype=jnp.int32)
    row_global = keep_ids * section_count + my_position
    source_ids = jnp.sum((ends[None, :] <= row_global[:, None]).astype(jnp.int32), axis=1)
    return received[source_ids]


def per_device(
    patches, live, rounds, ln_gain, fc1_weight, fc1_bias, fc2_weight, fc2_bias, layer_scale
):
    sections = lax.axis_size("section")
    dps = lax.axis_size("dp")
    my_section = lax.axis_index("section")
    up = my_section % 2 == 0
    keep_rows = 3 * sections // 8

    def send(value, hops):
        return lax.ppermute(value, AXES, shift_pairs(sections, dps, hops))

    def swap(value):
        return lax.ppermute(value, AXES, swap_pairs(sections, dps))

    routed = route(patches[0], live[0], rounds[0], my_section, sections, keep_rows)
    rows32 = routed.astype(jnp.float32)
    mean = jnp.mean(rows32, axis=1, keepdims=True)
    centered = rows32 - mean
    var = jnp.mean(centered * centered, axis=1, keepdims=True)
    normed = (centered * lax.rsqrt(var + 1e-06) * ln_gain).astype(jnp.bfloat16)
    other = swap(normed)
    even = jnp.where(up, normed, other)
    odd = jnp.where(up, other, normed)

    def gather(own):
        far3 = send(own, 3)
        far6 = send(far3, 3)
        level0 = jnp.concatenate([own, far3, far6], axis=0)
        level1 = send(level0, 1)
        level2 = send(level1, 1)
        return level0, level1, level2

    def encode(levels):
        level0, level1, level2 = levels
        n = level0.shape[0] // 3
        ends = jnp.where(up, level2[2 * n :], level0[:n])
        rows = jnp.concatenate([level0[n:], level1, level2[: 2 * n], ends], axis=0)
        pre = jnp.dot(rows, fc1_weight, preferred_element_type=jnp.float32) + fc1_bias
        hidden = jax.nn.gelu(pre, approximate=False).astype(jnp.bfloat16)
        return jnp.dot(hidden, fc2_weight, preferred_element_type=jnp.float32).astype(jnp.bfloat16)

    def scatter(part):
        n = part.shape[0] // 8
        ends = part[7 * n :]
        none = jnp.zeros_like(ends)
        sum0 = jnp.concatenate([jnp.where(up, none, ends), part[: 2 * n]], axis=0)
        sum1 = part[2 * n : 5 * n]
        sum2 = jnp.concatenate([part[5 * n : 7 * n], jnp.where(up, ends, none)], axis=0)

        def add(a, b):
            return (a.astype(jnp.float32) + b.astype(jnp.float32)).astype(jnp.bfloat16)

        total = add(send(sum2, -1), sum1)
        total = add(send(total, -1), sum0)
        back = add(send(total[2 * n :], -3), total[n : 2 * n])
        return add(send(back, -3), total[:n])

    sum_even = scatter(encode(gather(even)))
    sum_odd = scatter(encode(gather(odd)))

    mine = jnp.where(up, sum_even, sum_odd)
    theirs = jnp.where(up, sum_odd, sum_even)
    summed = mine.astype(jnp.float32) + swap(theirs).astype(jnp.float32)
    encoded = (rows32 + layer_scale * (summed + fc2_bias)).astype(jnp.bfloat16)
    return encoded[None]


def solution(mesh):
    placed = (
        P("dp", "section", None),
        P("dp", None),
        P("dp", None),
        P(),
        P(None, "dp"),
        P("dp"),
        P("dp", None),
        P(),
        P(),
    )
    return jax.shard_map(
        per_device, mesh=mesh, in_specs=placed, out_specs=P("dp", "section", None), check_vma=False
    )
```

time: 519 us -> 238 us (0.46)
  the two profiles are of different devices: /device:TPU:4 before, /device:TPU:1 now
where the time goes in v1:
time: 238 us; the launch traced here: 237 us
  starting transfers between devices  108 us (45%)
  waiting for transfers between devices  87.9 us (37%)
  matrix products  15 us (6%)
  local copies, waits for them, and re-layouts  13 us (5%)
  other arithmetic  12.2 us (5%)
    ppermute x16, starting transfers between devices, send(): return lax.ppermute(value, AXES, shift_pairs(sections, dps, hops))  61 us
    ppermute x16, waiting for transfers between devices, send(): return lax.ppermute(value, AXES, shift_pairs(sections, dps, hops))  55.8 us
    all_to_all x1, starting transfers between devices, route(): lax.all_to_all(send_rows, 'section', split_axis=0, concat_axis=0, tiled=T...  35.5 us
    all_to_all x1, waiting for transfers between devices, route(): lax.all_to_all(send_rows, 'section', split_axis=0, concat_axis=0, tiled=T...  30.2 us
    dot_general x2, matrix products, encode(): jnp.dot(hidden, fc2_weight, preferred_element_type=jnp.float32)  15 us
    ppermute x2, starting transfers between devices, swap(): return lax.ppermute(value, AXES, swap_pairs(sections, dps))  11.7 us
    unnamed x21, local copies, waits for them, and re-layouts  8.63 us
  transfers between devices with their start and end apart: 19, of which 16 were waited for; matrix products, arithmetic and copies ran while one was open for 7% of the time, Pallas kernels for 0%

profile of v1, /device:TPU:1, one launch (start us, length us, event | category | flops | bytes accessed | tf_op | source)
XLA Modules:
  0.0 236.7 jit_solution(10708236503409212089)
XLA Ops:
  0.0 0.8 copy.15
  1.0 1.4 fusion.94
  2.4 0.7 and_select_fusion
  3.1 0.8 select_reduce_fusion
  4.0 0.7 fusion.99
  4.7 1.3 scatter_custom_fusion
  5.9 0.5 broadcast.497
  6.4 0.9 reduce.1
  7.3 1.2 reshape.119
  8.5 35.5 %all-to-all-start = ((bf16[64,2,1600]{2,1,0:T(2,128)(2,1)}), bf16[64,2,1600]{2,1,0:T(2,128)(2,1)S(1)}, u32[]{:S(2)}, u32[]{:S(2)}) async-start(bf16[64,2,1600]{2,1,0:T(2,128)(2,1)} %reshape.119), calls=%async_computation | async-start | bytes 851968 | tf_op jit(solution)/shard_map/all_to_all | solution.py:47
  44.0 0.7 multiply_add_fusion
  44.9 30.2 %all-to-all-done = bf16[64,2,1600]{2,1,0:T(2,128)(2,1)S(1)} async-done(((bf16[64,2,1600]{2,1,0:T(2,128)(2,1)}), bf16[64,2,1600]{2,1,0:T(2,128)(2,1)S(1)}, u32[]{:S(2)}, u32[]{:S(2)}) %all-to-all-start) | async-done | bytes 409632 | tf_op jit(solution)/shard_map/all_to_all | solution.py:47
  75.1 0.6 reshape.120
  75.8 0.7 gather_fusion
  76.6 0.2 fusion.24
  77.0 2.6 %collective-permute-start = (bf16[24,3200]{1,0:T(8,128)(2,1)S(1)}, bf16[24,3200]{1,0:T(8,128)(2,1)S(1)}, u32[]{:S(2)}, u32[]{:S(2)}) collective-permute-start(bf16[24,3200]{1,0:T(8,128)(2,1)S(1)} %fusion.26), channel_id=1, source_target_pairs={{0,16},{1,17},{2,18},{3,19},{4,20},{5,21},{6,22},{7,23},{8,24},{9,... | collective-permute-start | bytes 460808 | tf_op jit(solution)/shard_map/ppermute | solution.py:68
  79.5 1.0 collective-permute-done
  80.7 1.9 collective-permute-start.1
  82.6 20.6 %collective-permute-start.9 = (bf16[24,3200]{1,0:T(8,128)(2,1)S(1)}, bf16[24,3200]{1,0:T(8,128)(2,1)S(1)}, u32[]{:S(2)}, u32[]{:S(2)}) collective-permute-start(bf16[24,3200]{1,0:T(8,128)(2,1)S(1)} %get-tuple-element.15), channel_id=1, source_target_pairs={{0,3},{1,4},{2,5},{3,6},{4,7},{5,8},{6,9},{7,10},{8,11},{9,12},{10... | collective-permute-start | bytes 460808 | tf_op jit(solution)/shard_map/ppermute | solution.py:65
  103.2 12.8 %collective-permute-done.1 = bf16[24,3200]{1,0:T(8,128)(2,1)S(1)} collective-permute-done((bf16[24,3200]{1,0:T(8,128)(2,1)S(1)}, bf16[24,3200]{1,0:T(8,128)(2,1)S(1)}, u32[]{:S(2)}, u32[]{:S(2)}) %collective-permute-start.1) | collective-permute-done | bytes 153632 | tf_op jit(solution)/shard_map/ppermute | solution.py:65
  116.0 0.7 constant_dynamic-update-slice_fusion.2
  116.7 1.9 collective-permute-start.2
  118.6 0.7 constant_dynamic-update-slice_fusion.5
  119.3 1.9 collective-permute-start.10
  121.2 9.4 %collective-permute-done.2 = bf16[24,3200]{1,0:T(8,128)(2,1)S(1)} collective-permute-done((bf16[24,3200]{1,0:T(8,128)(2,1)S(1)}, bf16[24,3200]{1,0:T(8,128)(2,1)S(1)}, u32[]{:S(2)}, u32[]{:S(2)}) %collective-permute-start.2) | collective-permute-done | bytes 153632 | tf_op jit(solution)/shard_map/ppermute | solution.py:65
  130.6 1.9 collective-permute-start.3
  132.6 8.8 %collective-permute-start.11 = (bf16[72,3200]{1,0:T(8,128)(2,1)S(1)}, bf16[72,3200]{1,0:T(8,128)(2,1)S(1)}, u32[]{:S(2)}, u32[]{:S(2)}) collective-permute-start(bf16[72,3200]{1,0:T(8,128)(2,1)S(1)} %pad_maximum_fusion.2), channel_id=1, source_target_pairs={{0,1},{1,2},{2,3},{3,4},{4,5},{5,6},{6,7},{7,8},{8,9},{9,10},{10,1... | collective-permute-start | bytes 1382408 | tf_op jit(solution)/shard_map/ppermute | solution.py:65
  141.4 0.7 constant_dynamic-update-slice_fusion.1
  142.1 0.7 constant_dynamic-update-slice_fusion.4
  142.7 3.5 %collective-permute-done.3 = bf16[72,3200]{1,0:T(8,128)(2,1)S(1)} collective-permute-done((bf16[72,3200]{1,0:T(8,128)(2,1)S(1)}, bf16[72,3200]{1,0:T(8,128)(2,1)S(1)}, u32[]{:S(2)}, u32[]{:S(2)}) %collective-permute-start.3) | collective-permute-done | bytes 460832 | tf_op jit(solution)/shard_map/ppermute | solution.py:65
  146.2 1.9 collective-permute-start.4
  148.1 0.8 constant_dynamic-update-slice_fusion
  148.9 2.5 %collective-permute-done.11 = bf16[72,3200]{1,0:T(8,128)(2,1)S(1)} collective-permute-done((bf16[72,3200]{1,0:T(8,128)(2,1)S(1)}, bf16[72,3200]{1,0:T(8,128)(2,1)S(1)}, u32[]{:S(2)}, u32[]{:S(2)}) %collective-permute-start.11) | collective-permute-done | bytes 460832 | tf_op jit(solution)/shard_map/ppermute | solution.py:65
  151.5 1.9 collective-permute-start.12
  153.4 0.8 constant_dynamic-update-slice_fusion.3
  154.2 2.2 collective-permute-done.4
  156.4 0.7 slice_dynamic-update-slice_fusion.1
  157.1 0.7 fusion.93
  157.8 7.0 %convolution_convert_fusion.1 = bf16[192,3200]{1,0:T(8,128)(2,1)S(1)} fusion(bf16[640,3200]{1,0:T(8,128)(2,1)} %param.15, bf16[192,3200]{1,0:T(8,128)(2,1)} %fusion.93, bf16[3200,640]{1,0:T(8,128)(2,1)} %param.13, f32[640]{0:T(1024)S(1)} %copy-done.4), kind=kOutput, calls=%fused_computation.3 | convolution fusion | flops 1581588480 | bytes 10652160 | tf_op jit(solution)/shard_map/dot_general | solution.py:95
  164.9 1.7 slice_dynamic-update-slice_fusion
  166.6 1.6 fusion.92
  168.2 8.0 %convolution_convert_fusion = bf16[192,3200]{1,0:T(8,128)(2,1)} fusion(bf16[640,3200]{1,0:T(8,128)(2,1)} %param.15, bf16[192,3200]{1,0:T(8,128)(2,1)} %fusion.92, bf16[3200,640]{1,0:T(8,128)(2,1)} %param.13, f32[640]{0:T(1024)S(1)} %copy-done.4), kind=kOutput, calls=%fused_computation.2 | convolution fusion | flops 1581588480 | bytes 10652160 | tf_op jit(solution)/shard_map/dot_general | solution.py:95
  176.2 0.9 broadcast_select_fusion.1
  177.2 1.1 fusion.160
  178.3 3.4 %collective-permute-start.5 = (bf16[72,3200]{1,0:T(8,128)(2,1)S(1)}, bf16[72,3200]{1,0:T(8,128)(2,1)S(1)}, u32[]{:S(2)}, u32[]{:S(2)}) collective-permute-start(bf16[72,3200]{1,0:T(8,128)(2,1)S(1)} %pad_maximum_fusion.1), channel_id=1, source_target_pairs={{0,47},{1,0},{2,1},{3,2},{4,3},{5,4},{6,5},{7,6},{8,7},{9,8},{10,9... | collective-permute-start | bytes 1382408 | tf_op jit(solution)/shard_map/ppermute | solution.py:65
  181.7 1.9 collective-permute-start.13
  183.7 5.1 %collective-permute-done.5 = bf16[72,3200]{1,0:T(8,128)(2,1)S(1)} collective-permute-done((bf16[72,3200]{1,0:T(8,128)(2,1)S(1)}, bf16[72,3200]{1,0:T(8,128)(2,1)S(1)}, u32[]{:S(2)}, u32[]{:S(2)}) %collective-permute-start.5) | collective-permute-done | bytes 460832 | tf_op jit(solution)/shard_map/ppermute | solution.py:65
  188.9 2.4 %collective-permute-start.6 = (bf16[72,3200]{1,0:T(8,128)(2,1)S(1)}, bf16[72,3200]{1,0:T(8,128)(2,1)S(1)}, u32[]{:S(2)}, u32[]{:S(2)}) collective-permute-start(bf16[72,3200]{1,0:T(8,128)(2,1)S(1)} %add_convert_fusion.3), channel_id=1, source_target_pairs={{0,47},{1,0},{2,1},{3,2},{4,3},{5,4},{6,5},{7,6},{8,7},{9,8},{10,9... | collective-permute-start | bytes 1382408 | tf_op jit(solution)/shard_map/ppermute | solution.py:65
  191.4 2.3 collective-permute-done.13
  193.7 1.1 add_convert_fusion.1
  194.9 2.4 %collective-permute-start.14 = (bf16[72,3200]{1,0:T(8,128)(2,1)S(1)}, bf16[72,3200]{1,0:T(8,128)(2,1)S(1)}, u32[]{:S(2)}, u32[]{:S(2)}) collective-permute-start(bf16[72,3200]{1,0:T(8,128)(2,1)S(1)} %add_convert_fusion.1), channel_id=1, source_target_pairs={{0,47},{1,0},{2,1},{3,2},{4,3},{5,4},{6,5},{7,6},{8,7},{9,8},{10,9... | collective-permute-start | bytes 1382408 | tf_op jit(solution)/shard_map/ppermute | solution.py:65
  197.3 2.1 collective-permute-done.6
  199.5 1.9 collective-permute-start.7
  201.5 3.9 %collective-permute-done.14 = bf16[72,3200]{1,0:T(8,128)(2,1)S(1)} collective-permute-done((bf16[72,3200]{1,0:T(8,128)(2,1)S(1)}, bf16[72,3200]{1,0:T(8,128)(2,1)S(1)}, u32[]{:S(2)}, u32[]{:S(2)}) %collective-permute-start.14) | collective-permute-done | bytes 460832 | tf_op jit(solution)/shard_map/ppermute | solution.py:65
  205.5 1.9 collective-permute-start.15
  207.4 2.8 %collective-permute-done.7 = bf16[24,3200]{1,0:T(8,128)(2,1)S(1)} collective-permute-done((bf16[24,3200]{1,0:T(8,128)(2,1)S(1)}, bf16[24,3200]{1,0:T(8,128)(2,1)S(1)}, u32[]{:S(2)}, u32[]{:S(2)}) %collective-permute-start.7) | collective-permute-done | bytes 153632 | tf_op jit(solution)/shard_map/ppermute | solution.py:65
  210.3 1.9 collective-permute-start.8
  212.2 2.2 collective-permute-done.15
  214.5 4.2 %collective-permute-start.16 = (bf16[24,3200]{1,0:T(8,128)(2,1)S(1)}, bf16[24,3200]{1,0:T(8,128)(2,1)S(1)}, u32[]{:S(2)}, u32[]{:S(2)}) collective-permute-start(bf16[24,3200]{1,0:T(8,128)(2,1)S(1)} %add_convert_fusion.5), channel_id=1, source_target_pairs={{0,45},{1,46},{2,47},{3,0},{4,1},{5,2},{6,3},{7,4},{8,5},{9,6},{10... | collective-permute-start | bytes 460808 | tf_op jit(solution)/shard_map/ppermute | solution.py:65
  218.8 2.7 %collective-permute-done.8 = bf16[24,3200]{1,0:T(8,128)(2,1)S(1)} collective-permute-done((bf16[24,3200]{1,0:T(8,128)(2,1)S(1)}, bf16[24,3200]{1,0:T(8,128)(2,1)S(1)}, u32[]{:S(2)}, u32[]{:S(2)}) %collective-permute-start.8) | collective-permute-done | bytes 153632 | tf_op jit(solution)/shard_map/ppermute | solution.py:65
  221.5 4.2 %collective-permute-done.16 = bf16[24,3200]{1,0:T(8,128)(2,1)S(1)} collective-permute-done((bf16[24,3200]{1,0:T(8,128)(2,1)S(1)}, bf16[24,3200]{1,0:T(8,128)(2,1)S(1)}, u32[]{:S(2)}, u32[]{:S(2)}) %collective-permute-start.16) | collective-permute-done | bytes 153632 | tf_op jit(solution)/shard_map/ppermute | solution.py:65
  225.7 9.2 %collective-permute-start.17 = (bf16[24,3200]{1,0:T(8,128)(2,1)S(1)}, bf16[24,3200]{1,0:T(8,128)(2,1)S(1)}, u32[]{:S(2)}, u32[]{:S(2)}) collective-permute-start(bf16[24,3200]{1,0:T(8,128)(2,1)S(1)} %broadcast_select_fusion), channel_id=1, source_target_pairs={{0,16},{1,17},{2,18},{3,19},{4,20},{5,21},{6,22},{7,23},{8,24},{9,... | collective-permute-start | bytes 460808 | tf_op jit(solution)/shard_map/ppermute | solution.py:68
  234.9 1.0 collective-permute-done.17
  235.9 0.8 fusion.91
  (38 shorter events, 1.7 us)
Async XLA Ops:
  0.0 4.6 %copy-start = (bf16[1,64,3200]{2,1,0:T(8,128)(2,1)S(1)}, bf16[1,64,3200]{2,1,0:T(8,128)(2,1)}, u32[]{:S(2)}) copy-start(bf16[1,64,3200]{2,1,0:T(8,128)(2,1)} %param.9) | copy-start | bytes 1228804
  8.5 66.6 %all-to-all-start = ((bf16[64,2,1600]{2,1,0:T(2,128)(2,1)}), bf16[64,2,1600]{2,1,0:T(2,128)(2,1)S(1)}, u32[]{:S(2)}, u32[]{:S(2)}) async-start(bf16[64,2,1600]{2,1,0:T(2,128)(2,1)} %reshape.119), calls=%async_computation | async-start | bytes 851968 | tf_op jit(solution)/shard_map/all_to_all | solution.py:47
  75.7 1.1 copy-start.1
  77.0 3.6 %collective-permute-start = (bf16[24,3200]{1,0:T(8,128)(2,1)S(1)}, bf16[24,3200]{1,0:T(8,128)(2,1)S(1)}, u32[]{:S(2)}, u32[]{:S(2)}) collective-permute-start(bf16[24,3200]{1,0:T(8,128)(2,1)S(1)} %fusion.26), channel_id=1, source_target_pairs={{0,16},{1,17},{2,18},{3,19},{4,20},{5,21},{6,22},{7,23},{8,24},{9,... | collective-permute-start | bytes 460808 | tf_op jit(solution)/shard_map/ppermute | solution.py:68
  80.7 35.3 %collective-permute-start.1 = (bf16[24,3200]{1,0:T(8,128)(2,1)S(1)}, bf16[24,3200]{1,0:T(8,128)(2,1)S(1)}, u32[]{:S(2)}, u32[]{:S(2)}) collective-permute-start(bf16[24,3200]{1,0:T(8,128)(2,1)S(1)} %get-tuple-element.16), channel_id=1, source_target_pairs={{0,3},{1,4},{2,5},{3,6},{4,7},{5,8},{6,9},{7,10},{8,11},{9,12},{10... | collective-permute-start | bytes 460808 | tf_op jit(solution)/shard_map/ppermute | solution.py:65
  82.6 36.0 %collective-permute-start.9 = (bf16[24,3200]{1,0:T(8,128)(2,1)S(1)}, bf16[24,3200]{1,0:T(8,128)(2,1)S(1)}, u32[]{:S(2)}, u32[]{:S(2)}) collective-permute-start(bf16[24,3200]{1,0:T(8,128)(2,1)S(1)} %get-tuple-element.15), channel_id=1, source_target_pairs={{0,3},{1,4},{2,5},{3,6},{4,7},{5,8},{6,9},{7,10},{8,11},{9,12},{10... | collective-permute-start | bytes 460808 | tf_op jit(solution)/shard_map/ppermute | solution.py:65
  116.7 13.9 %collective-permute-start.2 = (bf16[24,3200]{1,0:T(8,128)(2,1)S(1)}, bf16[24,3200]{1,0:T(8,128)(2,1)S(1)}, u32[]{:S(2)}, u32[]{:S(2)}) collective-permute-start(bf16[24,3200]{1,0:T(8,128)(2,1)S(1)} %collective-permute-done.1), channel_id=1, source_target_pairs={{0,3},{1,4},{2,5},{3,6},{4,7},{5,8},{6,9},{7,10},{8,11},{9,12},{10... | collective-permute-start | bytes 460808 | tf_op jit(solution)/shard_map/ppermute | solution.py:65
  119.3 13.3 %collective-permute-start.10 = (bf16[24,3200]{1,0:T(8,128)(2,1)S(1)}, bf16[24,3200]{1,0:T(8,128)(2,1)S(1)}, u32[]{:S(2)}, u32[]{:S(2)}) collective-permute-start(bf16[24,3200]{1,0:T(8,128)(2,1)S(1)} %collective-permute-done.9), channel_id=1, source_target_pairs={{0,3},{1,4},{2,5},{3,6},{4,7},{5,8},{6,9},{7,10},{8,11},{9,12},{10... | collective-permute-start | bytes 460808 | tf_op jit(solution)/shard_map/ppermute | solution.py:65
  130.6 15.6 %collective-permute-start.3 = (bf16[72,3200]{1,0:T(8,128)(2,1)S(1)}, bf16[72,3200]{1,0:T(8,128)(2,1)S(1)}, u32[]{:S(2)}, u32[]{:S(2)}) collective-permute-start(bf16[72,3200]{1,0:T(8,128)(2,1)S(1)} %pad_maximum_fusion), channel_id=1, source_target_pairs={{0,1},{1,2},{2,3},{3,4},{4,5},{5,6},{6,7},{7,8},{8,9},{9,10},{10,1... | collective-permute-start | bytes 1382408 | tf_op jit(solution)/shard_map/ppermute | solution.py:65
  132.6 18.9 %collective-permute-start.11 = (bf16[72,3200]{1,0:T(8,128)(2,1)S(1)}, bf16[72,3200]{1,0:T(8,128)(2,1)S(1)}, u32[]{:S(2)}, u32[]{:S(2)}) collective-permute-start(bf16[72,3200]{1,0:T(8,128)(2,1)S(1)} %pad_maximum_fusion.2), channel_id=1, source_target_pairs={{0,1},{1,2},{2,3},{3,4},{4,5},{5,6},{6,7},{7,8},{8,9},{9,10},{10,1... | collective-permute-start | bytes 1382408 | tf_op jit(solution)/shard_map/ppermute | solution.py:65
  146.2 10.2 %collective-permute-start.4 = (bf16[72,3200]{1,0:T(8,128)(2,1)S(1)}, bf16[72,3200]{1,0:T(8,128)(2,1)S(1)}, u32[]{:S(2)}, u32[]{:S(2)}) collective-permute-start(bf16[72,3200]{1,0:T(8,128)(2,1)S(1)} %collective-permute-done.3), channel_id=1, source_target_pairs={{0,1},{1,2},{2,3},{3,4},{4,5},{5,6},{6,7},{7,8},{8,9},{9,10},{10,1... | collective-permute-start | bytes 1382408 | tf_op jit(solution)/shard_map/ppermute | solution.py:65
  148.9 8.9 %copy-start.4 = (f32[640]{0:T(1024)S(1)}, f32[640]{0:T(1024)}, u32[]{:S(2)}) copy-start(f32[640]{0:T(1024)} %param.14) | copy-start | bytes 7684
  151.5 13.4 %collective-permute-start.12 = (bf16[72,3200]{1,0:T(8,128)(2,1)S(1)}, bf16[72,3200]{1,0:T(8,128)(2,1)}, u32[]{:S(2)}, u32[]{:S(2)}) collective-permute-start(bf16[72,3200]{1,0:T(8,128)(2,1)S(1)} %collective-permute-done.11), channel_id=1, source_target_pairs={{0,1},{1,2},{2,3},{3,4},{4,5},{5,6},{6,7},{7,8},{8,9},{9,10},{10,1... | collective-permute-start | bytes 1382408 | tf_op jit(solution)/shard_map/ppermute | solution.py:65
  178.3 10.5 %collective-permute-start.5 = (bf16[72,3200]{1,0:T(8,128)(2,1)S(1)}, bf16[72,3200]{1,0:T(8,128)(2,1)S(1)}, u32[]{:S(2)}, u32[]{:S(2)}) collective-permute-start(bf16[72,3200]{1,0:T(8,128)(2,1)S(1)} %pad_maximum_fusion.1), channel_id=1, source_target_pairs={{0,47},{1,0},{2,1},{3,2},{4,3},{5,4},{6,5},{7,6},{8,7},{9,8},{10,9... | collective-permute-start | bytes 1382408 | tf_op jit(solution)/shard_map/ppermute | solution.py:65
  181.7 12.0 %collective-permute-start.13 = (bf16[72,3200]{1,0:T(8,128)(2,1)S(1)}, bf16[72,3200]{1,0:T(8,128)(2,1)S(1)}, u32[]{:S(2)}, u32[]{:S(2)}) collective-permute-start(bf16[72,3200]{1,0:T(8,128)(2,1)S(1)} %pad_maximum_fusion.3), channel_id=1, source_target_pairs={{0,47},{1,0},{2,1},{3,2},{4,3},{5,4},{6,5},{7,6},{8,7},{9,8},{10,9... | collective-permute-start | bytes 1382408 | tf_op jit(solution)/shard_map/ppermute | solution.py:65
  188.9 10.5 %collective-permute-start.6 = (bf16[72,3200]{1,0:T(8,128)(2,1)S(1)}, bf16[72,3200]{1,0:T(8,128)(2,1)S(1)}, u32[]{:S(2)}, u32[]{:S(2)}) collective-permute-start(bf16[72,3200]{1,0:T(8,128)(2,1)S(1)} %add_convert_fusion.3), channel_id=1, source_target_pairs={{0,47},{1,0},{2,1},{3,2},{4,3},{5,4},{6,5},{7,6},{8,7},{9,8},{10,9... | collective-permute-start | bytes 1382408 | tf_op jit(solution)/shard_map/ppermute | solution.py:65
  194.9 10.5 %collective-permute-start.14 = (bf16[72,3200]{1,0:T(8,128)(2,1)S(1)}, bf16[72,3200]{1,0:T(8,128)(2,1)S(1)}, u32[]{:S(2)}, u32[]{:S(2)}) collective-permute-start(bf16[72,3200]{1,0:T(8,128)(2,1)S(1)} %add_convert_fusion.1), channel_id=1, source_target_pairs={{0,47},{1,0},{2,1},{3,2},{4,3},{5,4},{6,5},{7,6},{8,7},{9,8},{10,9... | collective-permute-start | bytes 1382408 | tf_op jit(solution)/shard_map/ppermute | solution.py:65
  199.5 10.7 %collective-permute-start.7 = (bf16[24,3200]{1,0:T(8,128)(2,1)S(1)}, bf16[24,3200]{1,0:T(8,128)(2,1)S(1)}, u32[]{:S(2)}, u32[]{:S(2)}) collective-permute-start(bf16[24,3200]{1,0:T(8,128)(2,1)S(1)} %slice.84), channel_id=1, source_target_pairs={{0,45},{1,46},{2,47},{3,0},{4,1},{5,2},{6,3},{7,4},{8,5},{9,6},{10... | collective-permute-start | bytes 460808 | tf_op jit(solution)/shard_map/ppermute | solution.py:65
  205.4 30.4 %copy-start.2 = (f32[3200]{0:T(1024)S(1)}, f32[3200]{0:T(1024)}, u32[]{:S(2)}) copy-start(f32[3200]{0:T(1024)} %param.16) | copy-start | bytes 38404
  205.5 30.4 %copy-start.3 = (f32[3200]{0:T(1024)S(1)}, f32[3200]{0:T(1024)}, u32[]{:S(2)}) copy-start(f32[3200]{0:T(1024)} %param.17) | copy-start | bytes 38404
  205.5 9.0 %collective-permute-start.15 = (bf16[24,3200]{1,0:T(8,128)(2,1)S(1)}, bf16[24,3200]{1,0:T(8,128)(2,1)S(1)}, u32[]{:S(2)}, u32[]{:S(2)}) collective-permute-start(bf16[24,3200]{1,0:T(8,128)(2,1)S(1)} %slice.93), channel_id=1, source_target_pairs={{0,45},{1,46},{2,47},{3,0},{4,1},{5,2},{6,3},{7,4},{8,5},{9,6},{10... | collective-permute-start | bytes 460808 | tf_op jit(solution)/shard_map/ppermute | solution.py:65
  210.3 11.1 %collective-permute-start.8 = (bf16[24,3200]{1,0:T(8,128)(2,1)S(1)}, bf16[24,3200]{1,0:T(8,128)(2,1)S(1)}, u32[]{:S(2)}, u32[]{:S(2)}) collective-permute-start(bf16[24,3200]{1,0:T(8,128)(2,1)S(1)} %add_convert_fusion.7), channel_id=1, source_target_pairs={{0,45},{1,46},{2,47},{3,0},{4,1},{5,2},{6,3},{7,4},{8,5},{9,6},{10... | collective-permute-start | bytes 460808 | tf_op jit(solution)/shard_map/ppermute | solution.py:65
  214.5 11.1 %collective-permute-start.16 = (bf16[24,3200]{1,0:T(8,128)(2,1)S(1)}, bf16[24,3200]{1,0:T(8,128)(2,1)S(1)}, u32[]{:S(2)}, u32[]{:S(2)}) collective-permute-start(bf16[24,3200]{1,0:T(8,128)(2,1)S(1)} %add_convert_fusion.5), channel_id=1, source_target_pairs={{0,45},{1,46},{2,47},{3,0},{4,1},{5,2},{6,3},{7,4},{8,5},{9,6},{10... | collective-permute-start | bytes 460808 | tf_op jit(solution)/shard_map/ppermute | solution.py:65
  225.7 10.2 %collective-permute-start.17 = (bf16[24,3200]{1,0:T(8,128)(2,1)S(1)}, bf16[24,3200]{1,0:T(8,128)(2,1)S(1)}, u32[]{:S(2)}, u32[]{:S(2)}) collective-permute-start(bf16[24,3200]{1,0:T(8,128)(2,1)S(1)} %broadcast_select_fusion), channel_id=1, source_target_pairs={{0,16},{1,17},{2,18},{3,19},{4,20},{5,21},{6,22},{7,23},{8,24},{9,... | collective-permute-start | bytes 460808 | tf_op jit(solution)/shard_map/ppermute | solution.py:68

commit v2 on v0

v2 whole, which is shorter than its diff:
```python
import jax
import jax.numpy as jnp
from jax import lax
from jax.experimental import pallas as pl
from jax.experimental.pallas import tpu as pltpu
from jax.sharding import PartitionSpec as P

AXES = ("section", "dp")


def shift_pairs(sections, dps, hops):
    ring = 2 * dps
    pairs = []
    for section in range(sections):
        for dp in range(dps):
            there = (section // 2 % 2 * dps + dp + hops) % ring
            target = (section // 4 * 2 + there // dps) * 2 + section % 2
            pairs.append((section * dps + dp, target * dps + there % dps))
    return pairs


def half_groups(sections):
    return [[s for s in range(sections) if s // 2 % 2 == half] for half in range(2)]


def plan_kernel(mine_ref, live_ref, order_ref, patches_ref, far_ref, near_ref, pick_far_ref, pick_near_ref):
    sections = live_ref.shape[1]
    half = sections // 2
    keep = pick_far_ref.shape[0]
    mine = mine_ref[0]
    my_half = mine // 2 % 2
    live = live_ref[...].astype(jnp.float32)
    order = order_ref[...]
    down = lax.broadcasted_iota(jnp.int32, (sections, sections), 0)
    along = lax.broadcasted_iota(jnp.int32, (sections, sections), 1)
    live_down = jnp.sum(jnp.where(down == along, live, 0.0), axis=1, keepdims=True)
    starts_down = jnp.sum(jnp.where(along < down, live, 0.0), axis=1, keepdims=True)
    is_me = lax.broadcasted_iota(jnp.int32, (sections, 1), 0) == mine
    my_start = jnp.sum(jnp.where(is_me, starts_down, 0.0), axis=0, keepdims=True)
    my_live = jnp.sum(jnp.where(is_me, live_down, 0.0), axis=0, keepdims=True)
    peer = down % half
    toward = jnp.where(down < half, 1 - my_half, my_half)
    target = peer // 2 * 4 + toward * 2 + peer % 2
    place = jnp.sum(jnp.where(order == target, along, 0).astype(jnp.float32), axis=1, keepdims=True)
    slot = (place - my_start).astype(jnp.int32) & (sections - 1)
    wanted = (along == slot) & (slot.astype(jnp.float32) < my_live)
    move = jnp.where(wanted, 1.0, 0.0).astype(jnp.bfloat16)
    sent = jnp.dot(move, patches_ref[...], preferred_element_type=jnp.float32).astype(jnp.bfloat16)
    far_ref[...] = sent[:half]
    near_ref[...] = sent[half:]
    peers = lax.broadcasted_iota(jnp.int32, (sections, half), 1)
    source = peers // 2 * 4 + my_half * 2 + peers % 2
    from_it = lax.broadcasted_iota(jnp.int32, (sections, half), 0) == source
    first = jnp.sum(jnp.where(from_it, starts_down, 0.0), axis=0, keepdims=True)
    last = first + jnp.sum(jnp.where(from_it, live_down, 0.0), axis=0, keepdims=True)
    rounds = lax.broadcasted_iota(jnp.int32, (keep, half), 0) * sections
    lanes = lax.broadcasted_iota(jnp.int32, (1, sections), 1)
    for owner, pick_ref in ((mine ^ 2, pick_far_ref), (mine, pick_near_ref)):
        at = jnp.sum(jnp.where(order == owner, lanes, 0).astype(jnp.float32), axis=1, keepdims=True)
        number = rounds.astype(jnp.float32) + at
        pick_ref[...] = jnp.where((number >= first) & (number < last), 1.0, 0.0).astype(jnp.bfloat16)


def plan(patches, live, order, mine, keep):
    slots, width = patches.shape
    half = live.shape[1] // 2
    vmem = pl.BlockSpec(memory_space=pltpu.VMEM)
    return pl.pallas_call(
        plan_kernel,
        out_shape=(
            jax.ShapeDtypeStruct((half, width), jnp.bfloat16),
            jax.ShapeDtypeStruct((half, width), jnp.bfloat16),
            jax.ShapeDtypeStruct((keep, half), jnp.bfloat16),
            jax.ShapeDtypeStruct((keep, half), jnp.bfloat16),
        ),
        in_specs=[pl.BlockSpec(memory_space=pltpu.SMEM), vmem, vmem, vmem],
        out_specs=(vmem, vmem, vmem, vmem),
        compiler_params=pltpu.CompilerParams(vmem_limit_bytes=16 * 1024 * 1024),
    )(mine[None], live, order, patches)


def pick(chosen, rows):
    return jnp.dot(chosen, rows, preferred_element_type=jnp.float32).astype(jnp.bfloat16)


def per_device(
    patches, live, rounds, ln_gain, fc1_weight, fc1_bias, fc2_weight, fc2_bias, layer_scale
):
    sections = lax.axis_size("section")
    dps = lax.axis_size("dp")
    mine = lax.axis_index("section").astype(jnp.int32)
    keep_rows = 3 * sections // 8
    groups = half_groups(sections)

    def exchange(rows):
        return lax.all_to_all(
            rows, "section", split_axis=0, concat_axis=0, axis_index_groups=groups, tiled=True
        )

    far, near, pick_far, pick_near = plan(patches[0], live, rounds, mine, keep_rows)
    crossing = pick(pick_far, exchange(far))
    crossed = lax.ppermute(crossing, AXES, shift_pairs(sections, dps, dps))
    crossing, near = lax.optimization_barrier((crossing, near))
    stayed = pick(pick_near, exchange(near))
    routed = stayed + crossed

    return finish(
        routed, sections, dps, ln_gain, fc1_weight, fc1_bias, fc2_weight, fc2_bias, layer_scale
    )


def finish(routed, sections, dps, ln_gain, fc1_weight, fc1_bias, fc2_weight, fc2_bias, layer_scale):
    keep = routed.shape[0]

    def send(value, hops):
        return lax.ppermute(value, AXES, shift_pairs(sections, dps, hops))

    def encode(rows):
        pre = jnp.dot(rows, fc1_weight, preferred_element_type=jnp.float32) + fc1_bias
        hidden = jax.nn.gelu(pre, approximate=False).astype(jnp.bfloat16)
        return jnp.dot(hidden, fc2_weight, preferred_element_type=jnp.float32).astype(jnp.bfloat16)

    def add(a, b):
        return (a.astype(jnp.float32) + b.astype(jnp.float32)).astype(jnp.bfloat16)

    rows32 = routed.astype(jnp.float32)
    mean = jnp.mean(rows32, axis=1, keepdims=True)
    centered = rows32 - mean
    var = jnp.mean(centered * centered, axis=1, keepdims=True)
    normed = (centered * lax.rsqrt(var + 1e-06) * ln_gain).astype(jnp.bfloat16)

    up3, down3 = send(normed, 3), send(normed, -3)
    up6, down6 = send(up3, 3), send(down3, -3)
    up036 = jnp.concatenate([normed, up3, up6], axis=0)
    down036 = jnp.concatenate([normed, down3, down6], axis=0)
    up147, down147 = send(up036, 1), send(down036, -1)
    up258, down25 = send(up147, 1), send(down147[: 2 * keep], -1)

    part0 = encode(jnp.concatenate([up036[keep:], down036], axis=0))
    part1 = encode(jnp.concatenate([up147, down147], axis=0))
    part2 = encode(jnp.concatenate([up258, down25], axis=0))

    none = jnp.zeros((keep, routed.shape[1]), jnp.bfloat16)
    up_sum = add(send(part2[: 3 * keep], -1), part1[: 3 * keep])
    down_sum = add(
        jnp.concatenate([send(part2[3 * keep :], 1), none], axis=0), part1[3 * keep :]
    )
    up_sum = add(send(up_sum, -1), jnp.concatenate([none, part0[: 2 * keep]], axis=0))
    down_sum = add(send(down_sum, 1), part0[2 * keep :])
    up_back = add(send(up_sum[2 * keep :], -3), up_sum[keep : 2 * keep])
    down_back = add(send(down_sum[2 * keep :], 3), down_sum[keep : 2 * keep])
    up_home, down_home = send(up_back, -3), send(down_back, 3)
    summed = (up_home.astype(jnp.float32) + up_sum[:keep].astype(jnp.float32)) + (
        down_home.astype(jnp.float32) + down_sum[:keep].astype(jnp.float32)
    )
    return (rows32 + layer_scale * (summed + fc2_bias)).astype(jnp.bfloat16)[None]


def solution(mesh):
    placed = (
        P("dp", "section", None),
        P("dp", None),
        P("dp", None),
        P(),
        P(None, "dp"),
        P("dp"),
        P("dp", None),
        P(),
        P(),
    )
    return jax.shard_map(
        per_device, mesh=mesh, in_specs=placed, out_specs=P("dp", "section", None), check_vma=False
    )
```

time: 519 us -> 223 us (0.43)
  the two profiles are of different devices: /device:TPU:4 before, /device:TPU:16 now
where the time goes in v2:
time: 223 us; the launch traced here: 222 us
  starting transfers between devices  120 us (54%)
  waiting for transfers between devices  50.1 us (22%)
  blocking collectives  22 us (10%)
  matrix products  17.9 us (8%)
  local copies, waits for them, and re-layouts  7.43 us (3%)
  other arithmetic  3.96 us (2%)
    ppermute x16, starting transfers between devices, send(): return lax.ppermute(value, AXES, shift_pairs(sections, dps, hops))  93.2 us
    ppermute x16, waiting for transfers between devices, send(): return lax.ppermute(value, AXES, shift_pairs(sections, dps, hops))  43.9 us
    all_to_all x1, blocking collectives, exchange(): lax.all_to_all(rows, 'section', split_axis=0, concat_axis=0, axis_index_g...  22 us
    ppermute x1, starting transfers between devices, per_device(): crossed = lax.ppermute(crossing, AXES, shift_pairs(sections, dps, dps))  20.5 us
    dot_general x3, matrix products, encode(): jnp.dot(hidden, fc2_weight, preferred_element_type=jnp.float32)  17.5 us
    ppermute x1, waiting for transfers between devices, per_device(): crossed = lax.ppermute(crossing, AXES, shift_pairs(sections, dps, dps))  6.18 us
    unnamed x23, local copies, waits for them, and re-layouts  6.11 us
    all_to_all x1, starting transfers between devices, exchange(): lax.all_to_all(rows, 'section', split_axis=0, concat_axis=0, axis_index_g...  5.99 us
  transfers between devices with their start and end apart: 18, of which 11 were waited for; matrix products, arithmetic and copies ran while one was open for 7% of the time, Pallas kernels for 0%

profile of v2, /device:TPU:16, one launch (start us, length us, event | category | flops | bytes accessed | tf_op | source)
XLA Modules:
  0.0 221.7 jit_solution(16361596891556751238)
XLA Ops:
  0.0 1.0 copy-done
  1.0 0.7 copy-done.1
  1.7 0.7 copy-done.2
  2.3 0.3 shard_map.91
  2.7 0.5 broadcast.404
  3.2 0.7 reduce
  3.9 0.3 reshape.20
  4.2 22.0 %all_to_all.24 = bf16[32,2,1600]{2,1,0:T(2,128)(2,1)S(1)} all-to-all(bf16[32,2,1600]{2,1,0:T(2,128)(2,1)S(1)} %reshape.20), channel_id=1, replica_groups={{0,16,64,80,128,144,192,208,256,272,320,336,384,400,448,464,512,528,576..., dimensions={0} | all-to-all | bytes 409600 | tf_op jit(solution)/shard_map/all_to_all | solution.py:96
  26.1 0.3 reshape.21
  26.4 0.2 convolution_convert_fusion.4
  26.6 0.7 reduce.1
  27.3 0.9 reshape.22
  28.3 6.0 %all-to-all-start.1 = ((bf16[32,2,1600]{2,1,0:T(2,128)(2,1)}), bf16[32,2,1600]{2,1,0:T(2,128)(2,1)S(1)}, u32[]{:S(2)}, u32[]{:S(2)}) async-start(bf16[32,2,1600]{2,1,0:T(2,128)(2,1)} %reshape.22), calls=%async_computation.1 | async-start | bytes 425984 | tf_op jit(solution)/shard_map/all_to_all | solution.py:96
  34.3 20.5 %collective-permute-start = (bf16[24,3200]{1,0:T(8,128)(2,1)S(1)}, bf16[24,3200]{1,0:T(8,128)(2,1)S(1)}, u32[]{:S(2)}, u32[]{:S(2)}) collective-permute-start(bf16[24,3200]{1,0:T(8,128)(2,1)S(1)} %convolution_convert_fusion.4), channel_id=1, source_target_pairs={{0,32},{1,33},{2,34},{3,35},{4,36},{5,37},{6,38},{7,39},{8,40},{9,... | collective-permute-start | bytes 460808 | tf_op jit(solution)/shard_map/ppermute | solution.py:102
  54.8 0.0 all-to-all-done.1
  54.8 0.3 reshape.23
  55.1 6.2 %collective-permute-done = bf16[24,3200]{1,0:T(8,128)(2,1)S(1)} collective-permute-done((bf16[24,3200]{1,0:T(8,128)(2,1)S(1)}, bf16[24,3200]{1,0:T(8,128)(2,1)S(1)}, u32[]{:S(2)}, u32[]{:S(2)}) %collective-permute-start) | collective-permute-done | bytes 153632 | tf_op jit(solution)/shard_map/ppermute | solution.py:102
  61.2 0.3 fusion.240
  61.5 0.2 multiply_reduce_fusion
  61.8 0.1 multiply_convert_fusion
  61.9 28.0 %collective-permute-start.5 = (bf16[24,3200]{1,0:T(8,128)(2,1)S(1)}, bf16[24,3200]{1,0:T(8,128)(2,1)S(1)}, u32[]{:S(2)}, u32[]{:S(2)}) collective-permute-start(bf16[24,3200]{1,0:T(8,128)(2,1)S(1)} %multiply_convert_fusion), channel_id=1, source_target_pairs={{0,45},{1,46},{2,47},{3,0},{4,1},{5,2},{6,3},{7,4},{8,5},{9,6},{10... | collective-permute-start | bytes 460808 | tf_op jit(solution)/shard_map/ppermute | solution.py:116
  89.9 1.9 collective-permute-start.1
  91.8 4.5 %collective-permute-done.5 = bf16[24,3200]{1,0:T(8,128)(2,1)S(1)} collective-permute-done((bf16[24,3200]{1,0:T(8,128)(2,1)S(1)}, bf16[24,3200]{1,0:T(8,128)(2,1)S(1)}, u32[]{:S(2)}, u32[]{:S(2)}) %collective-permute-start.5) | collective-permute-done | bytes 153632 | tf_op jit(solution)/shard_map/ppermute | solution.py:116
  96.3 9.7 %collective-permute-start.6 = (bf16[24,3200]{1,0:T(8,128)(2,1)S(1)}, bf16[24,3200]{1,0:T(8,128)(2,1)S(1)}, u32[]{:S(2)}, u32[]{:S(2)}) collective-permute-start(bf16[24,3200]{1,0:T(8,128)(2,1)S(1)} %collective-permute-done.5), channel_id=1, source_target_pairs={{0,45},{1,46},{2,47},{3,0},{4,1},{5,2},{6,3},{7,4},{8,5},{9,6},{10... | collective-permute-start | bytes 460808 | tf_op jit(solution)/shard_map/ppermute | solution.py:116
  106.1 1.4 collective-permute-done.1
  107.5 1.9 collective-permute-start.2
  109.4 0.7 constant_dynamic-update-slice_fusion.4
  110.0 1.6 collective-permute-done.6
  111.7 8.8 %collective-permute-done.2 = bf16[24,3200]{1,0:T(8,128)(2,1)S(1)} collective-permute-done((bf16[24,3200]{1,0:T(8,128)(2,1)S(1)}, bf16[24,3200]{1,0:T(8,128)(2,1)S(1)}, u32[]{:S(2)}, u32[]{:S(2)}) %collective-permute-start.2) | collective-permute-done | bytes 153632 | tf_op jit(solution)/shard_map/ppermute | solution.py:116
  120.5 0.1 fusion.8
  120.6 1.9 collective-permute-start.3
  122.5 5.1 %collective-permute-start.7 = (bf16[72,3200]{1,0:T(8,128)(2,1)S(1)}, bf16[72,3200]{1,0:T(8,128)(2,1)S(1)}, u32[]{:S(2)}, u32[]{:S(2)}) collective-permute-start(bf16[72,3200]{1,0:T(8,128)(2,1)S(1)} %get-tuple-element.18), channel_id=1, source_target_pairs={{0,47},{1,0},{2,1},{3,2},{4,3},{5,4},{6,5},{7,6},{8,7},{9,8},{10,9... | collective-permute-start | bytes 1382408 | tf_op jit(solution)/shard_map/ppermute | solution.py:116
  127.7 0.7 constant_dynamic-update-slice_fusion.3
  128.3 0.8 constant_dynamic-update-slice_fusion.2
  129.1 3.4 %collective-permute-done.3 = bf16[72,3200]{1,0:T(8,128)(2,1)S(1)} collective-permute-done((bf16[72,3200]{1,0:T(8,128)(2,1)S(1)}, bf16[72,3200]{1,0:T(8,128)(2,1)S(1)}, u32[]{:S(2)}, u32[]{:S(2)}) %collective-permute-start.3) | collective-permute-done | bytes 460832 | tf_op jit(solution)/shard_map/ppermute | solution.py:116
  132.5 2.6 %collective-permute-start.4 = (bf16[72,3200]{1,0:T(8,128)(2,1)S(1)}, bf16[72,3200]{1,0:T(8,128)(2,1)S(1)}, u32[]{:S(2)}, u32[]{:S(2)}) collective-permute-start(bf16[72,3200]{1,0:T(8,128)(2,1)S(1)} %collective-permute-done.3), channel_id=1, source_target_pairs={{0,1},{1,2},{2,3},{3,4},{4,5},{5,6},{6,7},{7,8},{8,9},{9,10},{10,1... | collective-permute-start | bytes 1382408 | tf_op jit(solution)/shard_map/ppermute | solution.py:116
  135.2 0.7 constant_dynamic-update-slice_fusion.1
  135.9 4.4 %collective-permute-start.8 = (bf16[48,3200]{1,0:T(8,128)(2,1)S(1)}, bf16[48,3200]{1,0:T(8,128)(2,1)S(1)}, u32[]{:S(2)}, u32[]{:S(2)}) collective-permute-start(bf16[48,3200]{1,0:T(8,128)(2,1)S(1)} %slice.54), channel_id=1, source_target_pairs={{0,47},{1,0},{2,1},{3,2},{4,3},{5,4},{6,5},{7,6},{8,7},{9,8},{10,9... | collective-permute-start | bytes 921608 | tf_op jit(solution)/shard_map/ppermute | solution.py:116
  140.3 0.7 constant_dynamic-update-slice_fusion
  141.0 3.7 %collective-permute-done.8 = bf16[48,3200]{1,0:T(8,128)(2,1)S(1)} collective-permute-done((bf16[48,3200]{1,0:T(8,128)(2,1)S(1)}, bf16[48,3200]{1,0:T(8,128)(2,1)S(1)}, u32[]{:S(2)}, u32[]{:S(2)}) %collective-permute-start.8) | collective-permute-done | bytes 307232 | tf_op jit(solution)/shard_map/ppermute | solution.py:116
  144.7 5.6 %convolution_convert_fusion.2 = bf16[120,3200]{1,0:T(8,128)(2,1)S(1)} fusion(bf16[640,3200]{1,0:T(8,128)(2,1)} %param.15, bf16[3200,640]{1,0:T(8,128)(2,1)} %param.13, bf16[48,3200]{1,0:T(8,128)(2,1)S(1)} %collective-permute-done.8, bf16[72,3200]{1,0:T(8,128)(2,1)S(1)} %collective-permute-done.4, f32[640]{0:T(1024)S(1)} %copy-done.7), kind=kOutput, calls=%fused_computation.2 | convolution fusion | flops 990028800 | bytes 9730560 | tf_op jit(solution)/shard_map/dot_general | solution.py:121
  150.3 2.2 %collective-permute-start.13 = (bf16[48,3200]{1,0:T(8,128)(2,1)S(1)}, bf16[48,3200]{1,0:T(8,128)(2,1)S(1)}, u32[]{:S(2)}, u32[]{:S(2)}) collective-permute-start(bf16[48,3200]{1,0:T(8,128)(2,1)S(1)} %slice.61), channel_id=1, source_target_pairs={{0,1},{1,2},{2,3},{3,4},{4,5},{5,6},{6,7},{7,8},{8,9},{9,10},{10,1... | collective-permute-start | bytes 921608 | tf_op jit(solution)/shard_map/ppermute | solution.py:116
  152.6 5.3 %collective-permute-start.9 = (bf16[72,3200]{1,0:T(8,128)(2,1)S(1)}, bf16[72,3200]{1,0:T(8,128)(2,1)S(1)}, u32[]{:S(2)}, u32[]{:S(2)}) collective-permute-start(bf16[72,3200]{1,0:T(8,128)(2,1)S(1)} %slice.55), channel_id=1, source_target_pairs={{0,47},{1,0},{2,1},{3,2},{4,3},{5,4},{6,5},{7,6},{8,7},{9,8},{10,9... | collective-permute-start | bytes 1382408 | tf_op jit(solution)/shard_map/ppermute | solution.py:116
  157.9 6.1 %convolution_convert_fusion = bf16[144,3200]{1,0:T(8,128)(2,1)S(1)} fusion(bf16[640,3200]{1,0:T(8,128)(2,1)} %param.15, bf16[3200,640]{1,0:T(8,128)(2,1)} %param.13, bf16[72,3200]{1,0:T(8,128)(2,1)S(1)} %collective-permute-done.7, bf16[72,3200]{1,0:T(8,128)(2,1)} %copy-done.6, f32[640]{0:T(1024)S(1)} %copy-done.7), kind=kOutput, calls=%fused_computation | convolution fusion | flops 1188034560 | bytes 10037760 | tf_op jit(solution)/shard_map/dot_general | solution.py:121
  164.0 0.0 collective-permute-done.13
  164.0 1.8 collective-permute-done.9
  165.7 0.2 add_convert_fusion.3
  165.9 3.8 %collective-permute-start.10 = (bf16[72,3200]{1,0:T(8,128)(2,1)S(1)}, bf16[72,3200]{1,0:T(8,128)(2,1)S(1)}, u32[]{:S(2)}, u32[]{:S(2)}) collective-permute-start(bf16[72,3200]{1,0:T(8,128)(2,1)S(1)} %get-tuple-element.15), channel_id=1, source_target_pairs={{0,47},{1,0},{2,1},{3,2},{4,3},{5,4},{6,5},{7,6},{8,7},{9,8},{10,9... | collective-permute-start | bytes 1382408 | tf_op jit(solution)/shard_map/ppermute | solution.py:116
  169.7 5.8 %convolution_convert_fusion.1 = bf16[120,3200]{1,0:T(8,128)(2,1)S(1)} fusion(bf16[640,3200]{1,0:T(8,128)(2,1)} %param.15, bf16[120,3200]{1,0:T(8,128)(2,1)} %constant_dynamic-update-slice_fusion, bf16[3200,640]{1,0:T(8,128)(2,1)} %param.13, f32[640]{0:T(1024)S(1)} %copy-done.7), kind=kOutput, calls=%fused_computation.1 | convolution fusion | flops 988492800 | bytes 9730560 | tf_op jit(solution)/shard_map/dot_general | solution.py:121
  175.5 0.0 copy-start.4
  175.5 0.0 copy-start.5
  175.6 2.7 %collective-permute-start.14 = (bf16[72,3200]{1,0:T(8,128)(2,1)S(1)}, bf16[72,3200]{1,0:T(8,128)(2,1)S(1)}, u32[]{:S(2)}, u32[]{:S(2)}) collective-permute-start(bf16[72,3200]{1,0:T(8,128)(2,1)S(1)} %get-tuple-element.16), channel_id=1, source_target_pairs={{0,1},{1,2},{2,3},{3,4},{4,5},{5,6},{6,7},{7,8},{8,9},{9,10},{10,1... | collective-permute-start | bytes 1382408 | tf_op jit(solution)/shard_map/ppermute | solution.py:116
  178.3 0.1 add_convert_fusion.2
  178.4 5.3 %collective-permute-start.11 = (bf16[24,3200]{1,0:T(8,128)(2,1)S(1)}, bf16[24,3200]{1,0:T(8,128)(2,1)S(1)}, u32[]{:S(2)}, u32[]{:S(2)}) collective-permute-start(bf16[24,3200]{1,0:T(8,128)(2,1)S(1)} %slice.58), channel_id=1, source_target_pairs={{0,45},{1,46},{2,47},{3,0},{4,1},{5,2},{6,3},{7,4},{8,5},{9,6},{10... | collective-permute-start | bytes 460808 | tf_op jit(solution)/shard_map/ppermute | solution.py:116
  183.7 3.4 %collective-permute-done.14 = bf16[72,3200]{1,0:T(8,128)(2,1)S(1)} collective-permute-done((bf16[72,3200]{1,0:T(8,128)(2,1)S(1)}, bf16[72,3200]{1,0:T(8,128)(2,1)S(1)}, u32[]{:S(2)}, u32[]{:S(2)}) %collective-permute-start.14) | collective-permute-done | bytes 460832 | tf_op jit(solution)/shard_map/ppermute | solution.py:116
  187.2 0.1 add_convert_fusion
  187.3 7.7 %collective-permute-start.15 = (bf16[24,3200]{1,0:T(8,128)(2,1)S(1)}, bf16[24,3200]{1,0:T(8,128)(2,1)S(1)}, u32[]{:S(2)}, u32[]{:S(2)}) collective-permute-start(bf16[24,3200]{1,0:T(8,128)(2,1)S(1)} %slice.64), channel_id=1, source_target_pairs={{0,3},{1,4},{2,5},{3,6},{4,7},{5,8},{6,9},{7,10},{8,11},{9,12},{10... | collective-permute-start | bytes 460808 | tf_op jit(solution)/shard_map/ppermute | solution.py:116
  195.1 0.0 collective-permute-done.11
  195.1 8.6 %collective-permute-start.12 = (bf16[24,3200]{1,0:T(8,128)(2,1)S(1)}, bf16[24,3200]{1,0:T(8,128)(2,1)S(1)}, u32[]{:S(2)}, u32[]{:S(2)}) collective-permute-start(bf16[24,3200]{1,0:T(8,128)(2,1)S(1)} %add_convert_fusion.6), channel_id=1, source_target_pairs={{0,45},{1,46},{2,47},{3,0},{4,1},{5,2},{6,3},{7,4},{8,5},{9,6},{10... | collective-permute-start | bytes 460808 | tf_op jit(solution)/shard_map/ppermute | solution.py:116
  203.7 6.1 %collective-permute-done.15 = bf16[24,3200]{1,0:T(8,128)(2,1)S(1)} collective-permute-done((bf16[24,3200]{1,0:T(8,128)(2,1)S(1)}, bf16[24,3200]{1,0:T(8,128)(2,1)S(1)}, u32[]{:S(2)}, u32[]{:S(2)}) %collective-permute-start.15) | collective-permute-done | bytes 153632 | tf_op jit(solution)/shard_map/ppermute | solution.py:116
  209.8 0.1 add_convert_fusion.5
  209.8 1.9 collective-permute-start.16
  211.8 9.1 %collective-permute-done.16 = bf16[24,3200]{1,0:T(8,128)(2,1)S(1)} collective-permute-done((bf16[24,3200]{1,0:T(8,128)(2,1)S(1)}, bf16[24,3200]{1,0:T(8,128)(2,1)S(1)}, u32[]{:S(2)}, u32[]{:S(2)}) %collective-permute-start.16) | collective-permute-done | bytes 153632 | tf_op jit(solution)/shard_map/ppermute | solution.py:116
  220.9 0.8 fusion.83
  (24 shorter events, 0.2 us)
Async XLA Ops:
  0.0 1.0 copy-start
  1.0 0.7 copy-start.1
  1.7 0.7 copy-start.2
  2.3 59.5 %copy-start.3 = (f32[3200]{0:T(1024)S(1)}, f32[3200]{0:T(1024)}, u32[]{:S(2)}) copy-start(f32[3200]{0:T(1024)} %param.12) | copy-start | bytes 38404
  26.1 118.5 %copy-start.7 = (f32[640]{0:T(1024)S(1)}, f32[640]{0:T(1024)}, u32[]{:S(2)}) copy-start(f32[640]{0:T(1024)} %param.14) | copy-start | bytes 7684
  28.3 26.5 %all-to-all-start.1 = ((bf16[32,2,1600]{2,1,0:T(2,128)(2,1)}), bf16[32,2,1600]{2,1,0:T(2,128)(2,1)S(1)}, u32[]{:S(2)}, u32[]{:S(2)}) async-start(bf16[32,2,1600]{2,1,0:T(2,128)(2,1)} %reshape.22), calls=%async_computation.1 | async-start | bytes 425984 | tf_op jit(solution)/shard_map/all_to_all | solution.py:96
  34.3 27.0 %collective-permute-start = (bf16[24,3200]{1,0:T(8,128)(2,1)S(1)}, bf16[24,3200]{1,0:T(8,128)(2,1)S(1)}, u32[]{:S(2)}, u32[]{:S(2)}) collective-permute-start(bf16[24,3200]{1,0:T(8,128)(2,1)S(1)} %convolution_convert_fusion.4), channel_id=1, source_target_pairs={{0,32},{1,33},{2,34},{3,35},{4,36},{5,37},{6,38},{7,39},{8,40},{9,... | collective-permute-start | bytes 460808 | tf_op jit(solution)/shard_map/ppermute | solution.py:102
  61.9 34.5 %collective-permute-start.5 = (bf16[24,3200]{1,0:T(8,128)(2,1)S(1)}, bf16[24,3200]{1,0:T(8,128)(2,1)S(1)}, u32[]{:S(2)}, u32[]{:S(2)}) collective-permute-start(bf16[24,3200]{1,0:T(8,128)(2,1)S(1)} %multiply_convert_fusion), channel_id=1, source_target_pairs={{0,45},{1,46},{2,47},{3,0},{4,1},{5,2},{6,3},{7,4},{8,5},{9,6},{10... | collective-permute-start | bytes 460808 | tf_op jit(solution)/shard_map/ppermute | solution.py:116
  89.9 17.6 %collective-permute-start.1 = (bf16[24,3200]{1,0:T(8,128)(2,1)S(1)}, bf16[24,3200]{1,0:T(8,128)(2,1)S(1)}, u32[]{:S(2)}, u32[]{:S(2)}) collective-permute-start(bf16[24,3200]{1,0:T(8,128)(2,1)S(1)} %multiply_convert_fusion), channel_id=1, source_target_pairs={{0,3},{1,4},{2,5},{3,6},{4,7},{5,8},{6,9},{7,10},{8,11},{9,12},{10... | collective-permute-start | bytes 460808 | tf_op jit(solution)/shard_map/ppermute | solution.py:116
  96.3 15.3 %collective-permute-start.6 = (bf16[24,3200]{1,0:T(8,128)(2,1)S(1)}, bf16[24,3200]{1,0:T(8,128)(2,1)S(1)}, u32[]{:S(2)}, u32[]{:S(2)}) collective-permute-start(bf16[24,3200]{1,0:T(8,128)(2,1)S(1)} %collective-permute-done.5), channel_id=1, source_target_pairs={{0,45},{1,46},{2,47},{3,0},{4,1},{5,2},{6,3},{7,4},{8,5},{9,6},{10... | collective-permute-start | bytes 460808 | tf_op jit(solution)/shard_map/ppermute | solution.py:116
  107.5 13.1 %collective-permute-start.2 = (bf16[24,3200]{1,0:T(8,128)(2,1)S(1)}, bf16[24,3200]{1,0:T(8,128)(2,1)S(1)}, u32[]{:S(2)}, u32[]{:S(2)}) collective-permute-start(bf16[24,3200]{1,0:T(8,128)(2,1)S(1)} %collective-permute-done.1), channel_id=1, source_target_pairs={{0,3},{1,4},{2,5},{3,6},{4,7},{5,8},{6,9},{7,10},{8,11},{9,12},{10... | collective-permute-start | bytes 460808 | tf_op jit(solution)/shard_map/ppermute | solution.py:116
  120.6 11.9 %collective-permute-start.3 = (bf16[72,3200]{1,0:T(8,128)(2,1)S(1)}, bf16[72,3200]{1,0:T(8,128)(2,1)S(1)}, u32[]{:S(2)}, u32[]{:S(2)}) collective-permute-start(bf16[72,3200]{1,0:T(8,128)(2,1)S(1)} %get-tuple-element.17), channel_id=1, source_target_pairs={{0,1},{1,2},{2,3},{3,4},{4,5},{5,6},{6,7},{7,8},{8,9},{9,10},{10,1... | collective-permute-start | bytes 1382408 | tf_op jit(solution)/shard_map/ppermute | solution.py:116
  122.5 13.3 %collective-permute-start.7 = (bf16[72,3200]{1,0:T(8,128)(2,1)S(1)}, bf16[72,3200]{1,0:T(8,128)(2,1)S(1)}, u32[]{:S(2)}, u32[]{:S(2)}) collective-permute-start(bf16[72,3200]{1,0:T(8,128)(2,1)S(1)} %get-tuple-element.18), channel_id=1, source_target_pairs={{0,47},{1,0},{2,1},{3,2},{4,3},{5,4},{6,5},{7,6},{8,7},{9,8},{10,9... | collective-permute-start | bytes 1382408 | tf_op jit(solution)/shard_map/ppermute | solution.py:116
  132.5 12.1 %copy-start.6 = (bf16[72,3200]{1,0:T(8,128)(2,1)}, bf16[72,3200]{1,0:T(8,128)(2,1)S(1)}, u32[]{:S(2)}) copy-start(bf16[72,3200]{1,0:T(8,128)(2,1)S(1)} %collective-permute-done.3) | copy-start | bytes 1382404
  132.5 12.1 %collective-permute-start.4 = (bf16[72,3200]{1,0:T(8,128)(2,1)S(1)}, bf16[72,3200]{1,0:T(8,128)(2,1)S(1)}, u32[]{:S(2)}, u32[]{:S(2)}) collective-permute-start(bf16[72,3200]{1,0:T(8,128)(2,1)S(1)} %collective-permute-done.3), channel_id=1, source_target_pairs={{0,1},{1,2},{2,3},{3,4},{4,5},{5,6},{6,7},{7,8},{8,9},{9,10},{10,1... | collective-permute-start | bytes 1382408 | tf_op jit(solution)/shard_map/ppermute | solution.py:116
  135.9 8.8 %collective-permute-start.8 = (bf16[48,3200]{1,0:T(8,128)(2,1)S(1)}, bf16[48,3200]{1,0:T(8,128)(2,1)S(1)}, u32[]{:S(2)}, u32[]{:S(2)}) collective-permute-start(bf16[48,3200]{1,0:T(8,128)(2,1)S(1)} %slice.54), channel_id=1, source_target_pairs={{0,47},{1,0},{2,1},{3,2},{4,3},{5,4},{6,5},{7,6},{8,7},{9,8},{10,9... | collective-permute-start | bytes 921608 | tf_op jit(solution)/shard_map/ppermute | solution.py:116
  150.3 13.6 %collective-permute-start.13 = (bf16[48,3200]{1,0:T(8,128)(2,1)S(1)}, bf16[48,3200]{1,0:T(8,128)(2,1)S(1)}, u32[]{:S(2)}, u32[]{:S(2)}) collective-permute-start(bf16[48,3200]{1,0:T(8,128)(2,1)S(1)} %slice.61), channel_id=1, source_target_pairs={{0,1},{1,2},{2,3},{3,4},{4,5},{5,6},{6,7},{7,8},{8,9},{9,10},{10,1... | collective-permute-start | bytes 921608 | tf_op jit(solution)/shard_map/ppermute | solution.py:116
  152.6 13.1 %collective-permute-start.9 = (bf16[72,3200]{1,0:T(8,128)(2,1)S(1)}, bf16[72,3200]{1,0:T(8,128)(2,1)S(1)}, u32[]{:S(2)}, u32[]{:S(2)}) collective-permute-start(bf16[72,3200]{1,0:T(8,128)(2,1)S(1)} %slice.55), channel_id=1, source_target_pairs={{0,47},{1,0},{2,1},{3,2},{4,3},{5,4},{6,5},{7,6},{8,7},{9,8},{10,9... | collective-permute-start | bytes 1382408 | tf_op jit(solution)/shard_map/ppermute | solution.py:116
  165.9 12.4 %collective-permute-start.10 = (bf16[72,3200]{1,0:T(8,128)(2,1)S(1)}, bf16[72,3200]{1,0:T(8,128)(2,1)S(1)}, u32[]{:S(2)}, u32[]{:S(2)}) collective-permute-start(bf16[72,3200]{1,0:T(8,128)(2,1)S(1)} %get-tuple-element.15), channel_id=1, source_target_pairs={{0,47},{1,0},{2,1},{3,2},{4,3},{5,4},{6,5},{7,6},{8,7},{9,8},{10,9... | collective-permute-start | bytes 1382408 | tf_op jit(solution)/shard_map/ppermute | solution.py:116
  175.5 45.4 %copy-start.4 = (f32[3200]{0:T(1024)S(1)}, f32[3200]{0:T(1024)}, u32[]{:S(2)}) copy-start(f32[3200]{0:T(1024)} %param.16) | copy-start | bytes 38404
  175.5 45.4 %copy-start.5 = (f32[3200]{0:T(1024)S(1)}, f32[3200]{0:T(1024)}, u32[]{:S(2)}) copy-start(f32[3200]{0:T(1024)} %param.17) | copy-start | bytes 38404
  175.6 11.6 %collective-permute-start.14 = (bf16[72,3200]{1,0:T(8,128)(2,1)S(1)}, bf16[72,3200]{1,0:T(8,128)(2,1)S(1)}, u32[]{:S(2)}, u32[]{:S(2)}) collective-permute-start(bf16[72,3200]{1,0:T(8,128)(2,1)S(1)} %get-tuple-element.16), channel_id=1, source_target_pairs={{0,1},{1,2},{2,3},{3,4},{4,5},{5,6},{6,7},{7,8},{8,9},{9,10},{10,1... | collective-permute-start | bytes 1382408 | tf_op jit(solution)/shard_map/ppermute | solution.py:116
  178.4 16.6 %collective-permute-start.11 = (bf16[24,3200]{1,0:T(8,128)(2,1)S(1)}, bf16[24,3200]{1,0:T(8,128)(2,1)S(1)}, u32[]{:S(2)}, u32[]{:S(2)}) collective-permute-start(bf16[24,3200]{1,0:T(8,128)(2,1)S(1)} %slice.58), channel_id=1, source_target_pairs={{0,45},{1,46},{2,47},{3,0},{4,1},{5,2},{6,3},{7,4},{8,5},{9,6},{10... | collective-permute-start | bytes 460808 | tf_op jit(solution)/shard_map/ppermute | solution.py:116
  187.3 22.4 %collective-permute-start.15 = (bf16[24,3200]{1,0:T(8,128)(2,1)S(1)}, bf16[24,3200]{1,0:T(8,128)(2,1)S(1)}, u32[]{:S(2)}, u32[]{:S(2)}) collective-permute-start(bf16[24,3200]{1,0:T(8,128)(2,1)S(1)} %slice.64), channel_id=1, source_target_pairs={{0,3},{1,4},{2,5},{3,6},{4,7},{5,8},{6,9},{7,10},{8,11},{9,12},{10... | collective-permute-start | bytes 460808 | tf_op jit(solution)/shard_map/ppermute | solution.py:116
  195.1 16.6 %collective-permute-start.12 = (bf16[24,3200]{1,0:T(8,128)(2,1)S(1)}, bf16[24,3200]{1,0:T(8,128)(2,1)S(1)}, u32[]{:S(2)}, u32[]{:S(2)}) collective-permute-start(bf16[24,3200]{1,0:T(8,128)(2,1)S(1)} %add_convert_fusion.6), channel_id=1, source_target_pairs={{0,45},{1,46},{2,47},{3,0},{4,1},{5,2},{6,3},{7,4},{8,5},{9,6},{10... | collective-permute-start | bytes 460808 | tf_op jit(solution)/shard_map/ppermute | solution.py:116
  209.8 11.1 %collective-permute-start.16 = (bf16[24,3200]{1,0:T(8,128)(2,1)S(1)}, bf16[24,3200]{1,0:T(8,128)(2,1)S(1)}, u32[]{:S(2)}, u32[]{:S(2)}) collective-permute-start(bf16[24,3200]{1,0:T(8,128)(2,1)S(1)} %add_convert_fusion.5), channel_id=1, source_target_pairs={{0,3},{1,4},{2,5},{3,6},{4,7},{5,8},{6,9},{7,10},{8,11},{9,12},{10... | collective-permute-start | bytes 460808 | tf_op jit(solution)/shard_map/ppermute | solution.py:116

commit v3 on v2

v3 whole, which is shorter than its diff:
```python
import jax
import jax.numpy as jnp
from jax import lax
from jax.experimental import pallas as pl
from jax.experimental.pallas import tpu as pltpu
from jax.sharding import PartitionSpec as P

AXES = ("section", "dp")


def shift_pairs(sections, dps, hops):
    ring = 2 * dps
    pairs = []
    for section in range(sections):
        for dp in range(dps):
            there = (section // 2 % 2 * dps + dp + hops) % ring
            target = (section // 4 * 2 + there // dps) * 2 + section % 2
            pairs.append((section * dps + dp, target * dps + there % dps))
    return pairs


def opposite_pairs(sections, dps, hops):
    up, down = shift_pairs(sections, dps, hops), shift_pairs(sections, dps, -hops)
    return [up[i] if i // dps % 2 == 0 else down[i] for i in range(sections * dps)]


def half_groups(sections):
    return [[s for s in range(sections) if s // 2 % 2 == half] for half in range(2)]


def plan_kernel(mine_ref, live_ref, order_ref, patches_ref, rows_ref, pick_far_ref, pick_near_ref):
    sections = live_ref.shape[1]
    keep = pick_far_ref.shape[0]
    mine = mine_ref[0]
    my_half = mine // 2 % 2
    live = live_ref[...].astype(jnp.float32)
    order = order_ref[...]
    down = lax.broadcasted_iota(jnp.int32, (sections, sections), 0)
    along = lax.broadcasted_iota(jnp.int32, (sections, sections), 1)
    live_down = jnp.sum(jnp.where(down == along, live, 0.0), axis=1, keepdims=True)
    starts_down = jnp.sum(jnp.where(along < down, live, 0.0), axis=1, keepdims=True)
    is_me = lax.broadcasted_iota(jnp.int32, (sections, 1), 0) == mine
    my_start = jnp.sum(jnp.where(is_me, starts_down, 0.0), axis=0, keepdims=True)
    my_live = jnp.sum(jnp.where(is_me, live_down, 0.0), axis=0, keepdims=True)
    peer = down // 2
    toward = jnp.where(down % 2 == 0, 1 - my_half, my_half)
    target = peer // 2 * 4 + toward * 2 + peer % 2
    place = jnp.sum(jnp.where(order == target, along, 0).astype(jnp.float32), axis=1, keepdims=True)
    slot = (place - my_start).astype(jnp.int32) & (sections - 1)
    wanted = (along == slot) & (slot.astype(jnp.float32) < my_live)
    move = jnp.where(wanted, 1.0, 0.0).astype(jnp.bfloat16)
    rows_ref[...] = jnp.dot(
        move, patches_ref[...], preferred_element_type=jnp.float32
    ).astype(jnp.bfloat16)
    lane = lax.broadcasted_iota(jnp.int32, (sections, sections), 1)
    source = lane // 4 * 4 + my_half * 2 + lane // 2 % 2
    from_it = down == source
    first = jnp.sum(jnp.where(from_it, starts_down, 0.0), axis=0, keepdims=True)
    last = first + jnp.sum(jnp.where(from_it, live_down, 0.0), axis=0, keepdims=True)
    rounds = lax.broadcasted_iota(jnp.int32, (keep, sections), 0) * sections
    lanes = lax.broadcasted_iota(jnp.int32, (1, sections), 1)
    for parity, owner, pick_ref in ((0, mine ^ 2, pick_far_ref), (1, mine, pick_near_ref)):
        at = jnp.sum(jnp.where(order == owner, lanes, 0).astype(jnp.float32), axis=1, keepdims=True)
        number = rounds.astype(jnp.float32) + at
        held = (number >= first) & (number < last) & (lanes % 2 == parity)
        pick_ref[...] = jnp.where(held, 1.0, 0.0).astype(jnp.bfloat16)


def plan(patches, live, order, mine, keep):
    slots, width = patches.shape
    vmem = pl.BlockSpec(memory_space=pltpu.VMEM)
    return pl.pallas_call(
        plan_kernel,
        out_shape=(
            jax.ShapeDtypeStruct((slots, width), jnp.bfloat16),
            jax.ShapeDtypeStruct((keep, slots), jnp.bfloat16),
            jax.ShapeDtypeStruct((keep, slots), jnp.bfloat16),
        ),
        in_specs=[pl.BlockSpec(memory_space=pltpu.SMEM), vmem, vmem, vmem],
        out_specs=(vmem, vmem, vmem),
        compiler_params=pltpu.CompilerParams(vmem_limit_bytes=16 * 1024 * 1024),
    )(mine[None], live, order, patches)


def pick(chosen, rows):
    return jnp.dot(chosen, rows, preferred_element_type=jnp.float32).astype(jnp.bfloat16)


def per_device(
    patches, live, rounds, ln_gain, fc1_weight, fc1_bias, fc2_weight, fc2_bias, layer_scale
):
    sections = lax.axis_size("section")
    dps = lax.axis_size("dp")
    mine = lax.axis_index("section").astype(jnp.int32)
    keep = 3 * sections // 8
    groups = half_groups(sections)
    width, units = fc1_weight.shape
    f32 = jnp.float32

    def send(value, hops):
        return lax.ppermute(value, AXES, shift_pairs(sections, dps, hops))

    pieces = sections // 4
    depth = units // pieces
    first = (mine >> 2) * depth
    upper = (mine & 1) == 0
    chosen = first + lax.broadcasted_iota(jnp.int32, (depth, units), 0)
    chosen = (chosen == lax.broadcasted_iota(jnp.int32, (depth, units), 1)).astype(jnp.bfloat16)
    piece1 = lax.dot_general(
        chosen, fc1_weight, (((1,), (1,)), ((), ())), preferred_element_type=f32
    ).astype(jnp.bfloat16)
    piece2 = lax.dynamic_slice_in_dim(fc2_weight, first, depth, axis=0)
    piece = lax.ppermute(
        jnp.where(upper, piece1, piece2), AXES, opposite_pairs(sections, dps, dps // 2)
    )
    rows, pick_far, pick_near = plan(patches[0], live, rounds, mine, keep)
    rows = lax.all_to_all(
        rows, "section", split_axis=0, concat_axis=0, axis_index_groups=groups, tiled=True
    )
    piece = lax.optimization_barrier((piece, rows))[0]
    away_bias = send(fc1_bias, dps // 2)
    fetched = lax.all_gather(
        piece, "section", axis=0, axis_index_groups=groups, tiled=True
    ).reshape(pieces, 2, depth, width)
    away1 = fetched[:, 0].reshape(units, width)
    away2 = fetched[:, 1].reshape(units, width)
    routed = pick(pick_near, rows) + send(pick(pick_far, rows), dps)

    rows32 = routed.astype(f32)
    mean = jnp.mean(rows32, axis=1, keepdims=True)
    centered = rows32 - mean
    var = jnp.mean(centered * centered, axis=1, keepdims=True)
    normed = (centered * lax.rsqrt(var + 1e-06) * ln_gain).astype(jnp.bfloat16)

    up2, down2 = send(normed, 2), send(normed, -2)
    up13 = send(jnp.concatenate([normed, up2], axis=0), 1)
    down13 = send(jnp.concatenate([normed, down2], axis=0), -1)
    up4 = send(up2, 2)
    blocks = jnp.concatenate([up13, up2, up4, down13, down2, normed], axis=0)

    pre = jnp.dot(blocks, fc1_weight, preferred_element_type=f32) + fc1_bias
    hidden = jax.nn.gelu(pre, approximate=False).astype(jnp.bfloat16)
    part = jnp.dot(hidden, fc2_weight, preferred_element_type=f32)
    pre = lax.dot_general(
        blocks, away1, (((1,), (1,)), ((), ())), preferred_element_type=f32
    ) + away_bias
    hidden = jax.nn.gelu(pre, approximate=False).astype(jnp.bfloat16)
    part = (part + jnp.dot(hidden, away2, preferred_element_type=f32)).astype(jnp.bfloat16)

    def add(*parts):
        return sum(p.astype(f32) for p in parts)

    up02 = send(part[: 2 * keep], -1)
    up_far = send(part[3 * keep : 4 * keep], -2)
    down02 = send(part[4 * keep : 6 * keep], 1)
    up_sum = add(part[2 * keep : 3 * keep], up02[keep:], up_far).astype(jnp.bfloat16)
    down_sum = add(part[6 * keep : 7 * keep], down02[keep:]).astype(jnp.bfloat16)
    summed = add(send(up_sum, -2), up02[:keep], send(down_sum, 2), down02[:keep], part[7 * keep :])
    encoded = (rows32 + layer_scale * (summed + fc2_bias)).astype(jnp.bfloat16)
    return encoded[None]


def solution(mesh):
    placed = (
        P("dp", "section", None),
        P("dp", None),
        P("dp", None),
        P(),
        P(None, "dp"),
        P("dp"),
        P("dp", None),
        P(),
        P(),
    )
    return jax.shard_map(
        per_device, mesh=mesh, in_specs=placed, out_specs=P("dp", "section", None), check_vma=False
    )
```

time: 223 us -> 212 us (0.951)
  the two profiles are of different devices: /device:TPU:16 before, /device:TPU:34 now
where the time goes in v3:
time: 212 us
  starting transfers between devices  117 us (55%)
  waiting for transfers between devices  48.9 us (23%)
  matrix products  20.4 us (10%)
  between operations  13.7 us (6%)
  local copies, waits for them, and re-layouts  9.9 us (5%)
    ppermute x12, starting transfers between devices, send(): return lax.ppermute(value, AXES, shift_pairs(sections, dps, hops))  93.7 us
    ppermute x12, waiting for transfers between devices, send(): return lax.ppermute(value, AXES, shift_pairs(sections, dps, hops))  35 us
    ppermute x1, starting transfers between devices, per_device(): lax.ppermute(jnp.where(upper, piece1, piece2), AXES, opposite_pairs(secti...  15.7 us
    ppermute x1, waiting for transfers between devices, per_device(): lax.ppermute(jnp.where(upper, piece1, piece2), AXES, opposite_pairs(secti...  13.9 us
    dot_general x1, matrix products, per_device(): part = jnp.dot(hidden, fc2_weight, preferred_element_type=f32)  8.33 us
    dot_general x1, matrix products, per_device(): jnp.dot(hidden, away2, preferred_element_type=f32)  8.15 us
    all_to_all x1, starting transfers between devices, per_device(): lax.all_to_all(rows, 'section', split_axis=0, concat_axis=0, axis_index_g...  7.62 us
    slice x1, local copies, waits for them, and re-layouts, per_device(): away1 = fetched[:, 0].reshape(units, width)  5.62 us
  transfers between devices with their start and end apart: 15, of which 8 were waited for; matrix products, arithmetic and copies ran while one was open for 9% of the time, Pallas kernels for 0%

profile of v3, /device:TPU:34, one launch (start us, length us, event | category | flops | bytes accessed | tf_op | source)
XLA Modules:
  0.0 211.7 jit_solution(18118900742258137622)
XLA Ops:
  6.5 0.0 copy-start
  6.5 1.0 copy-done
  7.5 0.0 copy-start.1
  7.5 0.7 copy-done.1
  8.2 0.0 copy-start.2
  8.2 0.7 copy-done.2
  8.8 0.3 shard_map.91
  9.2 0.9 all_to_all.8
  10.1 7.6 %all-to-all-start = ((bf16[32,2,3200]{2,1,0:T(2,128)(2,1)}), bf16[32,2,3200]{2,1,0:T(2,128)(2,1)S(1)}, u32[]{:S(2)}, u32[]{:S(2)}) async-start(bf16[32,2,3200]{2,1,0:T(2,128)(2,1)} %all_to_all.8), calls=%async_computation | async-start | bytes 819200 | tf_op jit(solution)/shard_map/all_to_all | solution.py:117
  17.7 0.0 all-gather.2.cloned.1.call-start
  17.8 3.4 %fusion.1 = bf16[40,3200]{1,0:T(8,128)(2,1)S(1)} fusion(bf16[3200,640]{1,0:T(8,128)(2,1)} %param.13, bf16[640,3200]{1,0:T(8,128)(2,1)} %param.15, s32[]{:T(128)S(6)} %select_n.12, pred[]{:T(512)S(6)} %eq.6, s32[40]{0:T(128)S(1)} %iota_add_fusion), kind=kOutput, calls=%fused_computation.3 | convolution fusion | flops 164121600 | bytes 4608165 | tf_op jit(solution)/shard_map/dot_general | solution.py:109
  21.3 0.0 copy-start.4
  21.3 0.0 copy-start.7
  21.3 15.7 %collective-permute-start.6 = (bf16[40,3200]{1,0:T(8,128)(2,1)S(1)}, bf16[40,3200]{1,0:T(8,128)(2,1)S(1)}, u32[]{:S(2)}, u32[]{:S(2)}) collective-permute-start(bf16[40,3200]{1,0:T(8,128)(2,1)S(1)} %fusion.1), channel_id=1, source_target_pairs={{0,8},{1,9},{2,10},{3,11},{4,12},{5,13},{6,14},{7,15},{8,32},{9,33... | collective-permute-start | bytes 768008 | tf_op jit(solution)/shard_map/ppermute | solution.py:113
  37.0 0.0 all-to-all-done
  37.0 0.2 all_to_all.10
  37.2 13.9 %collective-permute-done.6 = bf16[40,3200]{1,0:T(8,128)(2,1)S(1)} collective-permute-done((bf16[40,3200]{1,0:T(8,128)(2,1)S(1)}, bf16[40,3200]{1,0:T(8,128)(2,1)S(1)}, u32[]{:S(2)}, u32[]{:S(2)}) %collective-permute-start.6) | collective-permute-done | bytes 256032 | tf_op jit(solution)/shard_map/ppermute | solution.py:113
  51.0 0.0 copy-start.3
  51.1 0.7 copy-done.3
  51.8 0.0 all-gather.2.cloned.1.call-update
  51.8 0.2 convolution_convert_fusion.1
  52.0 20.3 %collective-permute-start = (bf16[24,3200]{1,0:T(8,128)(2,1)S(1)}, bf16[24,3200]{1,0:T(8,128)(2,1)S(1)}, u32[]{:S(2)}, u32[]{:S(2)}) collective-permute-start(bf16[24,3200]{1,0:T(8,128)(2,1)S(1)} %convolution_convert_fusion.1), channel_id=1, source_target_pairs={{0,32},{1,33},{2,34},{3,35},{4,36},{5,37},{6,38},{7,39},{8,40},{9,... | collective-permute-start | bytes 460808 | tf_op jit(solution)/shard_map/ppermute | solution.py:101
  72.3 5.4 %collective-permute-done = bf16[24,3200]{1,0:T(8,128)(2,1)S(1)} collective-permute-done((bf16[24,3200]{1,0:T(8,128)(2,1)S(1)}, bf16[24,3200]{1,0:T(8,128)(2,1)S(1)}, u32[]{:S(2)}, u32[]{:S(2)}) %collective-permute-start) | collective-permute-done | bytes 153632 | tf_op jit(solution)/shard_map/ppermute | solution.py:101
  77.6 0.3 fusion.151
  77.9 0.2 multiply_reduce_fusion
  78.1 0.0 copy-done.4
  78.2 0.1 multiply_convert_fusion
  78.3 36.6 %collective-permute-start.4 = (bf16[24,3200]{1,0:T(8,128)(2,1)S(1)}, bf16[24,3200]{1,0:T(8,128)(2,1)S(1)}, u32[]{:S(2)}, u32[]{:S(2)}) collective-permute-start(bf16[24,3200]{1,0:T(8,128)(2,1)S(1)} %multiply_convert_fusion), channel_id=1, source_target_pairs={{0,46},{1,47},{2,0},{3,1},{4,2},{5,3},{6,4},{7,5},{8,6},{9,7},{10,... | collective-permute-start | bytes 460808 | tf_op jit(solution)/shard_map/ppermute | solution.py:101
  114.8 1.9 collective-permute-start.1
  116.8 0.8 collective-permute-done.4
  117.6 6.5 %collective-permute-done.1 = bf16[24,3200]{1,0:T(8,128)(2,1)S(1)} collective-permute-done((bf16[24,3200]{1,0:T(8,128)(2,1)S(1)}, bf16[24,3200]{1,0:T(8,128)(2,1)S(1)}, u32[]{:S(2)}, u32[]{:S(2)}) %collective-permute-start.1) | collective-permute-done | bytes 153632 | tf_op jit(solution)/shard_map/ppermute | solution.py:101
  124.1 0.1 pad_maximum_fusion
  124.1 1.9 collective-permute-start.2
  126.0 0.0 copy-done.7
  126.1 2.1 collective-permute-start.7
  128.1 4.4 %collective-permute-start.5 = (bf16[48,3200]{1,0:T(8,128)(2,1)S(1)}, bf16[48,3200]{1,0:T(8,128)(2,1)S(1)}, u32[]{:S(2)}, u32[]{:S(2)}) collective-permute-start(bf16[48,3200]{1,0:T(8,128)(2,1)S(1)} %get-tuple-element.19), channel_id=1, source_target_pairs={{0,47},{1,0},{2,1},{3,2},{4,3},{5,4},{6,5},{7,6},{8,7},{9,8},{10,9... | collective-permute-start | bytes 921608 | tf_op jit(solution)/shard_map/ppermute | solution.py:101
  132.6 4.8 %collective-permute-start.3 = (bf16[24,3200]{1,0:T(8,128)(2,1)S(1)}, bf16[24,3200]{1,0:T(8,128)(2,1)S(1)}, u32[]{:S(2)}, u32[]{:S(2)}) collective-permute-start(bf16[24,3200]{1,0:T(8,128)(2,1)S(1)} %collective-permute-done.1), channel_id=1, source_target_pairs={{0,2},{1,3},{2,4},{3,5},{4,6},{5,7},{6,8},{7,9},{8,10},{9,11},{10,... | collective-permute-start | bytes 460808 | tf_op jit(solution)/shard_map/ppermute | solution.py:101
  137.4 0.0 collective-permute-done.2
  137.4 7.8 %collective-permute-done.3 = bf16[24,3200]{1,0:T(8,128)(2,1)S(1)} collective-permute-done((bf16[24,3200]{1,0:T(8,128)(2,1)S(1)}, bf16[24,3200]{1,0:T(8,128)(2,1)S(1)}, u32[]{:S(2)}, u32[]{:S(2)}) %collective-permute-start.3) | collective-permute-done | bytes 153632 | tf_op jit(solution)/shard_map/ppermute | solution.py:101
  145.2 0.0 collective-permute-done.5
  145.3 0.1 constant_dynamic-update-slice_fusion
  145.4 8.3 %fusion.24 = f32[192,3200]{1,0:T(8,128)} fusion(bf16[640,3200]{1,0:T(8,128)(2,1)} %param.15, bf16[192,3200]{1,0:T(8,128)(2,1)S(1)} %constant_dynamic-update-slice_fusion, bf16[3200,640]{1,0:T(8,128)(2,1)} %param.13, f32[640]{0:T(1024)S(1)} %copy-done.7), kind=kOutput, calls=%fused_computation.48 | convolution fusion | flops 1580974080 | bytes 11880960 | tf_op jit(solution)/shard_map/dot_general | solution.py:143
  153.7 0.0 all-gather.2.cloned.1.call-done
  153.7 5.6 %fusion.149 = (bf16[16,1,40,3200]{3,2,1,0:T(8,128)(2,1)}, bf16[16,1,40,3200]{3,2,1,0:T(8,128)(2,1)}) fusion(bf16[16,2,40,3200]{3,2,1,0:T(8,128)(2,1)} %bitcast.19), kind=kLoop, calls=%fused_computation.190 | loop fusion | bytes 16384000 | tf_op jit(solution)/shard_map/slice | solution.py:125
  159.4 0.0 collective-permute-done.7
  159.4 8.2 %fusion = bf16[192,3200]{1,0:T(8,128)(2,1)S(1)} fusion(f32[192,3200]{1,0:T(8,128)} %fusion.24, bf16[640,3200]{1,0:T(8,128)(2,1)} %bitcast.21, bf16[192,3200]{1,0:T(8,128)(2,1)S(1)} %constant_dynamic-update-slice_fusion, bf16[640,3200]{1,0:T(8,128)(2,1)} %bitcast.20, f32[640]{0:T(1024)S(1)} %collective-permute-done.7), kind=kOutput, calls=%fused_computation.1 | convolution fusion | flops 1582202880 | bytes 13109760 | tf_op jit(solution)/shard_map/dot_general | solution.py:148
  167.5 0.0 copy-start.5
  167.5 0.0 copy-start.6
  167.6 1.9 collective-permute-start.8
  169.5 3.9 %collective-permute-start.11 = (bf16[48,3200]{1,0:T(8,128)(2,1)S(1)}, bf16[48,3200]{1,0:T(8,128)(2,1)S(1)}, u32[]{:S(2)}, u32[]{:S(2)}) collective-permute-start(bf16[48,3200]{1,0:T(8,128)(2,1)S(1)} %get-tuple-element.18), channel_id=1, source_target_pairs={{0,1},{1,2},{2,3},{3,4},{4,5},{5,6},{6,7},{7,8},{8,9},{9,10},{10,1... | collective-permute-start | bytes 921608 | tf_op jit(solution)/shard_map/ppermute | solution.py:101
  173.5 7.5 %collective-permute-start.9 = (bf16[24,3200]{1,0:T(8,128)(2,1)S(1)}, bf16[24,3200]{1,0:T(8,128)(2,1)S(1)}, u32[]{:S(2)}, u32[]{:S(2)}) collective-permute-start(bf16[24,3200]{1,0:T(8,128)(2,1)S(1)} %slice.53), channel_id=1, source_target_pairs={{0,46},{1,47},{2,0},{3,1},{4,2},{5,3},{6,4},{7,5},{8,6},{9,7},{10,... | collective-permute-start | bytes 460808 | tf_op jit(solution)/shard_map/ppermute | solution.py:101
  180.9 5.6 %collective-permute-done.9 = bf16[24,3200]{1,0:T(8,128)(2,1)S(1)} collective-permute-done((bf16[24,3200]{1,0:T(8,128)(2,1)S(1)}, bf16[24,3200]{1,0:T(8,128)(2,1)S(1)}, u32[]{:S(2)}, u32[]{:S(2)}) %collective-permute-start.9) | collective-permute-done | bytes 153632 | tf_op jit(solution)/shard_map/ppermute | solution.py:101
  186.6 0.0 collective-permute-done.8
  186.6 0.0 collective-permute-done.11
  186.6 0.1 add_convert_fusion.2
  186.7 6.5 %collective-permute-start.10 = (bf16[24,3200]{1,0:T(8,128)(2,1)S(1)}, bf16[24,3200]{1,0:T(8,128)(2,1)S(1)}, u32[]{:S(2)}, u32[]{:S(2)}) collective-permute-start(bf16[24,3200]{1,0:T(8,128)(2,1)S(1)} %get-tuple-element.15), channel_id=1, source_target_pairs={{0,46},{1,47},{2,0},{3,1},{4,2},{5,3},{6,4},{7,5},{8,6},{9,7},{10,... | collective-permute-start | bytes 460808 | tf_op jit(solution)/shard_map/ppermute | solution.py:101
  193.2 1.9 collective-permute-start.12
  195.1 3.0 %collective-permute-done.10 = bf16[24,3200]{1,0:T(8,128)(2,1)S(1)} collective-permute-done((bf16[24,3200]{1,0:T(8,128)(2,1)S(1)}, bf16[24,3200]{1,0:T(8,128)(2,1)S(1)}, u32[]{:S(2)}, u32[]{:S(2)}) %collective-permute-start.10) | collective-permute-done | bytes 153632 | tf_op jit(solution)/shard_map/ppermute | solution.py:101
  198.1 6.0 %collective-permute-done.12 = bf16[24,3200]{1,0:T(8,128)(2,1)S(1)} collective-permute-done((bf16[24,3200]{1,0:T(8,128)(2,1)S(1)}, bf16[24,3200]{1,0:T(8,128)(2,1)S(1)}, u32[]{:S(2)}, u32[]{:S(2)}) %collective-permute-start.12) | collective-permute-done | bytes 153632 | tf_op jit(solution)/shard_map/ppermute | solution.py:101
  204.1 0.0 copy-done.5
  204.1 0.0 copy-done.6
  204.1 0.8 fusion.87
  (10 shorter events, 0.2 us)
Async XLA Ops:
  6.5 1.0 copy-start
  7.5 0.7 copy-start.1
  8.2 0.7 copy-start.2
  10.1 26.9 %all-to-all-start = ((bf16[32,2,3200]{2,1,0:T(2,128)(2,1)}), bf16[32,2,3200]{2,1,0:T(2,128)(2,1)S(1)}, u32[]{:S(2)}, u32[]{:S(2)}) async-start(bf16[32,2,3200]{2,1,0:T(2,128)(2,1)} %all_to_all.8), calls=%async_computation | async-start | bytes 819200 | tf_op jit(solution)/shard_map/all_to_all | solution.py:117
  17.7 136.0 %all-gather.2.cloned.1.call-start = ((), (), s32[]{:S(2)}) async-start(), calls=%async_computation.1 | async-start | bytes 8448000 | tf_op jit(solution)/shard_map/all_gather | solution.py:122
  21.3 56.9 %copy-start.4 = (f32[3200]{0:T(1024)S(1)}, f32[3200]{0:T(1024)}, u32[]{:S(2)}) copy-start(f32[3200]{0:T(1024)} %param.12) | copy-start | bytes 38404
  21.3 104.8 %copy-start.7 = (f32[640]{0:T(1024)S(1)}, f32[640]{0:T(1024)}, u32[]{:S(2)}) copy-start(f32[640]{0:T(1024)} %param.14) | copy-start | bytes 7684
  21.3 29.8 %collective-permute-start.6 = (bf16[40,3200]{1,0:T(8,128)(2,1)S(1)}, bf16[40,3200]{1,0:T(8,128)(2,1)S(1)}, u32[]{:S(2)}, u32[]{:S(2)}) collective-permute-start(bf16[40,3200]{1,0:T(8,128)(2,1)S(1)} %fusion.1), channel_id=1, source_target_pairs={{0,8},{1,9},{2,10},{3,11},{4,12},{5,13},{6,14},{7,15},{8,32},{9,33... | collective-permute-start | bytes 768008 | tf_op jit(solution)/shard_map/ppermute | solution.py:113
  51.0 0.7 copy-start.3
  52.0 25.6 %collective-permute-start = (bf16[24,3200]{1,0:T(8,128)(2,1)S(1)}, bf16[24,3200]{1,0:T(8,128)(2,1)S(1)}, u32[]{:S(2)}, u32[]{:S(2)}) collective-permute-start(bf16[24,3200]{1,0:T(8,128)(2,1)S(1)} %convolution_convert_fusion.1), channel_id=1, source_target_pairs={{0,32},{1,33},{2,34},{3,35},{4,36},{5,37},{6,38},{7,39},{8,40},{9,... | collective-permute-start | bytes 460808 | tf_op jit(solution)/shard_map/ppermute | solution.py:101
  78.3 39.3 %collective-permute-start.4 = (bf16[24,3200]{1,0:T(8,128)(2,1)S(1)}, bf16[24,3200]{1,0:T(8,128)(2,1)S(1)}, u32[]{:S(2)}, u32[]{:S(2)}) collective-permute-start(bf16[24,3200]{1,0:T(8,128)(2,1)S(1)} %multiply_convert_fusion), channel_id=1, source_target_pairs={{0,46},{1,47},{2,0},{3,1},{4,2},{5,3},{6,4},{7,5},{8,6},{9,7},{10,... | collective-permute-start | bytes 460808 | tf_op jit(solution)/shard_map/ppermute | solution.py:101
  114.8 9.2 %collective-permute-start.1 = (bf16[24,3200]{1,0:T(8,128)(2,1)S(1)}, bf16[24,3200]{1,0:T(8,128)(2,1)S(1)}, u32[]{:S(2)}, u32[]{:S(2)}) collective-permute-start(bf16[24,3200]{1,0:T(8,128)(2,1)S(1)} %multiply_convert_fusion), channel_id=1, source_target_pairs={{0,2},{1,3},{2,4},{3,5},{4,6},{5,7},{6,8},{7,9},{8,10},{9,11},{10,... | collective-permute-start | bytes 460808 | tf_op jit(solution)/shard_map/ppermute | solution.py:101
  124.1 13.2 %collective-permute-start.2 = (bf16[48,3200]{1,0:T(8,128)(2,1)S(1)}, bf16[48,3200]{1,0:T(8,128)(2,1)S(1)}, u32[]{:S(2)}, u32[]{:S(2)}) collective-permute-start(bf16[48,3200]{1,0:T(8,128)(2,1)S(1)} %get-tuple-element.20), channel_id=1, source_target_pairs={{0,1},{1,2},{2,3},{3,4},{4,5},{5,6},{6,7},{7,8},{8,9},{9,10},{10,1... | collective-permute-start | bytes 921608 | tf_op jit(solution)/shard_map/ppermute | solution.py:101
  126.1 33.3 %collective-permute-start.7 = (f32[640]{0:T(1024)S(1)}, f32[640]{0:T(1024)S(1)}, u32[]{:S(2)}, u32[]{:S(2)}) collective-permute-start(f32[640]{0:T(1024)S(1)} %copy-done.7), channel_id=1, source_target_pairs={{0,8},{1,9},{2,10},{3,11},{4,12},{5,13},{6,14},{7,15},{8,32},{9,33... | collective-permute-start | bytes 7688 | tf_op jit(solution)/shard_map/ppermute | solution.py:101
  128.1 17.1 %collective-permute-start.5 = (bf16[48,3200]{1,0:T(8,128)(2,1)S(1)}, bf16[48,3200]{1,0:T(8,128)(2,1)S(1)}, u32[]{:S(2)}, u32[]{:S(2)}) collective-permute-start(bf16[48,3200]{1,0:T(8,128)(2,1)S(1)} %get-tuple-element.19), channel_id=1, source_target_pairs={{0,47},{1,0},{2,1},{3,2},{4,3},{5,4},{6,5},{7,6},{8,7},{9,8},{10,9... | collective-permute-start | bytes 921608 | tf_op jit(solution)/shard_map/ppermute | solution.py:101
  132.6 12.6 %collective-permute-start.3 = (bf16[24,3200]{1,0:T(8,128)(2,1)S(1)}, bf16[24,3200]{1,0:T(8,128)(2,1)S(1)}, u32[]{:S(2)}, u32[]{:S(2)}) collective-permute-start(bf16[24,3200]{1,0:T(8,128)(2,1)S(1)} %collective-permute-done.1), channel_id=1, source_target_pairs={{0,2},{1,3},{2,4},{3,5},{4,6},{5,7},{6,8},{7,9},{8,10},{9,11},{10,... | collective-permute-start | bytes 460808 | tf_op jit(solution)/shard_map/ppermute | solution.py:101
  167.5 36.5 %copy-start.5 = (f32[3200]{0:T(1024)S(1)}, f32[3200]{0:T(1024)}, u32[]{:S(2)}) copy-start(f32[3200]{0:T(1024)} %param.16) | copy-start | bytes 38404
  167.5 36.5 %copy-start.6 = (f32[3200]{0:T(1024)S(1)}, f32[3200]{0:T(1024)}, u32[]{:S(2)}) copy-start(f32[3200]{0:T(1024)} %param.17) | copy-start | bytes 38404
  167.6 19.0 %collective-permute-start.8 = (bf16[48,3200]{1,0:T(8,128)(2,1)S(1)}, bf16[48,3200]{1,0:T(8,128)(2,1)S(1)}, u32[]{:S(2)}, u32[]{:S(2)}) collective-permute-start(bf16[48,3200]{1,0:T(8,128)(2,1)S(1)} %get-tuple-element.17), channel_id=1, source_target_pairs={{0,47},{1,0},{2,1},{3,2},{4,3},{5,4},{6,5},{7,6},{8,7},{9,8},{10,9... | collective-permute-start | bytes 921608 | tf_op jit(solution)/shard_map/ppermute | solution.py:101
  169.5 17.0 %collective-permute-start.11 = (bf16[48,3200]{1,0:T(8,128)(2,1)S(1)}, bf16[48,3200]{1,0:T(8,128)(2,1)S(1)}, u32[]{:S(2)}, u32[]{:S(2)}) collective-permute-start(bf16[48,3200]{1,0:T(8,128)(2,1)S(1)} %get-tuple-element.18), channel_id=1, source_target_pairs={{0,1},{1,2},{2,3},{3,4},{4,5},{5,6},{6,7},{7,8},{8,9},{9,10},{10,1... | collective-permute-start | bytes 921608 | tf_op jit(solution)/shard_map/ppermute | solution.py:101
  173.5 13.1 %collective-permute-start.9 = (bf16[24,3200]{1,0:T(8,128)(2,1)S(1)}, bf16[24,3200]{1,0:T(8,128)(2,1)S(1)}, u32[]{:S(2)}, u32[]{:S(2)}) collective-permute-start(bf16[24,3200]{1,0:T(8,128)(2,1)S(1)} %slice.53), channel_id=1, source_target_pairs={{0,46},{1,47},{2,0},{3,1},{4,2},{5,3},{6,4},{7,5},{8,6},{9,7},{10,... | collective-permute-start | bytes 460808 | tf_op jit(solution)/shard_map/ppermute | solution.py:101
  186.7 11.4 %collective-permute-start.10 = (bf16[24,3200]{1,0:T(8,128)(2,1)S(1)}, bf16[24,3200]{1,0:T(8,128)(2,1)S(1)}, u32[]{:S(2)}, u32[]{:S(2)}) collective-permute-start(bf16[24,3200]{1,0:T(8,128)(2,1)S(1)} %get-tuple-element.15), channel_id=1, source_target_pairs={{0,46},{1,47},{2,0},{3,1},{4,2},{5,3},{6,4},{7,5},{8,6},{9,7},{10,... | collective-permute-start | bytes 460808 | tf_op jit(solution)/shard_map/ppermute | solution.py:101
  193.2 10.9 %collective-permute-start.12 = (bf16[24,3200]{1,0:T(8,128)(2,1)S(1)}, bf16[24,3200]{1,0:T(8,128)(2,1)S(1)}, u32[]{:S(2)}, u32[]{:S(2)}) collective-permute-start(bf16[24,3200]{1,0:T(8,128)(2,1)S(1)} %get-tuple-element.16), channel_id=1, source_target_pairs={{0,2},{1,3},{2,4},{3,5},{4,6},{5,7},{6,8},{7,9},{8,10},{9,11},{10,... | collective-permute-start | bytes 460808 | tf_op jit(solution)/shard_map/ppermute | solution.py:101
Sparse Core Ops, SparseCore 0:
  51.9 100.6 all-gather.1

commit v4 on v3

--- a/solution.py
+++ b/solution.py
@@ -1,5 +1,6 @@
 import jax
 import jax.numpy as jnp
+import numpy as np
 from jax import lax
 from jax.experimental import pallas as pl
 from jax.experimental.pallas import tpu as pltpu
@@ -82,6 +83,45 @@
     )(mine[None], live, order, patches)
 
 
+def away_kernel(rows_ref, part_ref, bias_ref, fetched_ref, out_ref, w1, w2, hidden, sems):
+    units, width = w1.shape
+    first = pltpu.make_async_copy(fetched_ref.at[pl.ds(0, units)], w1, sems.at[0])
+    second = pltpu.make_async_copy(fetched_ref.at[pl.ds(units, units)], w2, sems.at[1])
+    first.start()
+    second.start()
+    first.wait()
+    for at in range(0, units, 256):
+        span = pl.ds(at, min(256, units - at))
+        pre = lax.dot_general(
+            rows_ref[...], w1[span], (((1,), (1,)), ((), ())), preferred_element_type=jnp.float32
+        ) + bias_ref[:, span]
+        hidden[:, span] = (0.5 * pre * (1.0 + lax.erf(pre * np.float32(0.5**0.5)))).astype(jnp.bfloat16)
+    second.wait()
+    for at in range(0, width, 640):
+        span = pl.ds(at, min(640, width - at))
+        out = jnp.dot(hidden[...], w2[:, span], preferred_element_type=jnp.float32)
+        out_ref[:, span] = (part_ref[:, span] + out).astype(jnp.bfloat16)
+
+
+def add_away(rows, part, bias, fetched):
+    count, width = rows.shape
+    units = bias.shape[0]
+    vmem = pl.BlockSpec(memory_space=pltpu.VMEM)
+    return pl.pallas_call(
+        away_kernel,
+        out_shape=jax.ShapeDtypeStruct((count, width), jnp.bfloat16),
+        in_specs=[vmem, vmem, vmem, pl.BlockSpec(memory_space=pl.ANY)],
+        out_specs=vmem,
+        scratch_shapes=[
+            pltpu.VMEM((units, width), jnp.bfloat16),
+            pltpu.VMEM((units, width), jnp.bfloat16),
+            pltpu.VMEM((count, units), jnp.bfloat16),
+            pltpu.SemaphoreType.DMA((2,)),
+        ],
+        compiler_params=pltpu.CompilerParams(vmem_limit_bytes=28 * 1024 * 1024),
+    )(rows, part, bias[None], fetched)
+
+
 def pick(chosen, rows):
     return jnp.dot(chosen, rows, preferred_element_type=jnp.float32).astype(jnp.bfloat16)
 
@@ -102,29 +142,29 @@
 
     pieces = sections // 4
     depth = units // pieces
-    first = (mine >> 2) * depth
-    upper = (mine & 1) == 0
+    member = (mine >> 2) * 2 + (mine & 1)
+    first = (member & (pieces - 1)) * depth
+    upper = member < pieces
     chosen = first + lax.broadcasted_iota(jnp.int32, (depth, units), 0)
     chosen = (chosen == lax.broadcasted_iota(jnp.int32, (depth, units), 1)).astype(jnp.bfloat16)
     piece1 = lax.dot_general(
         chosen, fc1_weight, (((1,), (1,)), ((), ())), preferred_element_type=f32
     ).astype(jnp.bfloat16)
     piece2 = lax.dynamic_slice_in_dim(fc2_weight, first, depth, axis=0)
-    piece = lax.ppermute(
-        jnp.where(upper, piece1, piece2), AXES, opposite_pairs(sections, dps, dps // 2)
-    )
+    piece = jnp.where(upper, piece1, piece2)
     rows, pick_far, pick_near = plan(patches[0], live, rounds, mine, keep)
+    piece, rows = lax.optimization_barrier((piece, rows))
+    piece = lax.ppermute(piece, AXES, opposite_pairs(sections, dps, dps // 2))
     rows = lax.all_to_all(
         rows, "section", split_axis=0, concat_axis=0, axis_index_groups=groups, tiled=True
     )
     piece = lax.optimization_barrier((piece, rows))[0]
-    away_bias = send(fc1_bias, dps // 2)
-    fetched = lax.all_gather(
-        piece, "section", axis=0, axis_index_groups=groups, tiled=True
-    ).reshape(pieces, 2, depth, width)
-    away1 = fetched[:, 0].reshape(units, width)
-    away2 = fetched[:, 1].reshape(units, width)
-    routed = pick(pick_near, rows) + send(pick(pick_far, rows), dps)
+    fetched = lax.all_gather(piece, "section", axis=0, axis_index_groups=groups, tiled=True)
+    crossing = pick(pick_far, rows)
+    bias = lax.optimization_barrier((fc1_bias, crossing))[0]
+    away_bias = send(bias, dps // 2)
+    crossed, away_bias = lax.optimization_barrier((send(crossing, dps), away_bias))
+    routed = pick(pick_near, rows) + crossed
 
     rows32 = routed.astype(f32)
     mean = jnp.mean(rows32, axis=1, keepdims=True)
@@ -141,11 +181,7 @@
     pre = jnp.dot(blocks, fc1_weight, preferred_element_type=f32) + fc1_bias
     hidden = jax.nn.gelu(pre, approximate=False).astype(jnp.bfloat16)
     part = jnp.dot(hidden, fc2_weight, preferred_element_type=f32)
-    pre = lax.dot_general(
-        blocks, away1, (((1,), (1,)), ((), ())), preferred_element_type=f32
-    ) + away_bias
-    hidden = jax.nn.gelu(pre, approximate=False).astype(jnp.bfloat16)
-    part = (part + jnp.dot(hidden, away2, preferred_element_type=f32)).astype(jnp.bfloat16)
+    part = add_away(blocks, part, away_bias, fetched)
 
     def add(*parts):
         return sum(p.astype(f32) for p in parts)

time: 212 us -> 208 us (0.981)
  the two profiles are of different devices: /device:TPU:34 before, /device:TPU:32 now
where the time goes in v4:
time: 208 us; the launch traced here: 207 us
  starting transfers between devices  115 us (55%)
  waiting for transfers between devices  47.9 us (23%)
  between operations  13.7 us (7%)
  local copies, waits for them, and re-layouts  11.1 us (5%)
  matrix products  11.1 us (5%)
  Pallas kernels  6.05 us (3%)
  other arithmetic  2.25 us (1%)
    ppermute x12, starting transfers between devices, send(): return lax.ppermute(value, AXES, shift_pairs(sections, dps, hops))  91.7 us
    ppermute x12, waiting for transfers between devices, send(): return lax.ppermute(value, AXES, shift_pairs(sections, dps, hops))  33 us
    ppermute x1, starting transfers between devices, per_device(): piece = lax.ppermute(piece, AXES, opposite_pairs(sections, dps, dps // 2))  15.7 us
    ppermute x1, waiting for transfers between devices, per_device(): piece = lax.ppermute(piece, AXES, opposite_pairs(sections, dps, dps // 2))  13.9 us
    unnamed x23, local copies, waits for them, and re-layouts  9.93 us
    all_to_all x1, starting transfers between devices, per_device(): lax.all_to_all(rows, 'section', split_axis=0, concat_axis=0, axis_index_g...  7.45 us
    dot_general x1, matrix products, per_device(): part = jnp.dot(hidden, fc2_weight, preferred_element_type=f32)  7.32 us
    pallas_call x1, Pallas kernels, add_away(): pl.pallas_call(away_kernel, out_shape=jax.ShapeDtypeStruct((count, width)...  5.71 us
  transfers between devices with their start and end apart: 15, of which 10 were waited for; matrix products, arithmetic and copies ran while one was open for 6% of the time, Pallas kernels for 0%

profile of v4, /device:TPU:32, one launch (start us, length us, event | category | flops | bytes accessed | tf_op | source)
XLA Modules:
  0.0 207.1 jit_solution(6174828183197499176)
XLA Ops:
  6.5 0.0 copy-start.1
  6.5 1.0 copy-done.1
  7.5 0.0 copy-start.2
  7.5 0.7 copy-done.2
  8.2 0.7 copy-done.3
  8.9 0.3 shard_map.91
  9.2 3.4 %fusion = bf16[40,3200]{1,0:T(8,128)(2,1)S(1)} fusion(bf16[3200,640]{1,0:T(8,128)(2,1)} %param.13, bf16[640,3200]{1,0:T(8,128)(2,1)} %param.15, s32[]{:T(128)S(6)} %select_n.12, pred[]{:T(512)S(6)} %lt.6, s32[40]{0:T(128)S(1)} %iota_add_fusion), kind=kOutput, calls=%fused_computation.1 | convolution fusion | flops 164121600 | bytes 4608165 | tf_op jit(solution)/shard_map/dot_general | solution.py:150
  12.7 0.9 all_to_all.8
  13.6 7.4 %all-to-all-start = ((bf16[32,2,3200]{2,1,0:T(2,128)(2,1)}), bf16[32,2,3200]{2,1,0:T(2,128)(2,1)S(1)}, u32[]{:S(2)}, u32[]{:S(2)}) async-start(bf16[32,2,3200]{2,1,0:T(2,128)(2,1)} %all_to_all.8), calls=%async_computation | async-start | bytes 819200 | tf_op jit(solution)/shard_map/all_to_all | solution.py:158
  21.0 0.0 copy-start.5
  21.0 0.0 all-gather.2.cloned.1.call-start
  21.1 15.7 %collective-permute-start.7 = (bf16[40,3200]{1,0:T(8,128)(2,1)S(1)}, bf16[40,3200]{1,0:T(8,128)(2,1)S(1)}, u32[]{:S(2)}, u32[]{:S(2)}) collective-permute-start(bf16[40,3200]{1,0:T(8,128)(2,1)S(1)} %fusion), channel_id=1, source_target_pairs={{0,8},{1,9},{2,10},{3,11},{4,12},{5,13},{6,14},{7,15},{8,32},{9,33... | collective-permute-start | bytes 768008 | tf_op jit(solution)/shard_map/ppermute | solution.py:157
  36.8 0.0 all-to-all-done
  36.8 0.2 all_to_all.10
  37.0 13.9 %collective-permute-done.7 = bf16[40,3200]{1,0:T(8,128)(2,1)S(1)} collective-permute-done((bf16[40,3200]{1,0:T(8,128)(2,1)S(1)}, bf16[40,3200]{1,0:T(8,128)(2,1)S(1)}, u32[]{:S(2)}, u32[]{:S(2)}) %collective-permute-start.7) | collective-permute-done | bytes 256032 | tf_op jit(solution)/shard_map/ppermute | solution.py:157
  50.9 0.7 copy-done.4
  51.6 0.0 all-gather.2.cloned.1.call-update
  51.6 0.2 convolution_convert_fusion.1
  51.8 20.2 %collective-permute-start = (bf16[24,3200]{1,0:T(8,128)(2,1)S(1)}, bf16[24,3200]{1,0:T(8,128)(2,1)S(1)}, u32[]{:S(2)}, u32[]{:S(2)}) collective-permute-start(bf16[24,3200]{1,0:T(8,128)(2,1)S(1)} %convolution_convert_fusion.1), channel_id=1, source_target_pairs={{0,32},{1,33},{2,34},{3,35},{4,36},{5,37},{6,38},{7,39},{8,40},{9,... | collective-permute-start | bytes 460808 | tf_op jit(solution)/shard_map/ppermute | solution.py:141
  71.9 0.0 copy-done.8
  71.9 11.8 %collective-permute-start.1 = (f32[640]{0:T(1024)S(1)}, f32[640]{0:T(1024)S(1)}, u32[]{:S(2)}, u32[]{:S(2)}) collective-permute-start(f32[640]{0:T(1024)S(1)} %copy-done.8), channel_id=1, source_target_pairs={{0,8},{1,9},{2,10},{3,11},{4,12},{5,13},{6,14},{7,15},{8,32},{9,33... | collective-permute-start | bytes 7688 | tf_op jit(solution)/shard_map/ppermute | solution.py:141
  83.7 0.2 convolution_convert_fusion.2
  83.9 2.9 %collective-permute-done.1 = f32[640]{0:T(1024)S(1)} collective-permute-done((f32[640]{0:T(1024)S(1)}, f32[640]{0:T(1024)S(1)}, u32[]{:S(2)}, u32[]{:S(2)}) %collective-permute-start.1) | collective-permute-done | bytes 2592 | tf_op jit(solution)/shard_map/ppermute | solution.py:141
  86.8 0.0 collective-permute-done
  86.8 0.2 convert_reduce_fusion
  86.9 0.2 fusion.14
  87.2 0.0 copy-done.5
  87.2 0.1 fusion.16
  87.3 27.3 %collective-permute-start.5 = (bf16[24,3200]{1,0:T(8,128)(2,1)S(1)}, bf16[24,3200]{1,0:T(8,128)(2,1)S(1)}, u32[]{:S(2)}, u32[]{:S(2)}) collective-permute-start(bf16[24,3200]{1,0:T(8,128)(2,1)S(1)} %fusion.16), channel_id=1, source_target_pairs={{0,46},{1,47},{2,0},{3,1},{4,2},{5,3},{6,4},{7,5},{8,6},{9,7},{10,... | collective-permute-start | bytes 460808 | tf_op jit(solution)/shard_map/ppermute | solution.py:141
  114.7 1.9 collective-permute-start.2
  116.6 0.8 collective-permute-done.5
  117.4 6.5 %collective-permute-done.2 = bf16[24,3200]{1,0:T(8,128)(2,1)S(1)} collective-permute-done((bf16[24,3200]{1,0:T(8,128)(2,1)S(1)}, bf16[24,3200]{1,0:T(8,128)(2,1)S(1)}, u32[]{:S(2)}, u32[]{:S(2)}) %collective-permute-start.2) | collective-permute-done | bytes 153632 | tf_op jit(solution)/shard_map/ppermute | solution.py:141
  123.9 1.9 collective-permute-start.3
  125.9 3.9 %collective-permute-start.6 = (bf16[48,3200]{1,0:T(8,128)(2,1)S(1)}, bf16[48,3200]{1,0:T(8,128)(2,1)S(1)}, u32[]{:S(2)}, u32[]{:S(2)}) collective-permute-start(bf16[48,3200]{1,0:T(8,128)(2,1)S(1)} %get-tuple-element.29), channel_id=1, source_target_pairs={{0,47},{1,0},{2,1},{3,2},{4,3},{5,4},{6,5},{7,6},{8,7},{9,8},{10,9... | collective-permute-start | bytes 921608 | tf_op jit(solution)/shard_map/ppermute | solution.py:141
  129.8 1.9 collective-permute-start.4
  131.7 4.2 %collective-permute-done.3 = bf16[48,3200]{1,0:T(8,128)(2,1)S(1)} collective-permute-done((bf16[48,3200]{1,0:T(8,128)(2,1)S(1)}, bf16[48,3200]{1,0:T(8,128)(2,1)S(1)}, u32[]{:S(2)}, u32[]{:S(2)}) %collective-permute-start.3) | collective-permute-done | bytes 307232 | tf_op jit(solution)/shard_map/ppermute | solution.py:141
  136.0 0.8 constant_dynamic-update-slice_fusion.5
  136.7 0.7 constant_dynamic-update-slice_fusion.4
  137.4 4.1 %collective-permute-done.4 = bf16[24,3200]{1,0:T(8,128)(2,1)S(1)} collective-permute-done((bf16[24,3200]{1,0:T(8,128)(2,1)S(1)}, bf16[24,3200]{1,0:T(8,128)(2,1)S(1)}, u32[]{:S(2)}, u32[]{:S(2)}) %collective-permute-start.4) | collective-permute-done | bytes 153632 | tf_op jit(solution)/shard_map/ppermute | solution.py:141
  141.5 0.7 constant_dynamic-update-slice_fusion.3
  142.2 0.0 collective-permute-done.6
  142.2 0.8 constant_dynamic-update-slice_fusion.2
  143.0 0.7 constant_dynamic-update-slice_fusion.1
  143.7 0.8 constant_dynamic-update-slice_fusion.rows_ref
  144.4 7.3 %fusion.11.part_ref = f32[192,3200]{1,0:T(8,128)S(1)} fusion(bf16[640,3200]{1,0:T(8,128)(2,1)} %param.15, bf16[192,3200]{1,0:T(8,128)(2,1)} %constant_dynamic-update-slice_fusion.rows_ref, bf16[3200,640]{1,0:T(8,128)(2,1)} %param.13, f32[640]{0:T(1024)S(1)} %copy-done.8), kind=kOutput, calls=%fused_computation.24 | convolution fusion | flops 1580974080 | bytes 11880960 | tf_op jit(solution)/shard_map/dot_general | solution.py:183
  151.8 1.0 all-gather.2.cloned.1.call-done.fetched_ref
  152.8 3.3 %copy-done = bf16[1280,3200]{1,0:T(8,128)(2,1)S(1)} copy-done((bf16[1280,3200]{1,0:T(8,128)(2,1)S(1)}, bf16[1280,3200]{1,0:T(8,128)(2,1)}, u32[]{:S(2)}) %copy-start) | copy-done | bytes 8192024
  156.1 5.7 %shard_map.92 = bf16[192,3200]{1,0:T(8,128)(2,1)S(1)} custom-call(bf16[192,3200]{1,0:T(8,128)(2,1)} %constant_dynamic-update-slice_fusion.rows_ref, f32[192,3200]{1,0:T(8,128)S(1)} %fusion.11.part_ref, f32[1,640]{1,0:T(1,128)S(1)} %broadcast_in_dim.7.bias_ref, bf16[1280,3200]{1,0:T(8,128)(2,1)S(1)} %copy-done), custom_call_target="tpu_custom_call" | custom-call | tf_op jit(solution)/shard_map/pallas_call | solution.py:110
  161.8 0.0 copy-start.6
  161.9 0.0 copy-start.7
  161.9 2.4 %collective-permute-start.8 = (bf16[48,3200]{1,0:T(8,128)(2,1)S(1)}, bf16[48,3200]{1,0:T(8,128)(2,1)S(1)}, u32[]{:S(2)}, u32[]{:S(2)}) collective-permute-start(bf16[48,3200]{1,0:T(8,128)(2,1)S(1)} %get-tuple-element.27), channel_id=1, source_target_pairs={{0,47},{1,0},{2,1},{3,2},{4,3},{5,4},{6,5},{7,6},{8,7},{9,8},{10,9... | collective-permute-start | bytes 921608 | tf_op jit(solution)/shard_map/ppermute | solution.py:141
  164.3 3.5 %collective-permute-start.11 = (bf16[48,3200]{1,0:T(8,128)(2,1)S(1)}, bf16[48,3200]{1,0:T(8,128)(2,1)S(1)}, u32[]{:S(2)}, u32[]{:S(2)}) collective-permute-start(bf16[48,3200]{1,0:T(8,128)(2,1)S(1)} %get-tuple-element.28), channel_id=1, source_target_pairs={{0,1},{1,2},{2,3},{3,4},{4,5},{5,6},{6,7},{7,8},{8,9},{9,10},{10,1... | collective-permute-start | bytes 921608 | tf_op jit(solution)/shard_map/ppermute | solution.py:141
  167.8 8.5 %collective-permute-start.9 = (bf16[24,3200]{1,0:T(8,128)(2,1)S(1)}, bf16[24,3200]{1,0:T(8,128)(2,1)S(1)}, u32[]{:S(2)}, u32[]{:S(2)}) collective-permute-start(bf16[24,3200]{1,0:T(8,128)(2,1)S(1)} %slice.43), channel_id=1, source_target_pairs={{0,46},{1,47},{2,0},{3,1},{4,2},{5,3},{6,4},{7,5},{8,6},{9,7},{10,... | collective-permute-start | bytes 460808 | tf_op jit(solution)/shard_map/ppermute | solution.py:141
  176.3 5.7 %collective-permute-done.9 = bf16[24,3200]{1,0:T(8,128)(2,1)S(1)} collective-permute-done((bf16[24,3200]{1,0:T(8,128)(2,1)S(1)}, bf16[24,3200]{1,0:T(8,128)(2,1)S(1)}, u32[]{:S(2)}, u32[]{:S(2)}) %collective-permute-start.9) | collective-permute-done | bytes 153632 | tf_op jit(solution)/shard_map/ppermute | solution.py:141
  182.1 0.0 collective-permute-done.8
  182.1 0.0 collective-permute-done.11
  182.1 0.1 add_convert_fusion.1
  182.2 6.5 %collective-permute-start.10 = (bf16[24,3200]{1,0:T(8,128)(2,1)S(1)}, bf16[24,3200]{1,0:T(8,128)(2,1)S(1)}, u32[]{:S(2)}, u32[]{:S(2)}) collective-permute-start(bf16[24,3200]{1,0:T(8,128)(2,1)S(1)} %get-tuple-element.25), channel_id=1, source_target_pairs={{0,46},{1,47},{2,0},{3,1},{4,2},{5,3},{6,4},{7,5},{8,6},{9,7},{10,... | collective-permute-start | bytes 460808 | tf_op jit(solution)/shard_map/ppermute | solution.py:141
  188.7 1.9 collective-permute-start.12
  190.6 3.1 %collective-permute-done.10 = bf16[24,3200]{1,0:T(8,128)(2,1)S(1)} collective-permute-done((bf16[24,3200]{1,0:T(8,128)(2,1)S(1)}, bf16[24,3200]{1,0:T(8,128)(2,1)S(1)}, u32[]{:S(2)}, u32[]{:S(2)}) %collective-permute-start.10) | collective-permute-done | bytes 153632 | tf_op jit(solution)/shard_map/ppermute | solution.py:141
  193.7 5.7 %collective-permute-done.12 = bf16[24,3200]{1,0:T(8,128)(2,1)S(1)} collective-permute-done((bf16[24,3200]{1,0:T(8,128)(2,1)S(1)}, bf16[24,3200]{1,0:T(8,128)(2,1)S(1)}, u32[]{:S(2)}, u32[]{:S(2)}) %collective-permute-start.12) | collective-permute-done | bytes 153632 | tf_op jit(solution)/shard_map/ppermute | solution.py:141
  199.4 0.0 copy-done.6
  199.4 0.0 copy-done.7
  199.4 0.8 fusion.49
  (11 shorter events, 0.1 us)
Async XLA Ops:
  6.5 1.0 copy-start.1
  7.5 0.7 copy-start.2
  8.2 0.7 copy-start.3
  13.6 58.4 %copy-start.8 = (f32[640]{0:T(1024)S(1)}, f32[640]{0:T(1024)}, u32[]{:S(2)}) copy-start(f32[640]{0:T(1024)} %param.14) | copy-start | bytes 7684
  13.6 23.3 %all-to-all-start = ((bf16[32,2,3200]{2,1,0:T(2,128)(2,1)}), bf16[32,2,3200]{2,1,0:T(2,128)(2,1)S(1)}, u32[]{:S(2)}, u32[]{:S(2)}) async-start(bf16[32,2,3200]{2,1,0:T(2,128)(2,1)} %all_to_all.8), calls=%async_computation | async-start | bytes 819200 | tf_op jit(solution)/shard_map/all_to_all | solution.py:158
  21.0 66.2 %copy-start.5 = (f32[3200]{0:T(1024)S(1)}, f32[3200]{0:T(1024)}, u32[]{:S(2)}) copy-start(f32[3200]{0:T(1024)} %param.12) | copy-start | bytes 38404
  21.0 131.8 %all-gather.2.cloned.1.call-start = ((), (), s32[]{:S(2)}) async-start(), calls=%async_computation.1 | async-start | bytes 8448000 | tf_op jit(solution)/shard_map/all_gather | solution.py:162
  21.1 29.8 %collective-permute-start.7 = (bf16[40,3200]{1,0:T(8,128)(2,1)S(1)}, bf16[40,3200]{1,0:T(8,128)(2,1)S(1)}, u32[]{:S(2)}, u32[]{:S(2)}) collective-permute-start(bf16[40,3200]{1,0:T(8,128)(2,1)S(1)} %fusion), channel_id=1, source_target_pairs={{0,8},{1,9},{2,10},{3,11},{4,12},{5,13},{6,14},{7,15},{8,32},{9,33... | collective-permute-start | bytes 768008 | tf_op jit(solution)/shard_map/ppermute | solution.py:157
  50.9 0.7 copy-start.4
  51.8 35.0 %collective-permute-start = (bf16[24,3200]{1,0:T(8,128)(2,1)S(1)}, bf16[24,3200]{1,0:T(8,128)(2,1)S(1)}, u32[]{:S(2)}, u32[]{:S(2)}) collective-permute-start(bf16[24,3200]{1,0:T(8,128)(2,1)S(1)} %convolution_convert_fusion.1), channel_id=1, source_target_pairs={{0,32},{1,33},{2,34},{3,35},{4,36},{5,37},{6,38},{7,39},{8,40},{9,... | collective-permute-start | bytes 460808 | tf_op jit(solution)/shard_map/ppermute | solution.py:141
  71.9 14.8 %collective-permute-start.1 = (f32[640]{0:T(1024)S(1)}, f32[640]{0:T(1024)S(1)}, u32[]{:S(2)}, u32[]{:S(2)}) collective-permute-start(f32[640]{0:T(1024)S(1)} %copy-done.8), channel_id=1, source_target_pairs={{0,8},{1,9},{2,10},{3,11},{4,12},{5,13},{6,14},{7,15},{8,32},{9,33... | collective-permute-start | bytes 7688 | tf_op jit(solution)/shard_map/ppermute | solution.py:141
  87.3 30.1 %collective-permute-start.5 = (bf16[24,3200]{1,0:T(8,128)(2,1)S(1)}, bf16[24,3200]{1,0:T(8,128)(2,1)S(1)}, u32[]{:S(2)}, u32[]{:S(2)}) collective-permute-start(bf16[24,3200]{1,0:T(8,128)(2,1)S(1)} %fusion.16), channel_id=1, source_target_pairs={{0,46},{1,47},{2,0},{3,1},{4,2},{5,3},{6,4},{7,5},{8,6},{9,7},{10,... | collective-permute-start | bytes 460808 | tf_op jit(solution)/shard_map/ppermute | solution.py:141
  114.7 9.2 %collective-permute-start.2 = (bf16[24,3200]{1,0:T(8,128)(2,1)S(1)}, bf16[24,3200]{1,0:T(8,128)(2,1)S(1)}, u32[]{:S(2)}, u32[]{:S(2)}) collective-permute-start(bf16[24,3200]{1,0:T(8,128)(2,1)S(1)} %fusion.16), channel_id=1, source_target_pairs={{0,2},{1,3},{2,4},{3,5},{4,6},{5,7},{6,8},{7,9},{8,10},{9,11},{10,... | collective-permute-start | bytes 460808 | tf_op jit(solution)/shard_map/ppermute | solution.py:141
  123.9 12.0 %collective-permute-start.3 = (bf16[48,3200]{1,0:T(8,128)(2,1)S(1)}, bf16[48,3200]{1,0:T(8,128)(2,1)S(1)}, u32[]{:S(2)}, u32[]{:S(2)}) collective-permute-start(bf16[48,3200]{1,0:T(8,128)(2,1)S(1)} %get-tuple-element.30), channel_id=1, source_target_pairs={{0,1},{1,2},{2,3},{3,4},{4,5},{5,6},{6,7},{7,8},{8,9},{9,10},{10,1... | collective-permute-start | bytes 921608 | tf_op jit(solution)/shard_map/ppermute | solution.py:141
  125.9 16.3 %collective-permute-start.6 = (bf16[48,3200]{1,0:T(8,128)(2,1)S(1)}, bf16[48,3200]{1,0:T(8,128)(2,1)S(1)}, u32[]{:S(2)}, u32[]{:S(2)}) collective-permute-start(bf16[48,3200]{1,0:T(8,128)(2,1)S(1)} %get-tuple-element.29), channel_id=1, source_target_pairs={{0,47},{1,0},{2,1},{3,2},{4,3},{5,4},{6,5},{7,6},{8,7},{9,8},{10,9... | collective-permute-start | bytes 921608 | tf_op jit(solution)/shard_map/ppermute | solution.py:141
  129.8 11.7 %collective-permute-start.4 = (bf16[24,3200]{1,0:T(8,128)(2,1)S(1)}, bf16[24,3200]{1,0:T(8,128)(2,1)S(1)}, u32[]{:S(2)}, u32[]{:S(2)}) collective-permute-start(bf16[24,3200]{1,0:T(8,128)(2,1)S(1)} %collective-permute-done.2), channel_id=1, source_target_pairs={{0,2},{1,3},{2,4},{3,5},{4,6},{5,7},{6,8},{7,9},{8,10},{9,11},{10,... | collective-permute-start | bytes 460808 | tf_op jit(solution)/shard_map/ppermute | solution.py:141
  152.8 3.3 %copy-start = (bf16[1280,3200]{1,0:T(8,128)(2,1)S(1)}, bf16[1280,3200]{1,0:T(8,128)(2,1)}, u32[]{:S(2)}) copy-start(bf16[1280,3200]{1,0:T(8,128)(2,1)} %all-gather.2.cloned.1.call-done.fetched_ref) | copy-start | bytes 24576004
  161.8 37.6 %copy-start.6 = (f32[3200]{0:T(1024)S(1)}, f32[3200]{0:T(1024)}, u32[]{:S(2)}) copy-start(f32[3200]{0:T(1024)} %param.16) | copy-start | bytes 38404
  161.9 37.5 %copy-start.7 = (f32[3200]{0:T(1024)S(1)}, f32[3200]{0:T(1024)}, u32[]{:S(2)}) copy-start(f32[3200]{0:T(1024)} %param.17) | copy-start | bytes 38404
  161.9 20.1 %collective-permute-start.8 = (bf16[48,3200]{1,0:T(8,128)(2,1)S(1)}, bf16[48,3200]{1,0:T(8,128)(2,1)S(1)}, u32[]{:S(2)}, u32[]{:S(2)}) collective-permute-start(bf16[48,3200]{1,0:T(8,128)(2,1)S(1)} %get-tuple-element.27), channel_id=1, source_target_pairs={{0,47},{1,0},{2,1},{3,2},{4,3},{5,4},{6,5},{7,6},{8,7},{9,8},{10,9... | collective-permute-start | bytes 921608 | tf_op jit(solution)/shard_map/ppermute | solution.py:141
  164.3 17.8 %collective-permute-start.11 = (bf16[48,3200]{1,0:T(8,128)(2,1)S(1)}, bf16[48,3200]{1,0:T(8,128)(2,1)S(1)}, u32[]{:S(2)}, u32[]{:S(2)}) collective-permute-start(bf16[48,3200]{1,0:T(8,128)(2,1)S(1)} %get-tuple-element.28), channel_id=1, source_target_pairs={{0,1},{1,2},{2,3},{3,4},{4,5},{5,6},{6,7},{7,8},{8,9},{9,10},{10,1... | collective-permute-start | bytes 921608 | tf_op jit(solution)/shard_map/ppermute | solution.py:141
  167.8 14.3 %collective-permute-start.9 = (bf16[24,3200]{1,0:T(8,128)(2,1)S(1)}, bf16[24,3200]{1,0:T(8,128)(2,1)S(1)}, u32[]{:S(2)}, u32[]{:S(2)}) collective-permute-start(bf16[24,3200]{1,0:T(8,128)(2,1)S(1)} %slice.43), channel_id=1, source_target_pairs={{0,46},{1,47},{2,0},{3,1},{4,2},{5,3},{6,4},{7,5},{8,6},{9,7},{10,... | collective-permute-start | bytes 460808 | tf_op jit(solution)/shard_map/ppermute | solution.py:141
  182.2 11.5 %collective-permute-start.10 = (bf16[24,3200]{1,0:T(8,128)(2,1)S(1)}, bf16[24,3200]{1,0:T(8,128)(2,1)S(1)}, u32[]{:S(2)}, u32[]{:S(2)}) collective-permute-start(bf16[24,3200]{1,0:T(8,128)(2,1)S(1)} %get-tuple-element.25), channel_id=1, source_target_pairs={{0,46},{1,47},{2,0},{3,1},{4,2},{5,3},{6,4},{7,5},{8,6},{9,7},{10,... | collective-permute-start | bytes 460808 | tf_op jit(solution)/shard_map/ppermute | solution.py:141
  188.7 10.7 %collective-permute-start.12 = (bf16[24,3200]{1,0:T(8,128)(2,1)S(1)}, bf16[24,3200]{1,0:T(8,128)(2,1)S(1)}, u32[]{:S(2)}, u32[]{:S(2)}) collective-permute-start(bf16[24,3200]{1,0:T(8,128)(2,1)S(1)} %get-tuple-element.26), channel_id=1, source_target_pairs={{0,2},{1,3},{2,4},{3,5},{4,6},{5,7},{6,8},{7,9},{8,10},{9,11},{10,... | collective-permute-start | bytes 460808 | tf_op jit(solution)/shard_map/ppermute | solution.py:141
Sparse Core Ops, SparseCore 0:
  51.7 101.0 all-gather.1

commit v5 on v4

--- a/solution.py
+++ b/solution.py
@@ -118,7 +118,7 @@
             pltpu.VMEM((count, units), jnp.bfloat16),
             pltpu.SemaphoreType.DMA((2,)),
         ],
-        compiler_params=pltpu.CompilerParams(vmem_limit_bytes=28 * 1024 * 1024),
+        compiler_params=pltpu.CompilerParams(vmem_limit_bytes=53 * 1024 * 1024),
     )(rows, part, bias[None], fetched)
 
 
@@ -153,7 +153,8 @@
     piece2 = lax.dynamic_slice_in_dim(fc2_weight, first, depth, axis=0)
     piece = jnp.where(upper, piece1, piece2)
     rows, pick_far, pick_near = plan(patches[0], live, rounds, mine, keep)
-    piece, rows = lax.optimization_barrier((piece, rows))
+    away_bias = send(fc1_bias, dps // 2)
+    away_bias, rows = lax.optimization_barrier((away_bias, rows))
     piece = lax.ppermute(piece, AXES, opposite_pairs(sections, dps, dps // 2))
     rows = lax.all_to_all(
         rows, "section", split_axis=0, concat_axis=0, axis_index_groups=groups, tiled=True
@@ -161,10 +162,7 @@
     piece = lax.optimization_barrier((piece, rows))[0]
     fetched = lax.all_gather(piece, "section", axis=0, axis_index_groups=groups, tiled=True)
     crossing = pick(pick_far, rows)
-    bias = lax.optimization_barrier((fc1_bias, crossing))[0]
-    away_bias = send(bias, dps // 2)
-    crossed, away_bias = lax.optimization_barrier((send(crossing, dps), away_bias))
-    routed = pick(pick_near, rows) + crossed
+    routed = pick(pick_near, rows) + send(crossing, dps)
 
     rows32 = routed.astype(f32)
     mean = jnp.mean(rows32, axis=1, keepdims=True)

time: 208 us -> 221 us (1.062)
  starting transfers between devices: 115 us -> 125 us
  local copies, waits for them, and re-layouts: 11.1 us -> 5.44 us
  waiting for transfers between devices: 47.9 us -> 52.2 us
  Pallas kernels: 6.05 us -> 9.07 us
    ppermute x12, starting transfers between devices: 91.7 us -> 109 us  [send(): return lax.ppermute(value, AXES, shift_pairs(sections, dps, hops))]
    ppermute x12, waiting for transfers between devices: 33 us -> 41.5 us  [send(): return lax.ppermute(value, AXES, shift_pairs(sections, dps, hops))]
    unnamed x23 -> x25, local copies, waits for them, and re-layouts: 9.93 us -> 3.16 us
    ppermute x1, starting transfers between devices: 15.7 us -> 9.38 us  [per_device(): piece = lax.ppermute(piece, AXES, opposite_pairs(sections, dps, dps // 2))]
    ppermute x1, waiting for transfers between devices: 13.9 us -> 10.8 us  [per_device(): piece = lax.ppermute(piece, AXES, opposite_pairs(sections, dps, dps // 2))]
    pallas_call x1, Pallas kernels: 5.71 us -> 8.73 us  [add_away(): pl.pallas_call(away_kernel, out_shape=jax.ShapeDtypeStruct((count, width)...]
where the time goes in v5:
time: 221 us; the launch traced here: 220 us
  starting transfers between devices  125 us (57%)
  waiting for transfers between devices  52.2 us (24%)
  between operations  13.7 us (6%)
  matrix products  12.6 us (6%)
  Pallas kernels  9.07 us (4%)
  local copies, waits for them, and re-layouts  5.44 us (2%)
    ppermute x12, starting transfers between devices, send(): return lax.ppermute(value, AXES, shift_pairs(sections, dps, hops))  109 us
    ppermute x12, waiting for transfers between devices, send(): return lax.ppermute(value, AXES, shift_pairs(sections, dps, hops))  41.5 us
    ppermute x1, waiting for transfers between devices, per_device(): piece = lax.ppermute(piece, AXES, opposite_pairs(sections, dps, dps // 2))  10.8 us
    ppermute x1, starting transfers between devices, per_device(): piece = lax.ppermute(piece, AXES, opposite_pairs(sections, dps, dps // 2))  9.38 us
    pallas_call x1, Pallas kernels, add_away(): pl.pallas_call(away_kernel, out_shape=jax.ShapeDtypeStruct((count, width)...  8.73 us
    dot_general x1, matrix products, per_device(): part = jnp.dot(hidden, fc2_weight, preferred_element_type=f32)  8.73 us
    all_to_all x1, starting transfers between devices, per_device(): lax.all_to_all(rows, 'section', split_axis=0, concat_axis=0, axis_index_g...  7.32 us
  transfers between devices with their start and end apart: 15, of which 10 were waited for; matrix products, arithmetic and copies ran while one was open for 6% of the time, Pallas kernels for 0%

profile of v5, /device:TPU:32, one launch (start us, length us, event | category | flops | bytes accessed | tf_op | source)
XLA Modules:
  0.0 219.8 jit_solution(18392186864846811096)
XLA Ops:
  6.5 15.7 %collective-permute-start = (f32[640]{0:T(1024)}, f32[640]{0:T(1024)S(1)}, u32[]{:S(2)}, u32[]{:S(2)}) collective-permute-start(f32[640]{0:T(1024)} %param.14), channel_id=1, source_target_pairs={{0,8},{1,9},{2,10},{3,11},{4,12},{5,13},{6,14},{7,15},{8,32},{9,33... | collective-permute-start | bytes 7688 | tf_op jit(solution)/shard_map/ppermute | solution.py:141
  22.3 0.0 copy-start
  22.3 1.0 copy-done
  23.3 0.0 copy-start.1
  23.3 0.7 copy-done.1
  23.9 0.0 copy-start.2
  23.9 0.7 copy-done.2
  24.6 0.3 shard_map.91
  24.9 5.5 %collective-permute-done = f32[640]{0:T(1024)S(1)} collective-permute-done((f32[640]{0:T(1024)}, f32[640]{0:T(1024)S(1)}, u32[]{:S(2)}, u32[]{:S(2)}) %collective-permute-start) | collective-permute-done | bytes 2592 | tf_op jit(solution)/shard_map/ppermute | solution.py:141
  30.4 0.9 all_to_all.8
  31.3 7.3 %all-to-all-start = ((bf16[32,2,3200]{2,1,0:T(2,128)(2,1)}), bf16[32,2,3200]{2,1,0:T(2,128)(2,1)S(1)}, u32[]{:S(2)}, u32[]{:S(2)}) async-start(bf16[32,2,3200]{2,1,0:T(2,128)(2,1)} %all_to_all.8), calls=%async_computation | async-start | bytes 819200 | tf_op jit(solution)/shard_map/all_to_all | solution.py:159
  38.7 0.0 all-gather.2.cloned.1.call-start
  38.7 3.4 %fusion = bf16[40,3200]{1,0:T(8,128)(2,1)S(1)} fusion(bf16[3200,640]{1,0:T(8,128)(2,1)} %param.13, bf16[640,3200]{1,0:T(8,128)(2,1)} %param.15, s32[]{:T(128)S(6)} %select_n.12, pred[]{:T(512)S(6)} %lt.6, s32[40]{0:T(128)S(1)} %iota_add_fusion), kind=kOutput, calls=%fused_computation.1 | convolution fusion | flops 164121600 | bytes 4608165 | tf_op jit(solution)/shard_map/dot_general | solution.py:150
  42.2 0.0 copy-start.6
  42.2 9.4 %collective-permute-start.7 = (bf16[40,3200]{1,0:T(8,128)(2,1)S(1)}, bf16[40,3200]{1,0:T(8,128)(2,1)S(1)}, u32[]{:S(2)}, u32[]{:S(2)}) collective-permute-start(bf16[40,3200]{1,0:T(8,128)(2,1)S(1)} %fusion), channel_id=1, source_target_pairs={{0,8},{1,9},{2,10},{3,11},{4,12},{5,13},{6,14},{7,15},{8,32},{9,33... | collective-permute-start | bytes 768008 | tf_op jit(solution)/shard_map/ppermute | solution.py:158
  51.6 0.0 all-to-all-done
  51.6 0.2 all_to_all.10
  51.7 10.8 %collective-permute-done.7 = bf16[40,3200]{1,0:T(8,128)(2,1)S(1)} collective-permute-done((bf16[40,3200]{1,0:T(8,128)(2,1)S(1)}, bf16[40,3200]{1,0:T(8,128)(2,1)S(1)}, u32[]{:S(2)}, u32[]{:S(2)}) %collective-permute-start.7) | collective-permute-done | bytes 256032 | tf_op jit(solution)/shard_map/ppermute | solution.py:158
  62.5 0.0 copy-start.5
  62.5 0.7 copy-done.5
  63.2 0.0 all-gather.2.cloned.1.call-update
  63.2 0.2 convolution_convert_fusion.1
  63.4 22.1 %collective-permute-start.1 = (bf16[24,3200]{1,0:T(8,128)(2,1)S(1)}, bf16[24,3200]{1,0:T(8,128)(2,1)S(1)}, u32[]{:S(2)}, u32[]{:S(2)}) collective-permute-start(bf16[24,3200]{1,0:T(8,128)(2,1)S(1)} %convolution_convert_fusion.1), channel_id=1, source_target_pairs={{0,32},{1,33},{2,34},{3,35},{4,36},{5,37},{6,38},{7,39},{8,40},{9,... | collective-permute-start | bytes 460808 | tf_op jit(solution)/shard_map/ppermute | solution.py:141
  85.5 3.5 %collective-permute-done.1 = bf16[24,3200]{1,0:T(8,128)(2,1)S(1)} collective-permute-done((bf16[24,3200]{1,0:T(8,128)(2,1)S(1)}, bf16[24,3200]{1,0:T(8,128)(2,1)S(1)}, u32[]{:S(2)}, u32[]{:S(2)}) %collective-permute-start.1) | collective-permute-done | bytes 153632 | tf_op jit(solution)/shard_map/ppermute | solution.py:141
  88.9 0.3 fusion.78
  89.2 0.2 multiply_reduce_fusion
  89.5 0.0 copy-done.6
  89.5 0.1 multiply_convert_fusion
  89.6 35.6 %collective-permute-start.5 = (bf16[24,3200]{1,0:T(8,128)(2,1)S(1)}, bf16[24,3200]{1,0:T(8,128)(2,1)S(1)}, u32[]{:S(2)}, u32[]{:S(2)}) collective-permute-start(bf16[24,3200]{1,0:T(8,128)(2,1)S(1)} %multiply_convert_fusion), channel_id=1, source_target_pairs={{0,46},{1,47},{2,0},{3,1},{4,2},{5,3},{6,4},{7,5},{8,6},{9,7},{10,... | collective-permute-start | bytes 460808 | tf_op jit(solution)/shard_map/ppermute | solution.py:141
  125.2 1.9 collective-permute-start.2
  127.1 0.8 collective-permute-done.5
  127.9 6.6 %collective-permute-done.2 = bf16[24,3200]{1,0:T(8,128)(2,1)S(1)} collective-permute-done((bf16[24,3200]{1,0:T(8,128)(2,1)S(1)}, bf16[24,3200]{1,0:T(8,128)(2,1)S(1)}, u32[]{:S(2)}, u32[]{:S(2)}) %collective-permute-start.2) | collective-permute-done | bytes 153632 | tf_op jit(solution)/shard_map/ppermute | solution.py:141
  134.5 6.4 %collective-permute-start.3 = (bf16[48,3200]{1,0:T(8,128)(2,1)S(1)}, bf16[48,3200]{1,0:T(8,128)(2,1)S(1)}, u32[]{:S(2)}, u32[]{:S(2)}) collective-permute-start(bf16[48,3200]{1,0:T(8,128)(2,1)S(1)} %get-tuple-element.22), channel_id=1, source_target_pairs={{0,1},{1,2},{2,3},{3,4},{4,5},{5,6},{6,7},{7,8},{8,9},{9,10},{10,1... | collective-permute-start | bytes 921608 | tf_op jit(solution)/shard_map/ppermute | solution.py:141
  140.9 0.0 copy-start.9
  140.9 4.7 %collective-permute-start.6 = (bf16[48,3200]{1,0:T(8,128)(2,1)S(1)}, bf16[48,3200]{1,0:T(8,128)(2,1)S(1)}, u32[]{:S(2)}, u32[]{:S(2)}) collective-permute-start(bf16[48,3200]{1,0:T(8,128)(2,1)S(1)} %get-tuple-element.21), channel_id=1, source_target_pairs={{0,47},{1,0},{2,1},{3,2},{4,3},{5,4},{6,5},{7,6},{8,7},{9,8},{10,9... | collective-permute-start | bytes 921608 | tf_op jit(solution)/shard_map/ppermute | solution.py:141
  145.6 1.9 collective-permute-start.4
  147.5 2.7 %collective-permute-done.3 = bf16[48,3200]{1,0:T(8,128)(2,1)S(1)} collective-permute-done((bf16[48,3200]{1,0:T(8,128)(2,1)S(1)}, bf16[48,3200]{1,0:T(8,128)(2,1)S(1)}, u32[]{:S(2)}, u32[]{:S(2)}) %collective-permute-start.3) | collective-permute-done | bytes 307232 | tf_op jit(solution)/shard_map/ppermute | solution.py:141
  150.3 7.3 %collective-permute-done.4 = bf16[24,3200]{1,0:T(8,128)(2,1)S(1)} collective-permute-done((bf16[24,3200]{1,0:T(8,128)(2,1)S(1)}, bf16[24,3200]{1,0:T(8,128)(2,1)S(1)}, u32[]{:S(2)}, u32[]{:S(2)}) %collective-permute-start.4) | collective-permute-done | bytes 153632 | tf_op jit(solution)/shard_map/ppermute | solution.py:141
  157.6 0.0 collective-permute-done.6
  157.7 0.1 constant_dynamic-update-slice_fusion.rows_ref
  157.8 0.0 copy-done.9
  157.8 0.0 copy-start.4
  157.8 8.7 %fusion.13.part_ref = f32[192,3200]{1,0:T(8,128)} fusion(bf16[640,3200]{1,0:T(8,128)(2,1)} %param.15, bf16[192,3200]{1,0:T(8,128)(2,1)S(1)} %constant_dynamic-update-slice_fusion.rows_ref, bf16[3200,640]{1,0:T(8,128)(2,1)} %param.13, f32[640]{0:T(1024)S(1)} %copy-done.9), kind=kOutput, calls=%fused_computation.26 | convolution fusion | flops 1580974080 | bytes 11880960 | tf_op jit(solution)/shard_map/dot_general | solution.py:181
  166.6 0.0 copy-done.4
  166.6 8.7 %shard_map.92 = bf16[192,3200]{1,0:T(8,128)(2,1)} custom-call(bf16[192,3200]{1,0:T(8,128)(2,1)} %copy-done.4, f32[192,3200]{1,0:T(8,128)} %fusion.13.part_ref, f32[1,640]{1,0:T(1,128)S(1)} %broadcast_in_dim.7.bias_ref, bf16[1280,3200]{1,0:T(8,128)(2,1)} %all-gather.2.cloned.1.call-done.fetched_ref), custom_call_target="tpu_custom_call" | custom-call | tf_op jit(solution)/shard_map/pallas_call | solution.py:110
  175.3 0.0 copy-start.3
  175.3 0.0 copy-start.7
  175.3 0.0 copy-start.8
  175.3 1.2 fusion.77
  176.5 4.2 %collective-permute-start.8 = (bf16[48,3200]{1,0:T(8,128)(2,1)S(1)}, bf16[48,3200]{1,0:T(8,128)(2,1)S(1)}, u32[]{:S(2)}, u32[]{:S(2)}) collective-permute-start(bf16[48,3200]{1,0:T(8,128)(2,1)S(1)} %get-tuple-element.19), channel_id=1, source_target_pairs={{0,47},{1,0},{2,1},{3,2},{4,3},{5,4},{6,5},{7,6},{8,7},{9,8},{10,9... | collective-permute-start | bytes 921608 | tf_op jit(solution)/shard_map/ppermute | solution.py:141
  180.7 1.9 collective-permute-start.11
  182.7 0.0 copy-done.3
  182.7 5.8 %collective-permute-start.9 = (bf16[24,3200]{1,0:T(8,128)(2,1)S(1)}, bf16[24,3200]{1,0:T(8,128)(2,1)S(1)}, u32[]{:S(2)}, u32[]{:S(2)}) collective-permute-start(bf16[24,3200]{1,0:T(8,128)(2,1)S(1)} %slice.43), channel_id=1, source_target_pairs={{0,46},{1,47},{2,0},{3,1},{4,2},{5,3},{6,4},{7,5},{8,6},{9,7},{10,... | collective-permute-start | bytes 460808 | tf_op jit(solution)/shard_map/ppermute | solution.py:141
  188.5 5.7 %collective-permute-done.9 = bf16[24,3200]{1,0:T(8,128)(2,1)S(1)} collective-permute-done((bf16[24,3200]{1,0:T(8,128)(2,1)S(1)}, bf16[24,3200]{1,0:T(8,128)(2,1)S(1)}, u32[]{:S(2)}, u32[]{:S(2)}) %collective-permute-start.9) | collective-permute-done | bytes 153632 | tf_op jit(solution)/shard_map/ppermute | solution.py:141
  194.2 0.0 collective-permute-done.8
  194.2 0.0 collective-permute-done.11
  194.2 0.1 add_convert_fusion.2
  194.3 6.5 %collective-permute-start.10 = (bf16[24,3200]{1,0:T(8,128)(2,1)S(1)}, bf16[24,3200]{1,0:T(8,128)(2,1)S(1)}, u32[]{:S(2)}, u32[]{:S(2)}) collective-permute-start(bf16[24,3200]{1,0:T(8,128)(2,1)S(1)} %get-tuple-element.17), channel_id=1, source_target_pairs={{0,46},{1,47},{2,0},{3,1},{4,2},{5,3},{6,4},{7,5},{8,6},{9,7},{10,... | collective-permute-start | bytes 460808 | tf_op jit(solution)/shard_map/ppermute | solution.py:141
  200.8 1.9 collective-permute-start.12
  202.8 3.1 %collective-permute-done.10 = bf16[24,3200]{1,0:T(8,128)(2,1)S(1)} collective-permute-done((bf16[24,3200]{1,0:T(8,128)(2,1)S(1)}, bf16[24,3200]{1,0:T(8,128)(2,1)S(1)}, u32[]{:S(2)}, u32[]{:S(2)}) %collective-permute-start.10) | collective-permute-done | bytes 153632 | tf_op jit(solution)/shard_map/ppermute | solution.py:141
  205.9 6.3 %collective-permute-done.12 = bf16[24,3200]{1,0:T(8,128)(2,1)S(1)} collective-permute-done((bf16[24,3200]{1,0:T(8,128)(2,1)S(1)}, bf16[24,3200]{1,0:T(8,128)(2,1)S(1)}, u32[]{:S(2)}, u32[]{:S(2)}) %collective-permute-start.12) | collective-permute-done | bytes 153632 | tf_op jit(solution)/shard_map/ppermute | solution.py:141
  212.2 0.0 copy-done.7
  212.2 0.0 copy-done.8
  212.2 0.8 fusion.45
  (12 shorter events, 0.2 us)
Async XLA Ops:
  6.5 23.9 %collective-permute-start = (f32[640]{0:T(1024)}, f32[640]{0:T(1024)S(1)}, u32[]{:S(2)}, u32[]{:S(2)}) collective-permute-start(f32[640]{0:T(1024)} %param.14), channel_id=1, source_target_pairs={{0,8},{1,9},{2,10},{3,11},{4,12},{5,13},{6,14},{7,15},{8,32},{9,33... | collective-permute-start | bytes 7688 | tf_op jit(solution)/shard_map/ppermute | solution.py:141
  22.3 1.0 copy-start
  23.3 0.7 copy-start.1
  23.9 0.7 copy-start.2
  31.3 20.2 %all-to-all-start = ((bf16[32,2,3200]{2,1,0:T(2,128)(2,1)}), bf16[32,2,3200]{2,1,0:T(2,128)(2,1)S(1)}, u32[]{:S(2)}, u32[]{:S(2)}) async-start(bf16[32,2,3200]{2,1,0:T(2,128)(2,1)} %all_to_all.8), calls=%async_computation | async-start | bytes 819200 | tf_op jit(solution)/shard_map/all_to_all | solution.py:159
  38.7 127.9 %all-gather.2.cloned.1.call-start = ((), (), s32[]{:S(2)}) async-start(), calls=%async_computation.1 | async-start | bytes 8448000 | tf_op jit(solution)/shard_map/all_gather | solution.py:163
  42.2 47.3 %copy-start.6 = (f32[3200]{0:T(1024)S(1)}, f32[3200]{0:T(1024)}, u32[]{:S(2)}) copy-start(f32[3200]{0:T(1024)} %param.12) | copy-start | bytes 38404
  42.2 20.3 %collective-permute-start.7 = (bf16[40,3200]{1,0:T(8,128)(2,1)S(1)}, bf16[40,3200]{1,0:T(8,128)(2,1)S(1)}, u32[]{:S(2)}, u32[]{:S(2)}) collective-permute-start(bf16[40,3200]{1,0:T(8,128)(2,1)S(1)} %fusion), channel_id=1, source_target_pairs={{0,8},{1,9},{2,10},{3,11},{4,12},{5,13},{6,14},{7,15},{8,32},{9,33... | collective-permute-start | bytes 768008 | tf_op jit(solution)/shard_map/ppermute | solution.py:158
  62.5 0.7 copy-start.5
  63.4 25.5 %collective-permute-start.1 = (bf16[24,3200]{1,0:T(8,128)(2,1)S(1)}, bf16[24,3200]{1,0:T(8,128)(2,1)S(1)}, u32[]{:S(2)}, u32[]{:S(2)}) collective-permute-start(bf16[24,3200]{1,0:T(8,128)(2,1)S(1)} %convolution_convert_fusion.1), channel_id=1, source_target_pairs={{0,32},{1,33},{2,34},{3,35},{4,36},{5,37},{6,38},{7,39},{8,40},{9,... | collective-permute-start | bytes 460808 | tf_op jit(solution)/shard_map/ppermute | solution.py:141
  89.6 38.3 %collective-permute-start.5 = (bf16[24,3200]{1,0:T(8,128)(2,1)S(1)}, bf16[24,3200]{1,0:T(8,128)(2,1)S(1)}, u32[]{:S(2)}, u32[]{:S(2)}) collective-permute-start(bf16[24,3200]{1,0:T(8,128)(2,1)S(1)} %multiply_convert_fusion), channel_id=1, source_target_pairs={{0,46},{1,47},{2,0},{3,1},{4,2},{5,3},{6,4},{7,5},{8,6},{9,7},{10,... | collective-permute-start | bytes 460808 | tf_op jit(solution)/shard_map/ppermute | solution.py:141
  125.2 9.3 %collective-permute-start.2 = (bf16[24,3200]{1,0:T(8,128)(2,1)S(1)}, bf16[24,3200]{1,0:T(8,128)(2,1)S(1)}, u32[]{:S(2)}, u32[]{:S(2)}) collective-permute-start(bf16[24,3200]{1,0:T(8,128)(2,1)S(1)} %multiply_convert_fusion), channel_id=1, source_target_pairs={{0,2},{1,3},{2,4},{3,5},{4,6},{5,7},{6,8},{7,9},{8,10},{9,11},{10,... | collective-permute-start | bytes 460808 | tf_op jit(solution)/shard_map/ppermute | solution.py:141
  134.5 15.7 %collective-permute-start.3 = (bf16[48,3200]{1,0:T(8,128)(2,1)S(1)}, bf16[48,3200]{1,0:T(8,128)(2,1)S(1)}, u32[]{:S(2)}, u32[]{:S(2)}) collective-permute-start(bf16[48,3200]{1,0:T(8,128)(2,1)S(1)} %get-tuple-element.22), channel_id=1, source_target_pairs={{0,1},{1,2},{2,3},{3,4},{4,5},{5,6},{6,7},{7,8},{8,9},{9,10},{10,1... | collective-permute-start | bytes 921608 | tf_op jit(solution)/shard_map/ppermute | solution.py:141
  140.9 16.9 %copy-start.9 = (f32[640]{0:T(1024)S(1)}, f32[640]{0:T(1024)}, u32[]{:S(2)}) copy-start(f32[640]{0:T(1024)} %param.14) | copy-start | bytes 7684
  140.9 16.7 %collective-permute-start.6 = (bf16[48,3200]{1,0:T(8,128)(2,1)S(1)}, bf16[48,3200]{1,0:T(8,128)(2,1)S(1)}, u32[]{:S(2)}, u32[]{:S(2)}) collective-permute-start(bf16[48,3200]{1,0:T(8,128)(2,1)S(1)} %get-tuple-element.21), channel_id=1, source_target_pairs={{0,47},{1,0},{2,1},{3,2},{4,3},{5,4},{6,5},{7,6},{8,7},{9,8},{10,9... | collective-permute-start | bytes 921608 | tf_op jit(solution)/shard_map/ppermute | solution.py:141
  145.6 12.0 %collective-permute-start.4 = (bf16[24,3200]{1,0:T(8,128)(2,1)S(1)}, bf16[24,3200]{1,0:T(8,128)(2,1)S(1)}, u32[]{:S(2)}, u32[]{:S(2)}) collective-permute-start(bf16[24,3200]{1,0:T(8,128)(2,1)S(1)} %collective-permute-done.2), channel_id=1, source_target_pairs={{0,2},{1,3},{2,4},{3,5},{4,6},{5,7},{6,8},{7,9},{8,10},{9,11},{10,... | collective-permute-start | bytes 460808 | tf_op jit(solution)/shard_map/ppermute | solution.py:141
  157.8 8.7 %copy-start.4 = (bf16[192,3200]{1,0:T(8,128)(2,1)}, bf16[192,3200]{1,0:T(8,128)(2,1)S(1)}, u32[]{:S(2)}) copy-start(bf16[192,3200]{1,0:T(8,128)(2,1)S(1)} %constant_dynamic-update-slice_fusion.rows_ref) | copy-start | bytes 3686404
  175.3 7.4 %copy-start.3 = (bf16[192,3200]{1,0:T(8,128)(2,1)S(1)}, bf16[192,3200]{1,0:T(8,128)(2,1)}, u32[]{:S(2)}) copy-start(bf16[192,3200]{1,0:T(8,128)(2,1)} %shard_map.92) | copy-start | bytes 3686404
  175.3 36.8 %copy-start.7 = (f32[3200]{0:T(1024)S(1)}, f32[3200]{0:T(1024)}, u32[]{:S(2)}) copy-start(f32[3200]{0:T(1024)} %param.16) | copy-start | bytes 38404
  175.3 36.8 %copy-start.8 = (f32[3200]{0:T(1024)S(1)}, f32[3200]{0:T(1024)}, u32[]{:S(2)}) copy-start(f32[3200]{0:T(1024)} %param.17) | copy-start | bytes 38404
  176.5 17.7 %collective-permute-start.8 = (bf16[48,3200]{1,0:T(8,128)(2,1)S(1)}, bf16[48,3200]{1,0:T(8,128)(2,1)S(1)}, u32[]{:S(2)}, u32[]{:S(2)}) collective-permute-start(bf16[48,3200]{1,0:T(8,128)(2,1)S(1)} %get-tuple-element.19), channel_id=1, source_target_pairs={{0,47},{1,0},{2,1},{3,2},{4,3},{5,4},{6,5},{7,6},{8,7},{9,8},{10,9... | collective-permute-start | bytes 921608 | tf_op jit(solution)/shard_map/ppermute | solution.py:141
  180.7 13.5 %collective-permute-start.11 = (bf16[48,3200]{1,0:T(8,128)(2,1)S(1)}, bf16[48,3200]{1,0:T(8,128)(2,1)S(1)}, u32[]{:S(2)}, u32[]{:S(2)}) collective-permute-start(bf16[48,3200]{1,0:T(8,128)(2,1)S(1)} %get-tuple-element.20), channel_id=1, source_target_pairs={{0,1},{1,2},{2,3},{3,4},{4,5},{5,6},{6,7},{7,8},{8,9},{9,10},{10,1... | collective-permute-start | bytes 921608 | tf_op jit(solution)/shard_map/ppermute | solution.py:141
  182.7 11.5 %collective-permute-start.9 = (bf16[24,3200]{1,0:T(8,128)(2,1)S(1)}, bf16[24,3200]{1,0:T(8,128)(2,1)S(1)}, u32[]{:S(2)}, u32[]{:S(2)}) collective-permute-start(bf16[24,3200]{1,0:T(8,128)(2,1)S(1)} %slice.43), channel_id=1, source_target_pairs={{0,46},{1,47},{2,0},{3,1},{4,2},{5,3},{6,4},{7,5},{8,6},{9,7},{10,... | collective-permute-start | bytes 460808 | tf_op jit(solution)/shard_map/ppermute | solution.py:141
  194.3 11.6 %collective-permute-start.10 = (bf16[24,3200]{1,0:T(8,128)(2,1)S(1)}, bf16[24,3200]{1,0:T(8,128)(2,1)S(1)}, u32[]{:S(2)}, u32[]{:S(2)}) collective-permute-start(bf16[24,3200]{1,0:T(8,128)(2,1)S(1)} %get-tuple-element.17), channel_id=1, source_target_pairs={{0,46},{1,47},{2,0},{3,1},{4,2},{5,3},{6,4},{7,5},{8,6},{9,7},{10,... | collective-permute-start | bytes 460808 | tf_op jit(solution)/shard_map/ppermute | solution.py:141
  200.8 11.3 %collective-permute-start.12 = (bf16[24,3200]{1,0:T(8,128)(2,1)S(1)}, bf16[24,3200]{1,0:T(8,128)(2,1)S(1)}, u32[]{:S(2)}, u32[]{:S(2)}) collective-permute-start(bf16[24,3200]{1,0:T(8,128)(2,1)S(1)} %get-tuple-element.18), channel_id=1, source_target_pairs={{0,2},{1,3},{2,4},{3,5},{4,6},{5,7},{6,8},{7,9},{8,10},{9,11},{10,... | collective-permute-start | bytes 460808 | tf_op jit(solution)/shard_map/ppermute | solution.py:141
Sparse Core Ops, SparseCore 0:
  63.4 100.7 all-gather.1

commit v6 on v4

--- a/solution.py
+++ b/solution.py
@@ -83,23 +83,19 @@
     )(mine[None], live, order, patches)
 
 
-def away_kernel(rows_ref, part_ref, bias_ref, fetched_ref, out_ref, w1, w2, hidden, sems):
-    units, width = w1.shape
-    first = pltpu.make_async_copy(fetched_ref.at[pl.ds(0, units)], w1, sems.at[0])
-    second = pltpu.make_async_copy(fetched_ref.at[pl.ds(units, units)], w2, sems.at[1])
-    first.start()
-    second.start()
-    first.wait()
+def away_kernel(rows_ref, part_ref, bias_ref, fetched_ref, out_ref, hidden):
+    width = rows_ref.shape[1]
+    units = hidden.shape[1]
     for at in range(0, units, 256):
-        span = pl.ds(at, min(256, units - at))
+        size = min(256, units - at)
+        span = pl.ds(at, size)
         pre = lax.dot_general(
-            rows_ref[...], w1[span], (((1,), (1,)), ((), ())), preferred_element_type=jnp.float32
+            rows_ref[...], fetched_ref[span], (((1,), (1,)), ((), ())), preferred_element_type=jnp.float32
         ) + bias_ref[:, span]
         hidden[:, span] = (0.5 * pre * (1.0 + lax.erf(pre * np.float32(0.5**0.5)))).astype(jnp.bfloat16)
-    second.wait()
     for at in range(0, width, 640):
         span = pl.ds(at, min(640, width - at))
-        out = jnp.dot(hidden[...], w2[:, span], preferred_element_type=jnp.float32)
+        out = jnp.dot(hidden[...], fetched_ref[pl.ds(units, units), span], preferred_element_type=jnp.float32)
         out_ref[:, span] = (part_ref[:, span] + out).astype(jnp.bfloat16)
 
 
@@ -110,13 +106,10 @@
     return pl.pallas_call(
         away_kernel,
         out_shape=jax.ShapeDtypeStruct((count, width), jnp.bfloat16),
-        in_specs=[vmem, vmem, vmem, pl.BlockSpec(memory_space=pl.ANY)],
+        in_specs=[vmem, vmem, vmem, vmem],
         out_specs=vmem,
         scratch_shapes=[
-            pltpu.VMEM((units, width), jnp.bfloat16),
-            pltpu.VMEM((units, width), jnp.bfloat16),
             pltpu.VMEM((count, units), jnp.bfloat16),
-            pltpu.SemaphoreType.DMA((2,)),
         ],
         compiler_params=pltpu.CompilerParams(vmem_limit_bytes=28 * 1024 * 1024),
     )(rows, part, bias[None], fetched)
@@ -152,8 +145,8 @@
     ).astype(jnp.bfloat16)
     piece2 = lax.dynamic_slice_in_dim(fc2_weight, first, depth, axis=0)
     piece = jnp.where(upper, piece1, piece2)
+    piece, live = lax.optimization_barrier((piece, live))
     rows, pick_far, pick_near = plan(patches[0], live, rounds, mine, keep)
-    piece, rows = lax.optimization_barrier((piece, rows))
     piece = lax.ppermute(piece, AXES, opposite_pairs(sections, dps, dps // 2))
     rows = lax.all_to_all(
         rows, "section", split_axis=0, concat_axis=0, axis_index_groups=groups, tiled=True

time: 208 us -> 204 us (0.981)
  local copies, waits for them, and re-layouts: 11.1 us -> 8.76 us
    ppermute x12, waiting for transfers between devices: 33 us -> 30.6 us  [send(): return lax.ppermute(value, AXES, shift_pairs(sections, dps, hops))]
    unnamed x23, local copies, waits for them, and re-layouts: 9.93 us -> 7.63 us
    all_gather x1, waiting for transfers between devices: 1.04 us -> 3.33 us  [per_device(): lax.all_gather(piece, 'section', axis=0, axis_index_groups=groups, tiled=...]
where the time goes in v6:
time: 204 us
  starting transfers between devices  115 us (56%)
  waiting for transfers between devices  47.8 us (23%)
  between operations  13.7 us (7%)
  matrix products  11.2 us (5%)
  local copies, waits for them, and re-layouts  8.76 us (4%)
  Pallas kernels  4.9 us (2%)
  other arithmetic  2.25 us (1%)
    ppermute x12, starting transfers between devices, send(): return lax.ppermute(value, AXES, shift_pairs(sections, dps, hops))  91.8 us
    ppermute x12, waiting for transfers between devices, send(): return lax.ppermute(value, AXES, shift_pairs(sections, dps, hops))  30.6 us
    ppermute x1, starting transfers between devices, per_device(): piece = lax.ppermute(piece, AXES, opposite_pairs(sections, dps, dps // 2))  15.7 us
    ppermute x1, waiting for transfers between devices, per_device(): piece = lax.ppermute(piece, AXES, opposite_pairs(sections, dps, dps // 2))  13.9 us
    unnamed x23, local copies, waits for them, and re-layouts  7.63 us
    all_to_all x1, starting transfers between devices, per_device(): lax.all_to_all(rows, 'section', split_axis=0, concat_axis=0, axis_index_g...  7.46 us
    dot_general x1, matrix products, per_device(): part = jnp.dot(hidden, fc2_weight, preferred_element_type=f32)  7.37 us
    pallas_call x1, Pallas kernels, add_away(): pl.pallas_call(away_kernel, out_shape=jax.ShapeDtypeStruct((count, width)...  4.55 us
  transfers between devices with their start and end apart: 15, of which 10 were waited for; matrix products, arithmetic and copies ran while one was open for 6% of the time, Pallas kernels for 0%

profile of v6, /device:TPU:32, one launch (start us, length us, event | category | flops | bytes accessed | tf_op | source)
XLA Modules:
  0.0 203.7 jit_solution(16882683728562114377)
XLA Ops:
  6.5 0.0 copy-start.1
  6.5 0.0 copy-start.2
  6.5 3.5 %fusion = bf16[40,3200]{1,0:T(8,128)(2,1)S(1)} fusion(bf16[3200,640]{1,0:T(8,128)(2,1)} %param.13, bf16[640,3200]{1,0:T(8,128)(2,1)} %param.15, s32[]{:T(128)S(6)} %select_n.12, pred[]{:T(512)S(6)} %lt.6, s32[40]{0:T(128)S(1)} %iota_add_fusion), kind=kOutput, calls=%fused_computation.1 | convolution fusion | flops 164121600 | bytes 4608165 | tf_op jit(solution)/shard_map/dot_general | solution.py:143
  10.1 0.0 copy-done.1
  10.1 0.0 copy-done.2
  10.1 0.0 copy-done.3
  10.1 0.3 shard_map.91
  10.4 0.9 all_to_all.8
  11.3 7.5 %all-to-all-start = ((bf16[32,2,3200]{2,1,0:T(2,128)(2,1)}), bf16[32,2,3200]{2,1,0:T(2,128)(2,1)S(1)}, u32[]{:S(2)}, u32[]{:S(2)}) async-start(bf16[32,2,3200]{2,1,0:T(2,128)(2,1)} %all_to_all.8), calls=%async_computation | async-start | bytes 819200 | tf_op jit(solution)/shard_map/all_to_all | solution.py:151
  18.8 0.0 copy-start.5
  18.8 0.0 all-gather.2.cloned.1.call-start
  18.9 15.7 %collective-permute-start.7 = (bf16[40,3200]{1,0:T(8,128)(2,1)S(1)}, bf16[40,3200]{1,0:T(8,128)(2,1)S(1)}, u32[]{:S(2)}, u32[]{:S(2)}) collective-permute-start(bf16[40,3200]{1,0:T(8,128)(2,1)S(1)} %fusion), channel_id=1, source_target_pairs={{0,8},{1,9},{2,10},{3,11},{4,12},{5,13},{6,14},{7,15},{8,32},{9,33... | collective-permute-start | bytes 768008 | tf_op jit(solution)/shard_map/ppermute | solution.py:150
  34.6 0.0 all-to-all-done
  34.6 0.2 all_to_all.10
  34.8 13.9 %collective-permute-done.7 = bf16[40,3200]{1,0:T(8,128)(2,1)S(1)} collective-permute-done((bf16[40,3200]{1,0:T(8,128)(2,1)S(1)}, bf16[40,3200]{1,0:T(8,128)(2,1)S(1)}, u32[]{:S(2)}, u32[]{:S(2)}) %collective-permute-start.7) | collective-permute-done | bytes 256032 | tf_op jit(solution)/shard_map/ppermute | solution.py:150
  48.6 0.7 copy-done.4
  49.3 0.0 all-gather.2.cloned.1.call-update
  49.4 0.2 convolution_convert_fusion.1
  49.5 20.1 %collective-permute-start = (bf16[24,3200]{1,0:T(8,128)(2,1)S(1)}, bf16[24,3200]{1,0:T(8,128)(2,1)S(1)}, u32[]{:S(2)}, u32[]{:S(2)}) collective-permute-start(bf16[24,3200]{1,0:T(8,128)(2,1)S(1)} %convolution_convert_fusion.1), channel_id=1, source_target_pairs={{0,32},{1,33},{2,34},{3,35},{4,36},{5,37},{6,38},{7,39},{8,40},{9,... | collective-permute-start | bytes 460808 | tf_op jit(solution)/shard_map/ppermute | solution.py:134
  69.7 0.0 copy-done.8
  69.7 11.8 %collective-permute-start.1 = (f32[640]{0:T(1024)S(1)}, f32[640]{0:T(1024)S(1)}, u32[]{:S(2)}, u32[]{:S(2)}) collective-permute-start(f32[640]{0:T(1024)S(1)} %copy-done.8), channel_id=1, source_target_pairs={{0,8},{1,9},{2,10},{3,11},{4,12},{5,13},{6,14},{7,15},{8,32},{9,33... | collective-permute-start | bytes 7688 | tf_op jit(solution)/shard_map/ppermute | solution.py:134
  81.5 0.2 convolution_convert_fusion.2
  81.7 2.8 %collective-permute-done.1 = f32[640]{0:T(1024)S(1)} collective-permute-done((f32[640]{0:T(1024)S(1)}, f32[640]{0:T(1024)S(1)}, u32[]{:S(2)}, u32[]{:S(2)}) %collective-permute-start.1) | collective-permute-done | bytes 2592 | tf_op jit(solution)/shard_map/ppermute | solution.py:134
  84.4 0.0 collective-permute-done
  84.4 0.2 convert_reduce_fusion
  84.6 0.2 fusion.14
  84.8 0.0 copy-done.5
  84.8 0.1 fusion.16
  85.0 27.4 %collective-permute-start.5 = (bf16[24,3200]{1,0:T(8,128)(2,1)S(1)}, bf16[24,3200]{1,0:T(8,128)(2,1)S(1)}, u32[]{:S(2)}, u32[]{:S(2)}) collective-permute-start(bf16[24,3200]{1,0:T(8,128)(2,1)S(1)} %fusion.16), channel_id=1, source_target_pairs={{0,46},{1,47},{2,0},{3,1},{4,2},{5,3},{6,4},{7,5},{8,6},{9,7},{10,... | collective-permute-start | bytes 460808 | tf_op jit(solution)/shard_map/ppermute | solution.py:134
  112.4 1.9 collective-permute-start.2
  114.3 0.8 collective-permute-done.5
  115.1 6.5 %collective-permute-done.2 = bf16[24,3200]{1,0:T(8,128)(2,1)S(1)} collective-permute-done((bf16[24,3200]{1,0:T(8,128)(2,1)S(1)}, bf16[24,3200]{1,0:T(8,128)(2,1)S(1)}, u32[]{:S(2)}, u32[]{:S(2)}) %collective-permute-start.2) | collective-permute-done | bytes 153632 | tf_op jit(solution)/shard_map/ppermute | solution.py:134
  121.7 1.9 collective-permute-start.3
  123.6 3.9 %collective-permute-start.6 = (bf16[48,3200]{1,0:T(8,128)(2,1)S(1)}, bf16[48,3200]{1,0:T(8,128)(2,1)S(1)}, u32[]{:S(2)}, u32[]{:S(2)}) collective-permute-start(bf16[48,3200]{1,0:T(8,128)(2,1)S(1)} %get-tuple-element.29), channel_id=1, source_target_pairs={{0,47},{1,0},{2,1},{3,2},{4,3},{5,4},{6,5},{7,6},{8,7},{9,8},{10,9... | collective-permute-start | bytes 921608 | tf_op jit(solution)/shard_map/ppermute | solution.py:134
  127.5 1.9 collective-permute-start.4
  129.5 2.5 %collective-permute-done.3 = bf16[48,3200]{1,0:T(8,128)(2,1)S(1)} collective-permute-done((bf16[48,3200]{1,0:T(8,128)(2,1)S(1)}, bf16[48,3200]{1,0:T(8,128)(2,1)S(1)}, u32[]{:S(2)}, u32[]{:S(2)}) %collective-permute-start.3) | collective-permute-done | bytes 307232 | tf_op jit(solution)/shard_map/ppermute | solution.py:134
  132.0 0.8 constant_dynamic-update-slice_fusion.5
  132.7 0.7 constant_dynamic-update-slice_fusion.4
  133.4 3.5 %collective-permute-done.4 = bf16[24,3200]{1,0:T(8,128)(2,1)S(1)} collective-permute-done((bf16[24,3200]{1,0:T(8,128)(2,1)S(1)}, bf16[24,3200]{1,0:T(8,128)(2,1)S(1)}, u32[]{:S(2)}, u32[]{:S(2)}) %collective-permute-start.4) | collective-permute-done | bytes 153632 | tf_op jit(solution)/shard_map/ppermute | solution.py:134
  136.9 0.7 constant_dynamic-update-slice_fusion.3
  137.6 0.0 collective-permute-done.6
  137.6 0.8 constant_dynamic-update-slice_fusion.2
  138.4 0.7 constant_dynamic-update-slice_fusion.1
  139.1 0.8 constant_dynamic-update-slice_fusion.rows_ref
  139.8 7.4 %fusion.11.part_ref = f32[192,3200]{1,0:T(8,128)S(1)} fusion(bf16[640,3200]{1,0:T(8,128)(2,1)} %param.15, bf16[192,3200]{1,0:T(8,128)(2,1)} %constant_dynamic-update-slice_fusion.rows_ref, bf16[3200,640]{1,0:T(8,128)(2,1)} %param.13, f32[640]{0:T(1024)S(1)} %copy-done.8), kind=kOutput, calls=%fused_computation.24 | convolution fusion | flops 1580974080 | bytes 11880960 | tf_op jit(solution)/shard_map/dot_general | solution.py:176
  147.2 3.3 %all-gather.2.cloned.1.call-done.fetched_ref = bf16[1280,3200]{1,0:T(8,128)(2,1)} async-done(((bf16[40,3200]{1,0:T(8,128)(2,1)}), bf16[1280,3200]{1,0:T(8,128)(2,1)}) %all-gather.2.cloned.1.call-update) | async-done | bytes 8192016 | tf_op jit(solution)/shard_map/all_gather | solution.py:155
  150.5 3.3 %copy-done = bf16[1280,3200]{1,0:T(8,128)(2,1)S(1)} copy-done((bf16[1280,3200]{1,0:T(8,128)(2,1)S(1)}, bf16[1280,3200]{1,0:T(8,128)(2,1)}, u32[]{:S(2)}) %copy-start) | copy-done | bytes 8192024
  153.9 4.6 %shard_map.92 = bf16[192,3200]{1,0:T(8,128)(2,1)S(1)} custom-call(bf16[192,3200]{1,0:T(8,128)(2,1)} %constant_dynamic-update-slice_fusion.rows_ref, f32[192,3200]{1,0:T(8,128)S(1)} %fusion.11.part_ref, f32[1,640]{1,0:T(1,128)S(1)} %broadcast_in_dim.7.bias_ref, bf16[1280,3200]{1,0:T(8,128)(2,1)S(1)} %copy-done), custom_call_target="tpu_custom_call" | custom-call | tf_op jit(solution)/shard_map/pallas_call | solution.py:106
  158.4 0.0 copy-start.6
  158.4 0.0 copy-start.7
  158.5 2.4 %collective-permute-start.8 = (bf16[48,3200]{1,0:T(8,128)(2,1)S(1)}, bf16[48,3200]{1,0:T(8,128)(2,1)S(1)}, u32[]{:S(2)}, u32[]{:S(2)}) collective-permute-start(bf16[48,3200]{1,0:T(8,128)(2,1)S(1)} %get-tuple-element.27), channel_id=1, source_target_pairs={{0,47},{1,0},{2,1},{3,2},{4,3},{5,4},{6,5},{7,6},{8,7},{9,8},{10,9... | collective-permute-start | bytes 921608 | tf_op jit(solution)/shard_map/ppermute | solution.py:134
  160.9 3.5 %collective-permute-start.11 = (bf16[48,3200]{1,0:T(8,128)(2,1)S(1)}, bf16[48,3200]{1,0:T(8,128)(2,1)S(1)}, u32[]{:S(2)}, u32[]{:S(2)}) collective-permute-start(bf16[48,3200]{1,0:T(8,128)(2,1)S(1)} %get-tuple-element.28), channel_id=1, source_target_pairs={{0,1},{1,2},{2,3},{3,4},{4,5},{5,6},{6,7},{7,8},{8,9},{9,10},{10,1... | collective-permute-start | bytes 921608 | tf_op jit(solution)/shard_map/ppermute | solution.py:134
  164.4 8.5 %collective-permute-start.9 = (bf16[24,3200]{1,0:T(8,128)(2,1)S(1)}, bf16[24,3200]{1,0:T(8,128)(2,1)S(1)}, u32[]{:S(2)}, u32[]{:S(2)}) collective-permute-start(bf16[24,3200]{1,0:T(8,128)(2,1)S(1)} %slice.43), channel_id=1, source_target_pairs={{0,46},{1,47},{2,0},{3,1},{4,2},{5,3},{6,4},{7,5},{8,6},{9,7},{10,... | collective-permute-start | bytes 460808 | tf_op jit(solution)/shard_map/ppermute | solution.py:134
  172.9 5.7 %collective-permute-done.9 = bf16[24,3200]{1,0:T(8,128)(2,1)S(1)} collective-permute-done((bf16[24,3200]{1,0:T(8,128)(2,1)S(1)}, bf16[24,3200]{1,0:T(8,128)(2,1)S(1)}, u32[]{:S(2)}, u32[]{:S(2)}) %collective-permute-start.9) | collective-permute-done | bytes 153632 | tf_op jit(solution)/shard_map/ppermute | solution.py:134
  178.6 0.0 collective-permute-done.8
  178.6 0.0 collective-permute-done.11
  178.7 0.1 add_convert_fusion.1
  178.8 6.5 %collective-permute-start.10 = (bf16[24,3200]{1,0:T(8,128)(2,1)S(1)}, bf16[24,3200]{1,0:T(8,128)(2,1)S(1)}, u32[]{:S(2)}, u32[]{:S(2)}) collective-permute-start(bf16[24,3200]{1,0:T(8,128)(2,1)S(1)} %get-tuple-element.25), channel_id=1, source_target_pairs={{0,46},{1,47},{2,0},{3,1},{4,2},{5,3},{6,4},{7,5},{8,6},{9,7},{10,... | collective-permute-start | bytes 460808 | tf_op jit(solution)/shard_map/ppermute | solution.py:134
  185.3 1.9 collective-permute-start.12
  187.2 3.1 %collective-permute-done.10 = bf16[24,3200]{1,0:T(8,128)(2,1)S(1)} collective-permute-done((bf16[24,3200]{1,0:T(8,128)(2,1)S(1)}, bf16[24,3200]{1,0:T(8,128)(2,1)S(1)}, u32[]{:S(2)}, u32[]{:S(2)}) %collective-permute-start.10) | collective-permute-done | bytes 153632 | tf_op jit(solution)/shard_map/ppermute | solution.py:134
  190.3 5.7 %collective-permute-done.12 = bf16[24,3200]{1,0:T(8,128)(2,1)S(1)} collective-permute-done((bf16[24,3200]{1,0:T(8,128)(2,1)S(1)}, bf16[24,3200]{1,0:T(8,128)(2,1)S(1)}, u32[]{:S(2)}, u32[]{:S(2)}) %collective-permute-start.12) | collective-permute-done | bytes 153632 | tf_op jit(solution)/shard_map/ppermute | solution.py:134
  196.0 0.0 copy-done.6
  196.0 0.0 copy-done.7
  196.0 0.8 fusion.49
  (11 shorter events, 0.1 us)
Async XLA Ops:
  6.5 3.5 %copy-start.1 = (bf16[1,64,3200]{2,1,0:T(8,128)(2,1)S(1)}, bf16[1,64,3200]{2,1,0:T(8,128)(2,1)}, u32[]{:S(2)}) copy-start(bf16[1,64,3200]{2,1,0:T(8,128)(2,1)} %param.9) | copy-start | bytes 1228804
  6.5 3.5 %copy-start.2 = (s32[1,64]{1,0:T(1,128)S(1)}, s32[1,64]{1,0:T(1,128)}, u32[]{:S(2)}) copy-start(s32[1,64]{1,0:T(1,128)} %live_ref) | copy-start | bytes 772
  6.5 3.5 %copy-start.3 = (s32[1,64]{1,0:T(1,128)S(1)}, s32[1,64]{1,0:T(1,128)}, u32[]{:S(2)}) copy-start(s32[1,64]{1,0:T(1,128)} %order_ref.1) | copy-start | bytes 772
  11.3 58.4 %copy-start.8 = (f32[640]{0:T(1024)S(1)}, f32[640]{0:T(1024)}, u32[]{:S(2)}) copy-start(f32[640]{0:T(1024)} %param.14) | copy-start | bytes 7684
  11.3 23.3 %all-to-all-start = ((bf16[32,2,3200]{2,1,0:T(2,128)(2,1)}), bf16[32,2,3200]{2,1,0:T(2,128)(2,1)S(1)}, u32[]{:S(2)}, u32[]{:S(2)}) async-start(bf16[32,2,3200]{2,1,0:T(2,128)(2,1)} %all_to_all.8), calls=%async_computation | async-start | bytes 819200 | tf_op jit(solution)/shard_map/all_to_all | solution.py:151
  18.8 66.0 %copy-start.5 = (f32[3200]{0:T(1024)S(1)}, f32[3200]{0:T(1024)}, u32[]{:S(2)}) copy-start(f32[3200]{0:T(1024)} %param.12) | copy-start | bytes 38404
  18.8 131.7 %all-gather.2.cloned.1.call-start = ((), (), s32[]{:S(2)}) async-start(), calls=%async_computation.1 | async-start | bytes 8448000 | tf_op jit(solution)/shard_map/all_gather | solution.py:155
  18.9 29.8 %collective-permute-start.7 = (bf16[40,3200]{1,0:T(8,128)(2,1)S(1)}, bf16[40,3200]{1,0:T(8,128)(2,1)S(1)}, u32[]{:S(2)}, u32[]{:S(2)}) collective-permute-start(bf16[40,3200]{1,0:T(8,128)(2,1)S(1)} %fusion), channel_id=1, source_target_pairs={{0,8},{1,9},{2,10},{3,11},{4,12},{5,13},{6,14},{7,15},{8,32},{9,33... | collective-permute-start | bytes 768008 | tf_op jit(solution)/shard_map/ppermute | solution.py:150
  48.6 0.7 copy-start.4
  49.5 34.9 %collective-permute-start = (bf16[24,3200]{1,0:T(8,128)(2,1)S(1)}, bf16[24,3200]{1,0:T(8,128)(2,1)S(1)}, u32[]{:S(2)}, u32[]{:S(2)}) collective-permute-start(bf16[24,3200]{1,0:T(8,128)(2,1)S(1)} %convolution_convert_fusion.1), channel_id=1, source_target_pairs={{0,32},{1,33},{2,34},{3,35},{4,36},{5,37},{6,38},{7,39},{8,40},{9,... | collective-permute-start | bytes 460808 | tf_op jit(solution)/shard_map/ppermute | solution.py:134
  69.7 14.7 %collective-permute-start.1 = (f32[640]{0:T(1024)S(1)}, f32[640]{0:T(1024)S(1)}, u32[]{:S(2)}, u32[]{:S(2)}) collective-permute-start(f32[640]{0:T(1024)S(1)} %copy-done.8), channel_id=1, source_target_pairs={{0,8},{1,9},{2,10},{3,11},{4,12},{5,13},{6,14},{7,15},{8,32},{9,33... | collective-permute-start | bytes 7688 | tf_op jit(solution)/shard_map/ppermute | solution.py:134
  85.0 30.2 %collective-permute-start.5 = (bf16[24,3200]{1,0:T(8,128)(2,1)S(1)}, bf16[24,3200]{1,0:T(8,128)(2,1)S(1)}, u32[]{:S(2)}, u32[]{:S(2)}) collective-permute-start(bf16[24,3200]{1,0:T(8,128)(2,1)S(1)} %fusion.16), channel_id=1, source_target_pairs={{0,46},{1,47},{2,0},{3,1},{4,2},{5,3},{6,4},{7,5},{8,6},{9,7},{10,... | collective-permute-start | bytes 460808 | tf_op jit(solution)/shard_map/ppermute | solution.py:134
  112.4 9.2 %collective-permute-start.2 = (bf16[24,3200]{1,0:T(8,128)(2,1)S(1)}, bf16[24,3200]{1,0:T(8,128)(2,1)S(1)}, u32[]{:S(2)}, u32[]{:S(2)}) collective-permute-start(bf16[24,3200]{1,0:T(8,128)(2,1)S(1)} %fusion.16), channel_id=1, source_target_pairs={{0,2},{1,3},{2,4},{3,5},{4,6},{5,7},{6,8},{7,9},{8,10},{9,11},{10,... | collective-permute-start | bytes 460808 | tf_op jit(solution)/shard_map/ppermute | solution.py:134
  121.7 10.3 %collective-permute-start.3 = (bf16[48,3200]{1,0:T(8,128)(2,1)S(1)}, bf16[48,3200]{1,0:T(8,128)(2,1)S(1)}, u32[]{:S(2)}, u32[]{:S(2)}) collective-permute-start(bf16[48,3200]{1,0:T(8,128)(2,1)S(1)} %get-tuple-element.30), channel_id=1, source_target_pairs={{0,1},{1,2},{2,3},{3,4},{4,5},{5,6},{6,7},{7,8},{8,9},{9,10},{10,1... | collective-permute-start | bytes 921608 | tf_op jit(solution)/shard_map/ppermute | solution.py:134
  123.6 14.0 %collective-permute-start.6 = (bf16[48,3200]{1,0:T(8,128)(2,1)S(1)}, bf16[48,3200]{1,0:T(8,128)(2,1)S(1)}, u32[]{:S(2)}, u32[]{:S(2)}) collective-permute-start(bf16[48,3200]{1,0:T(8,128)(2,1)S(1)} %get-tuple-element.29), channel_id=1, source_target_pairs={{0,47},{1,0},{2,1},{3,2},{4,3},{5,4},{6,5},{7,6},{8,7},{9,8},{10,9... | collective-permute-start | bytes 921608 | tf_op jit(solution)/shard_map/ppermute | solution.py:134
  127.5 9.4 %collective-permute-start.4 = (bf16[24,3200]{1,0:T(8,128)(2,1)S(1)}, bf16[24,3200]{1,0:T(8,128)(2,1)S(1)}, u32[]{:S(2)}, u32[]{:S(2)}) collective-permute-start(bf16[24,3200]{1,0:T(8,128)(2,1)S(1)} %collective-permute-done.2), channel_id=1, source_target_pairs={{0,2},{1,3},{2,4},{3,5},{4,6},{5,7},{6,8},{7,9},{8,10},{9,11},{10,... | collective-permute-start | bytes 460808 | tf_op jit(solution)/shard_map/ppermute | solution.py:134
  150.5 3.3 %copy-start = (bf16[1280,3200]{1,0:T(8,128)(2,1)S(1)}, bf16[1280,3200]{1,0:T(8,128)(2,1)}, u32[]{:S(2)}) copy-start(bf16[1280,3200]{1,0:T(8,128)(2,1)} %all-gather.2.cloned.1.call-done.fetched_ref) | copy-start | bytes 24576004
  158.4 37.6 %copy-start.6 = (f32[3200]{0:T(1024)S(1)}, f32[3200]{0:T(1024)}, u32[]{:S(2)}) copy-start(f32[3200]{0:T(1024)} %param.16) | copy-start | bytes 38404
  158.4 37.6 %copy-start.7 = (f32[3200]{0:T(1024)S(1)}, f32[3200]{0:T(1024)}, u32[]{:S(2)}) copy-start(f32[3200]{0:T(1024)} %param.17) | copy-start | bytes 38404
  158.5 20.1 %collective-permute-start.8 = (bf16[48,3200]{1,0:T(8,128)(2,1)S(1)}, bf16[48,3200]{1,0:T(8,128)(2,1)S(1)}, u32[]{:S(2)}, u32[]{:S(2)}) collective-permute-start(bf16[48,3200]{1,0:T(8,128)(2,1)S(1)} %get-tuple-element.27), channel_id=1, source_target_pairs={{0,47},{1,0},{2,1},{3,2},{4,3},{5,4},{6,5},{7,6},{8,7},{9,8},{10,9... | collective-permute-start | bytes 921608 | tf_op jit(solution)/shard_map/ppermute | solution.py:134
  160.9 17.8 %collective-permute-start.11 = (bf16[48,3200]{1,0:T(8,128)(2,1)S(1)}, bf16[48,3200]{1,0:T(8,128)(2,1)S(1)}, u32[]{:S(2)}, u32[]{:S(2)}) collective-permute-start(bf16[48,3200]{1,0:T(8,128)(2,1)S(1)} %get-tuple-element.28), channel_id=1, source_target_pairs={{0,1},{1,2},{2,3},{3,4},{4,5},{5,6},{6,7},{7,8},{8,9},{9,10},{10,1... | collective-permute-start | bytes 921608 | tf_op jit(solution)/shard_map/ppermute | solution.py:134
  164.4 14.3 %collective-permute-start.9 = (bf16[24,3200]{1,0:T(8,128)(2,1)S(1)}, bf16[24,3200]{1,0:T(8,128)(2,1)S(1)}, u32[]{:S(2)}, u32[]{:S(2)}) collective-permute-start(bf16[24,3200]{1,0:T(8,128)(2,1)S(1)} %slice.43), channel_id=1, source_target_pairs={{0,46},{1,47},{2,0},{3,1},{4,2},{5,3},{6,4},{7,5},{8,6},{9,7},{10,... | collective-permute-start | bytes 460808 | tf_op jit(solution)/shard_map/ppermute | solution.py:134
  178.8 11.5 %collective-permute-start.10 = (bf16[24,3200]{1,0:T(8,128)(2,1)S(1)}, bf16[24,3200]{1,0:T(8,128)(2,1)S(1)}, u32[]{:S(2)}, u32[]{:S(2)}) collective-permute-start(bf16[24,3200]{1,0:T(8,128)(2,1)S(1)} %get-tuple-element.25), channel_id=1, source_target_pairs={{0,46},{1,47},{2,0},{3,1},{4,2},{5,3},{6,4},{7,5},{8,6},{9,7},{10,... | collective-permute-start | bytes 460808 | tf_op jit(solution)/shard_map/ppermute | solution.py:134
  185.3 10.7 %collective-permute-start.12 = (bf16[24,3200]{1,0:T(8,128)(2,1)S(1)}, bf16[24,3200]{1,0:T(8,128)(2,1)S(1)}, u32[]{:S(2)}, u32[]{:S(2)}) collective-permute-start(bf16[24,3200]{1,0:T(8,128)(2,1)S(1)} %get-tuple-element.26), channel_id=1, source_target_pairs={{0,2},{1,3},{2,4},{3,5},{4,6},{5,7},{6,8},{7,9},{8,10},{9,11},{10,... | collective-permute-start | bytes 460808 | tf_op jit(solution)/shard_map/ppermute | solution.py:134
Sparse Core Ops, SparseCore 0:
  49.5 101.0 all-gather.1

commit v7 on v4

--- a/solution.py
+++ b/solution.py
@@ -118,7 +118,7 @@
             pltpu.VMEM((count, units), jnp.bfloat16),
             pltpu.SemaphoreType.DMA((2,)),
         ],
-        compiler_params=pltpu.CompilerParams(vmem_limit_bytes=28 * 1024 * 1024),
+        compiler_params=pltpu.CompilerParams(vmem_limit_bytes=46 * 1024 * 1024),
     )(rows, part, bias[None], fetched)
 
 
@@ -152,13 +152,13 @@
     ).astype(jnp.bfloat16)
     piece2 = lax.dynamic_slice_in_dim(fc2_weight, first, depth, axis=0)
     piece = jnp.where(upper, piece1, piece2)
+    piece, live = lax.optimization_barrier((piece, live))
     rows, pick_far, pick_near = plan(patches[0], live, rounds, mine, keep)
-    piece, rows = lax.optimization_barrier((piece, rows))
     piece = lax.ppermute(piece, AXES, opposite_pairs(sections, dps, dps // 2))
     rows = lax.all_to_all(
         rows, "section", split_axis=0, concat_axis=0, axis_index_groups=groups, tiled=True
     )
-    piece = lax.optimization_barrier((piece, rows))[0]
+    rows = lax.optimization_barrier((rows, piece))[0]
     fetched = lax.all_gather(piece, "section", axis=0, axis_index_groups=groups, tiled=True)
     crossing = pick(pick_far, rows)
     bias = lax.optimization_barrier((fc1_bias, crossing))[0]

time: 208 us -> 212 us (1.019)
  the two profiles are of different devices: /device:TPU:32 before, /device:TPU:2 now
where the time goes in v7:
time: 212 us
  starting transfers between devices  84.4 us (40%)
  waiting for transfers between devices  55.5 us (26%)
  blocking collectives  33.5 us (16%)
  between operations  13.7 us (6%)
  matrix products  10.9 us (5%)
  Pallas kernels  7.2 us (3%)
  local copies, waits for them, and re-layouts  4.65 us (2%)
    ppermute x12, starting transfers between devices, send(): return lax.ppermute(value, AXES, shift_pairs(sections, dps, hops))  68.7 us
    ppermute x12, waiting for transfers between devices, send(): return lax.ppermute(value, AXES, shift_pairs(sections, dps, hops))  43.2 us
    all_to_all x1, blocking collectives, per_device(): lax.all_to_all(rows, 'section', split_axis=0, concat_axis=0, axis_index_g...  33.5 us
    ppermute x1, starting transfers between devices, per_device(): piece = lax.ppermute(piece, AXES, opposite_pairs(sections, dps, dps // 2))  15.7 us
    ppermute x1, waiting for transfers between devices, per_device(): piece = lax.ppermute(piece, AXES, opposite_pairs(sections, dps, dps // 2))  12.3 us
    dot_general x1, matrix products, per_device(): part = jnp.dot(hidden, fc2_weight, preferred_element_type=f32)  6.96 us
    pallas_call x1, Pallas kernels, add_away(): pl.pallas_call(away_kernel, out_shape=jax.ShapeDtypeStruct((count, width)...  6.85 us
    unnamed x21, local copies, waits for them, and re-layouts  4.28 us
  transfers between devices with their start and end apart: 14, of which 9 were waited for; matrix products, arithmetic and copies ran while one was open for 6% of the time, Pallas kernels for 0%

profile of v7, /device:TPU:2, one launch (start us, length us, event | category | flops | bytes accessed | tf_op | source)
XLA Modules:
  0.0 211.8 jit_solution(15220387224368898267)
XLA Ops:
  6.5 0.0 all-gather.2.cloned.1.call-start
  6.5 0.0 copy-start
  6.5 0.0 copy-start.1
  6.5 0.0 copy-start.2
  6.6 3.5 %fusion = bf16[40,3200]{1,0:T(8,128)(2,1)S(1)} fusion(bf16[3200,640]{1,0:T(8,128)(2,1)} %param.13, bf16[640,3200]{1,0:T(8,128)(2,1)} %param.15, s32[]{:T(128)S(6)} %select_n.12, pred[]{:T(512)S(6)} %lt.6, s32[40]{0:T(128)S(1)} %iota_add_fusion), kind=kOutput, calls=%fused_computation.1 | convolution fusion | flops 164121600 | bytes 4608165 | tf_op jit(solution)/shard_map/dot_general | solution.py:150
  10.1 15.7 %collective-permute-start = (bf16[40,3200]{1,0:T(8,128)(2,1)S(1)}, bf16[40,3200]{1,0:T(8,128)(2,1)S(1)}, u32[]{:S(2)}, u32[]{:S(2)}) collective-permute-start(bf16[40,3200]{1,0:T(8,128)(2,1)S(1)} %fusion), channel_id=1, source_target_pairs={{0,8},{1,9},{2,10},{3,11},{4,12},{5,13},{6,14},{7,15},{8,32},{9,33... | collective-permute-start | bytes 768008 | tf_op jit(solution)/shard_map/ppermute | solution.py:157
  25.8 12.3 %collective-permute-done = bf16[40,3200]{1,0:T(8,128)(2,1)S(1)} collective-permute-done((bf16[40,3200]{1,0:T(8,128)(2,1)S(1)}, bf16[40,3200]{1,0:T(8,128)(2,1)S(1)}, u32[]{:S(2)}, u32[]{:S(2)}) %collective-permute-start) | collective-permute-done | bytes 256032 | tf_op jit(solution)/shard_map/ppermute | solution.py:157
  38.1 0.0 copy-start.3
  38.1 0.7 copy-done.3
  38.8 0.0 all-gather.2.cloned.1.call-update
  38.8 0.0 copy-done
  38.8 0.0 copy-done.1
  38.8 0.0 copy-done.2
  38.8 0.3 shard_map.91
  39.2 0.2 all_to_all.8
  39.3 0.0 copy-start.7
  39.4 33.5 %all_to_all.12 = bf16[32,2,3200]{2,1,0:T(2,128)(2,1)S(1)} all-to-all(bf16[32,2,3200]{2,1,0:T(2,128)(2,1)S(1)} %all_to_all.8), channel_id=1, replica_groups={{0,16,64,80,128,144,192,208,256,272,320,336,384,400,448,464,512,528,576..., dimensions={0} | all-to-all | bytes 819200 | tf_op jit(solution)/shard_map/all_to_all | solution.py:158
  72.8 0.0 copy-start.4
  72.8 0.2 all_to_all.10
  73.0 0.2 convolution_convert_fusion.1
  73.1 19.5 %collective-permute-start.1 = (bf16[24,3200]{1,0:T(8,128)(2,1)S(1)}, bf16[24,3200]{1,0:T(8,128)(2,1)S(1)}, u32[]{:S(2)}, u32[]{:S(2)}) collective-permute-start(bf16[24,3200]{1,0:T(8,128)(2,1)S(1)} %convolution_convert_fusion.1), channel_id=1, source_target_pairs={{0,32},{1,33},{2,34},{3,35},{4,36},{5,37},{6,38},{7,39},{8,40},{9,... | collective-permute-start | bytes 460808 | tf_op jit(solution)/shard_map/ppermute | solution.py:141
  92.6 0.0 copy-done.7
  92.6 7.0 %collective-permute-start.2 = (f32[640]{0:T(1024)S(1)}, f32[640]{0:T(1024)S(1)}, u32[]{:S(2)}, u32[]{:S(2)}) collective-permute-start(f32[640]{0:T(1024)S(1)} %copy-done.7), channel_id=1, source_target_pairs={{0,8},{1,9},{2,10},{3,11},{4,12},{5,13},{6,14},{7,15},{8,32},{9,33... | collective-permute-start | bytes 7688 | tf_op jit(solution)/shard_map/ppermute | solution.py:141
  99.7 16.2 %collective-permute-done.2 = f32[640]{0:T(1024)S(1)} collective-permute-done((f32[640]{0:T(1024)S(1)}, f32[640]{0:T(1024)S(1)}, u32[]{:S(2)}, u32[]{:S(2)}) %collective-permute-start.2) | collective-permute-done | bytes 2592 | tf_op jit(solution)/shard_map/ppermute | solution.py:141
  115.9 1.4 collective-permute-done.1
  117.3 0.3 fusion.78
  117.6 0.2 multiply_reduce_fusion
  117.8 0.0 copy-done.4
  117.8 0.1 multiply_convert_fusion
  118.0 1.9 collective-permute-start.6
  119.9 4.8 %collective-permute-start.3 = (bf16[24,3200]{1,0:T(8,128)(2,1)S(1)}, bf16[24,3200]{1,0:T(8,128)(2,1)S(1)}, u32[]{:S(2)}, u32[]{:S(2)}) collective-permute-start(bf16[24,3200]{1,0:T(8,128)(2,1)S(1)} %multiply_convert_fusion), channel_id=1, source_target_pairs={{0,2},{1,3},{2,4},{3,5},{4,6},{5,7},{6,8},{7,9},{8,10},{9,11},{10,... | collective-permute-start | bytes 460808 | tf_op jit(solution)/shard_map/ppermute | solution.py:141
  124.7 4.8 %collective-permute-done.6 = bf16[24,3200]{1,0:T(8,128)(2,1)S(1)} collective-permute-done((bf16[24,3200]{1,0:T(8,128)(2,1)S(1)}, bf16[24,3200]{1,0:T(8,128)(2,1)S(1)}, u32[]{:S(2)}, u32[]{:S(2)}) %collective-permute-start.6) | collective-permute-done | bytes 153632 | tf_op jit(solution)/shard_map/ppermute | solution.py:141
  129.5 0.0 collective-permute-done.3
  129.5 10.6 %collective-permute-start.4 = (bf16[48,3200]{1,0:T(8,128)(2,1)S(1)}, bf16[48,3200]{1,0:T(8,128)(2,1)S(1)}, u32[]{:S(2)}, u32[]{:S(2)}) collective-permute-start(bf16[48,3200]{1,0:T(8,128)(2,1)S(1)} %get-tuple-element.28), channel_id=1, source_target_pairs={{0,1},{1,2},{2,3},{3,4},{4,5},{5,6},{6,7},{7,8},{8,9},{9,10},{10,1... | collective-permute-start | bytes 921608 | tf_op jit(solution)/shard_map/ppermute | solution.py:141
  140.2 1.9 collective-permute-start.7
  142.1 3.4 %collective-permute-start.5 = (bf16[24,3200]{1,0:T(8,128)(2,1)S(1)}, bf16[24,3200]{1,0:T(8,128)(2,1)S(1)}, u32[]{:S(2)}, u32[]{:S(2)}) collective-permute-start(bf16[24,3200]{1,0:T(8,128)(2,1)S(1)} %collective-permute-done.3), channel_id=1, source_target_pairs={{0,2},{1,3},{2,4},{3,5},{4,6},{5,7},{6,8},{7,9},{8,10},{9,11},{10,... | collective-permute-start | bytes 460808 | tf_op jit(solution)/shard_map/ppermute | solution.py:141
  145.5 1.3 collective-permute-done.4
  146.8 0.8 constant_dynamic-update-slice_fusion.5
  147.5 0.7 constant_dynamic-update-slice_fusion.4
  148.2 5.4 %collective-permute-done.5 = bf16[24,3200]{1,0:T(8,128)(2,1)S(1)} collective-permute-done((bf16[24,3200]{1,0:T(8,128)(2,1)S(1)}, bf16[24,3200]{1,0:T(8,128)(2,1)S(1)}, u32[]{:S(2)}, u32[]{:S(2)}) %collective-permute-start.5) | collective-permute-done | bytes 153632 | tf_op jit(solution)/shard_map/ppermute | solution.py:141
  153.6 0.7 constant_dynamic-update-slice_fusion.3
  154.2 0.0 collective-permute-done.7
  154.2 0.8 constant_dynamic-update-slice_fusion.2
  155.0 0.7 constant_dynamic-update-slice_fusion.1
  155.7 0.8 constant_dynamic-update-slice_fusion.rows_ref
  156.4 7.0 %fusion.13.part_ref = f32[192,3200]{1,0:T(8,128)S(1)} fusion(bf16[640,3200]{1,0:T(8,128)(2,1)} %param.15, bf16[192,3200]{1,0:T(8,128)(2,1)} %constant_dynamic-update-slice_fusion.rows_ref, bf16[3200,640]{1,0:T(8,128)(2,1)} %param.13, f32[640]{0:T(1024)S(1)} %copy-done.7), kind=kOutput, calls=%fused_computation.26 | convolution fusion | flops 1580974080 | bytes 11880960 | tf_op jit(solution)/shard_map/dot_general | solution.py:183
  163.4 0.0 all-gather.2.cloned.1.call-done.fetched_ref
  163.4 6.9 %shard_map.92 = bf16[192,3200]{1,0:T(8,128)(2,1)S(1)} custom-call(bf16[192,3200]{1,0:T(8,128)(2,1)} %constant_dynamic-update-slice_fusion.rows_ref, f32[192,3200]{1,0:T(8,128)S(1)} %fusion.13.part_ref, f32[1,640]{1,0:T(1,128)S(1)} %broadcast_in_dim.7.bias_ref, bf16[1280,3200]{1,0:T(8,128)(2,1)} %all-gather.2.cloned.1.call-done.fetched_ref), custom_call_target="tpu_custom_call" | custom-call | tf_op jit(solution)/shard_map/pallas_call | solution.py:110
  170.3 0.0 copy-start.5
  170.3 0.0 copy-start.6
  170.4 2.3 %collective-permute-start.8 = (bf16[48,3200]{1,0:T(8,128)(2,1)S(1)}, bf16[48,3200]{1,0:T(8,128)(2,1)S(1)}, u32[]{:S(2)}, u32[]{:S(2)}) collective-permute-start(bf16[48,3200]{1,0:T(8,128)(2,1)S(1)} %get-tuple-element.25), channel_id=1, source_target_pairs={{0,47},{1,0},{2,1},{3,2},{4,3},{5,4},{6,5},{7,6},{8,7},{9,8},{10,9... | collective-permute-start | bytes 921608 | tf_op jit(solution)/shard_map/ppermute | solution.py:141
  172.7 3.5 %collective-permute-start.11 = (bf16[48,3200]{1,0:T(8,128)(2,1)S(1)}, bf16[48,3200]{1,0:T(8,128)(2,1)S(1)}, u32[]{:S(2)}, u32[]{:S(2)}) collective-permute-start(bf16[48,3200]{1,0:T(8,128)(2,1)S(1)} %get-tuple-element.26), channel_id=1, source_target_pairs={{0,1},{1,2},{2,3},{3,4},{4,5},{5,6},{6,7},{7,8},{8,9},{9,10},{10,1... | collective-permute-start | bytes 921608 | tf_op jit(solution)/shard_map/ppermute | solution.py:141
  176.3 4.3 %collective-permute-start.9 = (bf16[24,3200]{1,0:T(8,128)(2,1)S(1)}, bf16[24,3200]{1,0:T(8,128)(2,1)S(1)}, u32[]{:S(2)}, u32[]{:S(2)}) collective-permute-start(bf16[24,3200]{1,0:T(8,128)(2,1)S(1)} %slice.43), channel_id=1, source_target_pairs={{0,46},{1,47},{2,0},{3,1},{4,2},{5,3},{6,4},{7,5},{8,6},{9,7},{10,... | collective-permute-start | bytes 460808 | tf_op jit(solution)/shard_map/ppermute | solution.py:141
  180.6 4.9 %collective-permute-done.9 = bf16[24,3200]{1,0:T(8,128)(2,1)S(1)} collective-permute-done((bf16[24,3200]{1,0:T(8,128)(2,1)S(1)}, bf16[24,3200]{1,0:T(8,128)(2,1)S(1)}, u32[]{:S(2)}, u32[]{:S(2)}) %collective-permute-start.9) | collective-permute-done | bytes 153632 | tf_op jit(solution)/shard_map/ppermute | solution.py:141
  185.5 0.0 collective-permute-done.8
  185.5 0.0 collective-permute-done.11
  185.5 0.1 add_convert_fusion.2
  185.6 7.4 %collective-permute-start.10 = (bf16[24,3200]{1,0:T(8,128)(2,1)S(1)}, bf16[24,3200]{1,0:T(8,128)(2,1)S(1)}, u32[]{:S(2)}, u32[]{:S(2)}) collective-permute-start(bf16[24,3200]{1,0:T(8,128)(2,1)S(1)} %get-tuple-element.23), channel_id=1, source_target_pairs={{0,46},{1,47},{2,0},{3,1},{4,2},{5,3},{6,4},{7,5},{8,6},{9,7},{10,... | collective-permute-start | bytes 460808 | tf_op jit(solution)/shard_map/ppermute | solution.py:141
  193.0 1.9 collective-permute-start.12
  194.9 2.6 %collective-permute-done.10 = bf16[24,3200]{1,0:T(8,128)(2,1)S(1)} collective-permute-done((bf16[24,3200]{1,0:T(8,128)(2,1)S(1)}, bf16[24,3200]{1,0:T(8,128)(2,1)S(1)}, u32[]{:S(2)}, u32[]{:S(2)}) %collective-permute-start.10) | collective-permute-done | bytes 153632 | tf_op jit(solution)/shard_map/ppermute | solution.py:141
  197.5 6.6 %collective-permute-done.12 = bf16[24,3200]{1,0:T(8,128)(2,1)S(1)} collective-permute-done((bf16[24,3200]{1,0:T(8,128)(2,1)S(1)}, bf16[24,3200]{1,0:T(8,128)(2,1)S(1)}, u32[]{:S(2)}, u32[]{:S(2)}) %collective-permute-start.12) | collective-permute-done | bytes 153632 | tf_op jit(solution)/shard_map/ppermute | solution.py:141
  204.2 0.0 copy-done.5
  204.2 0.0 copy-done.6
  204.2 0.8 fusion.45
  (7 shorter events, 0.1 us)
Async XLA Ops:
  6.5 156.9 %all-gather.2.cloned.1.call-start = ((), (), s32[]{:S(2)}) async-start(), calls=%async_computation.1 | async-start | bytes 8448000 | tf_op jit(solution)/shard_map/all_gather | solution.py:162
  6.5 32.3 %copy-start = (bf16[1,64,3200]{2,1,0:T(8,128)(2,1)S(1)}, bf16[1,64,3200]{2,1,0:T(8,128)(2,1)}, u32[]{:S(2)}) copy-start(bf16[1,64,3200]{2,1,0:T(8,128)(2,1)} %param.9) | copy-start | bytes 1228804
  6.5 32.3 %copy-start.1 = (s32[1,64]{1,0:T(1,128)S(1)}, s32[1,64]{1,0:T(1,128)}, u32[]{:S(2)}) copy-start(s32[1,64]{1,0:T(1,128)} %live_ref) | copy-start | bytes 772
  6.5 32.3 %copy-start.2 = (s32[1,64]{1,0:T(1,128)S(1)}, s32[1,64]{1,0:T(1,128)}, u32[]{:S(2)}) copy-start(s32[1,64]{1,0:T(1,128)} %order_ref.1) | copy-start | bytes 772
  10.1 28.0 %collective-permute-start = (bf16[40,3200]{1,0:T(8,128)(2,1)S(1)}, bf16[40,3200]{1,0:T(8,128)(2,1)S(1)}, u32[]{:S(2)}, u32[]{:S(2)}) collective-permute-start(bf16[40,3200]{1,0:T(8,128)(2,1)S(1)} %fusion), channel_id=1, source_target_pairs={{0,8},{1,9},{2,10},{3,11},{4,12},{5,13},{6,14},{7,15},{8,32},{9,33... | collective-permute-start | bytes 768008 | tf_op jit(solution)/shard_map/ppermute | solution.py:157
  38.1 0.7 copy-start.3
  39.3 53.3 %copy-start.7 = (f32[640]{0:T(1024)S(1)}, f32[640]{0:T(1024)}, u32[]{:S(2)}) copy-start(f32[640]{0:T(1024)} %param.14) | copy-start | bytes 7684
  72.8 45.0 %copy-start.4 = (f32[3200]{0:T(1024)S(1)}, f32[3200]{0:T(1024)}, u32[]{:S(2)}) copy-start(f32[3200]{0:T(1024)} %param.12) | copy-start | bytes 38404
  73.1 44.1 %collective-permute-start.1 = (bf16[24,3200]{1,0:T(8,128)(2,1)S(1)}, bf16[24,3200]{1,0:T(8,128)(2,1)S(1)}, u32[]{:S(2)}, u32[]{:S(2)}) collective-permute-start(bf16[24,3200]{1,0:T(8,128)(2,1)S(1)} %convolution_convert_fusion.1), channel_id=1, source_target_pairs={{0,32},{1,33},{2,34},{3,35},{4,36},{5,37},{6,38},{7,39},{8,40},{9,... | collective-permute-start | bytes 460808 | tf_op jit(solution)/shard_map/ppermute | solution.py:141
  92.6 23.2 %collective-permute-start.2 = (f32[640]{0:T(1024)S(1)}, f32[640]{0:T(1024)S(1)}, u32[]{:S(2)}, u32[]{:S(2)}) collective-permute-start(f32[640]{0:T(1024)S(1)} %copy-done.7), channel_id=1, source_target_pairs={{0,8},{1,9},{2,10},{3,11},{4,12},{5,13},{6,14},{7,15},{8,32},{9,33... | collective-permute-start | bytes 7688 | tf_op jit(solution)/shard_map/ppermute | solution.py:141
  118.0 11.5 %collective-permute-start.6 = (bf16[24,3200]{1,0:T(8,128)(2,1)S(1)}, bf16[24,3200]{1,0:T(8,128)(2,1)S(1)}, u32[]{:S(2)}, u32[]{:S(2)}) collective-permute-start(bf16[24,3200]{1,0:T(8,128)(2,1)S(1)} %multiply_convert_fusion), channel_id=1, source_target_pairs={{0,46},{1,47},{2,0},{3,1},{4,2},{5,3},{6,4},{7,5},{8,6},{9,7},{10,... | collective-permute-start | bytes 460808 | tf_op jit(solution)/shard_map/ppermute | solution.py:141
  119.9 9.6 %collective-permute-start.3 = (bf16[24,3200]{1,0:T(8,128)(2,1)S(1)}, bf16[24,3200]{1,0:T(8,128)(2,1)S(1)}, u32[]{:S(2)}, u32[]{:S(2)}) collective-permute-start(bf16[24,3200]{1,0:T(8,128)(2,1)S(1)} %multiply_convert_fusion), channel_id=1, source_target_pairs={{0,2},{1,3},{2,4},{3,5},{4,6},{5,7},{6,8},{7,9},{8,10},{9,11},{10,... | collective-permute-start | bytes 460808 | tf_op jit(solution)/shard_map/ppermute | solution.py:141
  129.5 17.2 %collective-permute-start.4 = (bf16[48,3200]{1,0:T(8,128)(2,1)S(1)}, bf16[48,3200]{1,0:T(8,128)(2,1)S(1)}, u32[]{:S(2)}, u32[]{:S(2)}) collective-permute-start(bf16[48,3200]{1,0:T(8,128)(2,1)S(1)} %get-tuple-element.28), channel_id=1, source_target_pairs={{0,1},{1,2},{2,3},{3,4},{4,5},{5,6},{6,7},{7,8},{8,9},{9,10},{10,1... | collective-permute-start | bytes 921608 | tf_op jit(solution)/shard_map/ppermute | solution.py:141
  140.2 14.1 %collective-permute-start.7 = (bf16[48,3200]{1,0:T(8,128)(2,1)S(1)}, bf16[48,3200]{1,0:T(8,128)(2,1)S(1)}, u32[]{:S(2)}, u32[]{:S(2)}) collective-permute-start(bf16[48,3200]{1,0:T(8,128)(2,1)S(1)} %get-tuple-element.27), channel_id=1, source_target_pairs={{0,47},{1,0},{2,1},{3,2},{4,3},{5,4},{6,5},{7,6},{8,7},{9,8},{10,9... | collective-permute-start | bytes 921608 | tf_op jit(solution)/shard_map/ppermute | solution.py:141
  142.1 11.5 %collective-permute-start.5 = (bf16[24,3200]{1,0:T(8,128)(2,1)S(1)}, bf16[24,3200]{1,0:T(8,128)(2,1)S(1)}, u32[]{:S(2)}, u32[]{:S(2)}) collective-permute-start(bf16[24,3200]{1,0:T(8,128)(2,1)S(1)} %collective-permute-done.3), channel_id=1, source_target_pairs={{0,2},{1,3},{2,4},{3,5},{4,6},{5,7},{6,8},{7,9},{8,10},{9,11},{10,... | collective-permute-start | bytes 460808 | tf_op jit(solution)/shard_map/ppermute | solution.py:141
  170.3 33.9 %copy-start.5 = (f32[3200]{0:T(1024)S(1)}, f32[3200]{0:T(1024)}, u32[]{:S(2)}) copy-start(f32[3200]{0:T(1024)} %param.16) | copy-start | bytes 38404
  170.3 33.9 %copy-start.6 = (f32[3200]{0:T(1024)S(1)}, f32[3200]{0:T(1024)}, u32[]{:S(2)}) copy-start(f32[3200]{0:T(1024)} %param.17) | copy-start | bytes 38404
  170.4 15.1 %collective-permute-start.8 = (bf16[48,3200]{1,0:T(8,128)(2,1)S(1)}, bf16[48,3200]{1,0:T(8,128)(2,1)S(1)}, u32[]{:S(2)}, u32[]{:S(2)}) collective-permute-start(bf16[48,3200]{1,0:T(8,128)(2,1)S(1)} %get-tuple-element.25), channel_id=1, source_target_pairs={{0,47},{1,0},{2,1},{3,2},{4,3},{5,4},{6,5},{7,6},{8,7},{9,8},{10,9... | collective-permute-start | bytes 921608 | tf_op jit(solution)/shard_map/ppermute | solution.py:141
  172.7 12.8 %collective-permute-start.11 = (bf16[48,3200]{1,0:T(8,128)(2,1)S(1)}, bf16[48,3200]{1,0:T(8,128)(2,1)S(1)}, u32[]{:S(2)}, u32[]{:S(2)}) collective-permute-start(bf16[48,3200]{1,0:T(8,128)(2,1)S(1)} %get-tuple-element.26), channel_id=1, source_target_pairs={{0,1},{1,2},{2,3},{3,4},{4,5},{5,6},{6,7},{7,8},{8,9},{9,10},{10,1... | collective-permute-start | bytes 921608 | tf_op jit(solution)/shard_map/ppermute | solution.py:141
  176.3 9.3 %collective-permute-start.9 = (bf16[24,3200]{1,0:T(8,128)(2,1)S(1)}, bf16[24,3200]{1,0:T(8,128)(2,1)S(1)}, u32[]{:S(2)}, u32[]{:S(2)}) collective-permute-start(bf16[24,3200]{1,0:T(8,128)(2,1)S(1)} %slice.43), channel_id=1, source_target_pairs={{0,46},{1,47},{2,0},{3,1},{4,2},{5,3},{6,4},{7,5},{8,6},{9,7},{10,... | collective-permute-start | bytes 460808 | tf_op jit(solution)/shard_map/ppermute | solution.py:141
  185.6 11.9 %collective-permute-start.10 = (bf16[24,3200]{1,0:T(8,128)(2,1)S(1)}, bf16[24,3200]{1,0:T(8,128)(2,1)S(1)}, u32[]{:S(2)}, u32[]{:S(2)}) collective-permute-start(bf16[24,3200]{1,0:T(8,128)(2,1)S(1)} %get-tuple-element.23), channel_id=1, source_target_pairs={{0,46},{1,47},{2,0},{3,1},{4,2},{5,3},{6,4},{7,5},{8,6},{9,7},{10,... | collective-permute-start | bytes 460808 | tf_op jit(solution)/shard_map/ppermute | solution.py:141
  193.0 11.1 %collective-permute-start.12 = (bf16[24,3200]{1,0:T(8,128)(2,1)S(1)}, bf16[24,3200]{1,0:T(8,128)(2,1)S(1)}, u32[]{:S(2)}, u32[]{:S(2)}) collective-permute-start(bf16[24,3200]{1,0:T(8,128)(2,1)S(1)} %get-tuple-element.24), channel_id=1, source_target_pairs={{0,2},{1,3},{2,4},{3,5},{4,6},{5,7},{6,8},{7,9},{8,10},{9,11},{10,... | collective-permute-start | bytes 460808 | tf_op jit(solution)/shard_map/ppermute | solution.py:141
Sparse Core Ops, SparseCore 0:
  38.9 103.0 all-gather.1

commit v8 on v7

--- a/solution.py
+++ b/solution.py
@@ -155,10 +155,15 @@
     piece, live = lax.optimization_barrier((piece, live))
     rows, pick_far, pick_near = plan(patches[0], live, rounds, mine, keep)
     piece = lax.ppermute(piece, AXES, opposite_pairs(sections, dps, dps // 2))
-    rows = lax.all_to_all(
-        rows, "section", split_axis=0, concat_axis=0, axis_index_groups=groups, tiled=True
+    rows = lax.cond(
+        live[0, 0] > 0,
+        lambda rows: lax.all_to_all(
+            rows, "section", split_axis=0, concat_axis=0, axis_index_groups=groups, tiled=True
+        ),
+        jnp.zeros_like,
+        rows,
     )
-    rows = lax.optimization_barrier((rows, piece))[0]
+    piece = lax.optimization_barrier((piece, rows))[0]
     fetched = lax.all_gather(piece, "section", axis=0, axis_index_groups=groups, tiled=True)
     crossing = pick(pick_far, rows)
     bias = lax.optimization_barrier((fc1_bias, crossing))[0]

time: 212 us -> 198 us (0.934)
  the two profiles are of different devices: /device:TPU:2 before, /device:TPU:1 now
where the time goes in v8:
time: 198 us
  starting transfers between devices  85.4 us (43%)
  waiting for transfers between devices  56.4 us (28%)
  blocking collectives  17.3 us (9%)
  between operations  13.7 us (7%)
  matrix products  10.9 us (6%)
  Pallas kernels  7.26 us (4%)
  local copies, waits for them, and re-layouts  4.65 us (2%)
  other arithmetic  2.23 us (1%)
    ppermute x12, starting transfers between devices, send(): return lax.ppermute(value, AXES, shift_pairs(sections, dps, hops))  61.8 us
    ppermute x12, waiting for transfers between devices, send(): return lax.ppermute(value, AXES, shift_pairs(sections, dps, hops))  51.9 us
    ppermute x1, starting transfers between devices, per_device(): piece = lax.ppermute(piece, AXES, opposite_pairs(sections, dps, dps // 2))  23.5 us
    all_to_all x1, blocking collectives, per_device(): lax.all_to_all(rows, 'section', split_axis=0, concat_axis=0, axis_index_g...  17.3 us
    dot_general x1, matrix products, per_device(): part = jnp.dot(hidden, fc2_weight, preferred_element_type=f32)  7.04 us
    pallas_call x1, Pallas kernels, add_away(): pl.pallas_call(away_kernel, out_shape=jax.ShapeDtypeStruct((count, width)...  6.91 us
    ppermute x1, waiting for transfers between devices, per_device(): piece = lax.ppermute(piece, AXES, opposite_pairs(sections, dps, dps // 2))  4.48 us
    unnamed x21, local copies, waits for them, and re-layouts  4.28 us
  transfers between devices with their start and end apart: 14, of which 9 were waited for; matrix products, arithmetic and copies ran while one was open for 6% of the time, Pallas kernels for 0%

profile of v8, /device:TPU:1, one launch (start us, length us, event | category | flops | bytes accessed | tf_op | source)
XLA Modules:
  0.0 197.9 jit_solution(17788229343095804547)
XLA Ops:
  6.5 0.0 all-gather.2.cloned.1.call-start
  6.5 0.0 copy-start.1
  6.5 0.0 copy-start.2
  6.6 3.5 %fusion = bf16[40,3200]{1,0:T(8,128)(2,1)S(1)} fusion(bf16[3200,640]{1,0:T(8,128)(2,1)} %param.15, bf16[640,3200]{1,0:T(8,128)(2,1)} %param.17, s32[]{:T(128)S(6)} %select_n.12, pred[]{:T(512)S(6)} %lt.6, s32[40]{0:T(128)S(1)} %iota_add_fusion), kind=kOutput, calls=%fused_computation.1 | convolution fusion | flops 164121600 | bytes 4608165 | tf_op jit(solution)/shard_map/dot_general | solution.py:150
  10.1 23.5 %collective-permute-start.7 = (bf16[40,3200]{1,0:T(8,128)(2,1)S(1)}, bf16[40,3200]{1,0:T(8,128)(2,1)S(1)}, u32[]{:S(2)}, u32[]{:S(2)}) collective-permute-start(bf16[40,3200]{1,0:T(8,128)(2,1)S(1)} %fusion), channel_id=1, source_target_pairs={{0,8},{1,9},{2,10},{3,11},{4,12},{5,13},{6,14},{7,15},{8,32},{9,33... | collective-permute-start | bytes 768008 | tf_op jit(solution)/shard_map/ppermute | solution.py:157
  33.6 0.0 copy-done.1
  33.7 0.0 copy-done
  33.7 0.0 copy-done.2
  33.7 0.3 shard_map.91
  34.0 0.0 copy-start.7
  34.1 17.7 %conditional.1 = (bf16[64,3200]{1,0:T(8,128)(2,1)S(1)}) conditional(s32[]{:T(128)} %bitcast.2, () %tuple.16, bf16[64,3200]{1,0:T(8,128)(2,1)S(1)} %get-tuple-element.20), branch_computations={%region_0.1_spmd, %region_1.2_spmd} | conditional | bytes 2457608 | solution.py:158
  34.1 0.2 all_to_all.2
  34.2 17.3 %all_to_all.9 = bf16[32,2,3200]{2,1,0:T(2,128)(2,1)S(1)} all-to-all(bf16[32,2,3200]{2,1,0:T(2,128)(2,1)S(1)} %all_to_all.2), channel_id=1, replica_groups={{0,16,64,80,128,144,192,208,256,272,320,336,384,400,448,464,512,528,576..., dimensions={0} | all-to-all | bytes 819200 | tf_op jit(solution)/shard_map/cond/branch_1_fun/all_to_all | solution.py:160
  51.6 0.2 all_to_all.7
  51.7 0.0 copy-start.4
  51.7 4.5 %collective-permute-done.7 = bf16[40,3200]{1,0:T(8,128)(2,1)S(1)} collective-permute-done((bf16[40,3200]{1,0:T(8,128)(2,1)S(1)}, bf16[40,3200]{1,0:T(8,128)(2,1)S(1)}, u32[]{:S(2)}, u32[]{:S(2)}) %collective-permute-start.7) | collective-permute-done | bytes 256032 | tf_op jit(solution)/shard_map/ppermute | solution.py:157
  56.2 0.7 copy-done.3
  56.9 0.0 all-gather.2.cloned.1.call-update
  57.0 0.2 convolution_convert_fusion.1
  57.1 18.8 %collective-permute-start = (bf16[24,3200]{1,0:T(8,128)(2,1)S(1)}, bf16[24,3200]{1,0:T(8,128)(2,1)S(1)}, u32[]{:S(2)}, u32[]{:S(2)}) collective-permute-start(bf16[24,3200]{1,0:T(8,128)(2,1)S(1)} %convolution_convert_fusion.1), channel_id=1, source_target_pairs={{0,32},{1,33},{2,34},{3,35},{4,36},{5,37},{6,38},{7,39},{8,40},{9,... | collective-permute-start | bytes 460808 | tf_op jit(solution)/shard_map/ppermute | solution.py:141
  75.9 0.0 copy-done.7
  76.0 5.8 %collective-permute-start.1 = (f32[640]{0:T(1024)S(1)}, f32[640]{0:T(1024)S(1)}, u32[]{:S(2)}, u32[]{:S(2)}) collective-permute-start(f32[640]{0:T(1024)S(1)} %copy-done.7), channel_id=1, source_target_pairs={{0,8},{1,9},{2,10},{3,11},{4,12},{5,13},{6,14},{7,15},{8,32},{9,33... | collective-permute-start | bytes 7688 | tf_op jit(solution)/shard_map/ppermute | solution.py:141
  81.8 0.2 convolution_convert_fusion.2
  82.0 13.6 %collective-permute-done.1 = f32[640]{0:T(1024)S(1)} collective-permute-done((f32[640]{0:T(1024)S(1)}, f32[640]{0:T(1024)S(1)}, u32[]{:S(2)}, u32[]{:S(2)}) %collective-permute-start.1) | collective-permute-done | bytes 2592 | tf_op jit(solution)/shard_map/ppermute | solution.py:141
  95.6 3.0 %collective-permute-done = bf16[24,3200]{1,0:T(8,128)(2,1)S(1)} collective-permute-done((bf16[24,3200]{1,0:T(8,128)(2,1)S(1)}, bf16[24,3200]{1,0:T(8,128)(2,1)S(1)}, u32[]{:S(2)}, u32[]{:S(2)}) %collective-permute-start) | collective-permute-done | bytes 153632 | tf_op jit(solution)/shard_map/ppermute | solution.py:141
  98.6 0.2 convert_reduce_fusion
  98.8 0.2 fusion.14
  99.0 0.0 copy-done.4
  99.0 0.1 fusion.16
  99.1 1.9 collective-permute-start.5
  101.0 4.6 %collective-permute-start.2 = (bf16[24,3200]{1,0:T(8,128)(2,1)S(1)}, bf16[24,3200]{1,0:T(8,128)(2,1)S(1)}, u32[]{:S(2)}, u32[]{:S(2)}) collective-permute-start(bf16[24,3200]{1,0:T(8,128)(2,1)S(1)} %fusion.16), channel_id=1, source_target_pairs={{0,2},{1,3},{2,4},{3,5},{4,6},{5,7},{6,8},{7,9},{8,10},{9,11},{10,... | collective-permute-start | bytes 460808 | tf_op jit(solution)/shard_map/ppermute | solution.py:141
  105.6 5.6 %collective-permute-done.5 = bf16[24,3200]{1,0:T(8,128)(2,1)S(1)} collective-permute-done((bf16[24,3200]{1,0:T(8,128)(2,1)S(1)}, bf16[24,3200]{1,0:T(8,128)(2,1)S(1)}, u32[]{:S(2)}, u32[]{:S(2)}) %collective-permute-start.5) | collective-permute-done | bytes 153632 | tf_op jit(solution)/shard_map/ppermute | solution.py:141
  111.2 1.0 collective-permute-done.2
  112.3 3.4 %collective-permute-start.3 = (bf16[48,3200]{1,0:T(8,128)(2,1)S(1)}, bf16[48,3200]{1,0:T(8,128)(2,1)S(1)}, u32[]{:S(2)}, u32[]{:S(2)}) collective-permute-start(bf16[48,3200]{1,0:T(8,128)(2,1)S(1)} %get-tuple-element.34), channel_id=1, source_target_pairs={{0,1},{1,2},{2,3},{3,4},{4,5},{5,6},{6,7},{7,8},{8,9},{9,10},{10,1... | collective-permute-start | bytes 921608 | tf_op jit(solution)/shard_map/ppermute | solution.py:141
  115.7 3.1 %collective-permute-start.6 = (bf16[48,3200]{1,0:T(8,128)(2,1)S(1)}, bf16[48,3200]{1,0:T(8,128)(2,1)S(1)}, u32[]{:S(2)}, u32[]{:S(2)}) collective-permute-start(bf16[48,3200]{1,0:T(8,128)(2,1)S(1)} %get-tuple-element.33), channel_id=1, source_target_pairs={{0,47},{1,0},{2,1},{3,2},{4,3},{5,4},{6,5},{7,6},{8,7},{9,8},{10,9... | collective-permute-start | bytes 921608 | tf_op jit(solution)/shard_map/ppermute | solution.py:141
  118.8 3.9 %collective-permute-start.4 = (bf16[24,3200]{1,0:T(8,128)(2,1)S(1)}, bf16[24,3200]{1,0:T(8,128)(2,1)S(1)}, u32[]{:S(2)}, u32[]{:S(2)}) collective-permute-start(bf16[24,3200]{1,0:T(8,128)(2,1)S(1)} %collective-permute-done.2), channel_id=1, source_target_pairs={{0,2},{1,3},{2,4},{3,5},{4,6},{5,7},{6,8},{7,9},{8,10},{9,11},{10,... | collective-permute-start | bytes 460808 | tf_op jit(solution)/shard_map/ppermute | solution.py:141
  122.8 0.0 collective-permute-done.3
  122.8 0.8 constant_dynamic-update-slice_fusion.5
  123.5 0.7 constant_dynamic-update-slice_fusion.4
  124.2 13.3 %collective-permute-done.4 = bf16[24,3200]{1,0:T(8,128)(2,1)S(1)} collective-permute-done((bf16[24,3200]{1,0:T(8,128)(2,1)S(1)}, bf16[24,3200]{1,0:T(8,128)(2,1)S(1)}, u32[]{:S(2)}, u32[]{:S(2)}) %collective-permute-start.4) | collective-permute-done | bytes 153632 | tf_op jit(solution)/shard_map/ppermute | solution.py:141
  137.5 0.7 constant_dynamic-update-slice_fusion.3
  138.2 0.0 collective-permute-done.6
  138.2 0.8 constant_dynamic-update-slice_fusion.2
  138.9 0.7 constant_dynamic-update-slice_fusion.1
  139.6 0.8 constant_dynamic-update-slice_fusion.rows_ref
  140.4 7.0 %fusion.11.part_ref = f32[192,3200]{1,0:T(8,128)S(1)} fusion(bf16[640,3200]{1,0:T(8,128)(2,1)} %param.17, bf16[192,3200]{1,0:T(8,128)(2,1)} %constant_dynamic-update-slice_fusion.rows_ref, bf16[3200,640]{1,0:T(8,128)(2,1)} %param.15, f32[640]{0:T(1024)S(1)} %copy-done.7), kind=kOutput, calls=%fused_computation.24 | convolution fusion | flops 1580974080 | bytes 11880960 | tf_op jit(solution)/shard_map/dot_general | solution.py:188
  147.4 0.0 all-gather.2.cloned.1.call-done.fetched_ref
  147.4 6.9 %shard_map.92 = bf16[192,3200]{1,0:T(8,128)(2,1)S(1)} custom-call(bf16[192,3200]{1,0:T(8,128)(2,1)} %constant_dynamic-update-slice_fusion.rows_ref, f32[192,3200]{1,0:T(8,128)S(1)} %fusion.11.part_ref, f32[1,640]{1,0:T(1,128)S(1)} %broadcast_in_dim.7.bias_ref, bf16[1280,3200]{1,0:T(8,128)(2,1)} %all-gather.2.cloned.1.call-done.fetched_ref), custom_call_target="tpu_custom_call" | custom-call | tf_op jit(solution)/shard_map/pallas_call | solution.py:110
  154.4 0.0 copy-start.5
  154.4 0.0 copy-start.6
  154.4 3.1 %collective-permute-start.8 = (bf16[48,3200]{1,0:T(8,128)(2,1)S(1)}, bf16[48,3200]{1,0:T(8,128)(2,1)S(1)}, u32[]{:S(2)}, u32[]{:S(2)}) collective-permute-start(bf16[48,3200]{1,0:T(8,128)(2,1)S(1)} %get-tuple-element.31), channel_id=1, source_target_pairs={{0,47},{1,0},{2,1},{3,2},{4,3},{5,4},{6,5},{7,6},{8,7},{9,8},{10,9... | collective-permute-start | bytes 921608 | tf_op jit(solution)/shard_map/ppermute | solution.py:141
  157.5 2.2 %collective-permute-start.11 = (bf16[48,3200]{1,0:T(8,128)(2,1)S(1)}, bf16[48,3200]{1,0:T(8,128)(2,1)S(1)}, u32[]{:S(2)}, u32[]{:S(2)}) collective-permute-start(bf16[48,3200]{1,0:T(8,128)(2,1)S(1)} %get-tuple-element.32), channel_id=1, source_target_pairs={{0,1},{1,2},{2,3},{3,4},{4,5},{5,6},{6,7},{7,8},{8,9},{9,10},{10,1... | collective-permute-start | bytes 921608 | tf_op jit(solution)/shard_map/ppermute | solution.py:141
  159.8 3.9 %collective-permute-start.9 = (bf16[24,3200]{1,0:T(8,128)(2,1)S(1)}, bf16[24,3200]{1,0:T(8,128)(2,1)S(1)}, u32[]{:S(2)}, u32[]{:S(2)}) collective-permute-start(bf16[24,3200]{1,0:T(8,128)(2,1)S(1)} %slice.47), channel_id=1, source_target_pairs={{0,46},{1,47},{2,0},{3,1},{4,2},{5,3},{6,4},{7,5},{8,6},{9,7},{10,... | collective-permute-start | bytes 460808 | tf_op jit(solution)/shard_map/ppermute | solution.py:141
  163.6 5.3 %collective-permute-done.9 = bf16[24,3200]{1,0:T(8,128)(2,1)S(1)} collective-permute-done((bf16[24,3200]{1,0:T(8,128)(2,1)S(1)}, bf16[24,3200]{1,0:T(8,128)(2,1)S(1)}, u32[]{:S(2)}, u32[]{:S(2)}) %collective-permute-start.9) | collective-permute-done | bytes 153632 | tf_op jit(solution)/shard_map/ppermute | solution.py:141
  168.9 0.0 collective-permute-done.8
  168.9 0.0 collective-permute-done.11
  168.9 0.1 add_convert_fusion.1
  169.0 9.2 %collective-permute-start.10 = (bf16[24,3200]{1,0:T(8,128)(2,1)S(1)}, bf16[24,3200]{1,0:T(8,128)(2,1)S(1)}, u32[]{:S(2)}, u32[]{:S(2)}) collective-permute-start(bf16[24,3200]{1,0:T(8,128)(2,1)S(1)} %get-tuple-element.29), channel_id=1, source_target_pairs={{0,46},{1,47},{2,0},{3,1},{4,2},{5,3},{6,4},{7,5},{8,6},{9,7},{10,... | collective-permute-start | bytes 460808 | tf_op jit(solution)/shard_map/ppermute | solution.py:141
  178.2 1.9 collective-permute-start.12
  180.2 3.4 %collective-permute-done.10 = bf16[24,3200]{1,0:T(8,128)(2,1)S(1)} collective-permute-done((bf16[24,3200]{1,0:T(8,128)(2,1)S(1)}, bf16[24,3200]{1,0:T(8,128)(2,1)S(1)}, u32[]{:S(2)}, u32[]{:S(2)}) %collective-permute-start.10) | collective-permute-done | bytes 153632 | tf_op jit(solution)/shard_map/ppermute | solution.py:141
  183.6 6.6 %collective-permute-done.12 = bf16[24,3200]{1,0:T(8,128)(2,1)S(1)} collective-permute-done((bf16[24,3200]{1,0:T(8,128)(2,1)S(1)}, bf16[24,3200]{1,0:T(8,128)(2,1)S(1)}, u32[]{:S(2)}, u32[]{:S(2)}) %collective-permute-start.12) | collective-permute-done | bytes 153632 | tf_op jit(solution)/shard_map/ppermute | solution.py:141
  190.2 0.0 copy-done.5
  190.2 0.0 copy-done.6
  190.2 0.8 fusion.49
  (9 shorter events, 0.1 us)
Async XLA Ops:
  6.5 140.9 %all-gather.2.cloned.1.call-start = ((), (), s32[]{:S(2)}) async-start(), calls=%async_computation.1 | async-start | bytes 8448000 | tf_op jit(solution)/shard_map/all_gather | solution.py:167
  6.5 27.1 %copy-start.1 = (s32[1,64]{1,0:T(1,128)S(1)}, s32[1,64]{1,0:T(1,128)}, u32[]{:S(2)}) copy-start(s32[1,64]{1,0:T(1,128)} %live_ref) | copy-start | bytes 772
  6.5 27.1 %copy-start = (bf16[1,64,3200]{2,1,0:T(8,128)(2,1)S(1)}, bf16[1,64,3200]{2,1,0:T(8,128)(2,1)}, u32[]{:S(2)}) copy-start(bf16[1,64,3200]{2,1,0:T(8,128)(2,1)} %param.11) | copy-start | bytes 1228804
  6.5 27.1 %copy-start.2 = (s32[1,64]{1,0:T(1,128)S(1)}, s32[1,64]{1,0:T(1,128)}, u32[]{:S(2)}) copy-start(s32[1,64]{1,0:T(1,128)} %order_ref.1) | copy-start | bytes 772
  10.1 46.2 %collective-permute-start.7 = (bf16[40,3200]{1,0:T(8,128)(2,1)S(1)}, bf16[40,3200]{1,0:T(8,128)(2,1)S(1)}, u32[]{:S(2)}, u32[]{:S(2)}) collective-permute-start(bf16[40,3200]{1,0:T(8,128)(2,1)S(1)} %fusion), channel_id=1, source_target_pairs={{0,8},{1,9},{2,10},{3,11},{4,12},{5,13},{6,14},{7,15},{8,32},{9,33... | collective-permute-start | bytes 768008 | tf_op jit(solution)/shard_map/ppermute | solution.py:157
  34.0 41.9 %copy-start.7 = (f32[640]{0:T(1024)S(1)}, f32[640]{0:T(1024)}, u32[]{:S(2)}) copy-start(f32[640]{0:T(1024)} %param.16) | copy-start | bytes 7684
  51.7 47.3 %copy-start.4 = (f32[3200]{0:T(1024)S(1)}, f32[3200]{0:T(1024)}, u32[]{:S(2)}) copy-start(f32[3200]{0:T(1024)} %param.14) | copy-start | bytes 38404
  56.2 0.7 copy-start.3
  57.1 41.4 %collective-permute-start = (bf16[24,3200]{1,0:T(8,128)(2,1)S(1)}, bf16[24,3200]{1,0:T(8,128)(2,1)S(1)}, u32[]{:S(2)}, u32[]{:S(2)}) collective-permute-start(bf16[24,3200]{1,0:T(8,128)(2,1)S(1)} %convolution_convert_fusion.1), channel_id=1, source_target_pairs={{0,32},{1,33},{2,34},{3,35},{4,36},{5,37},{6,38},{7,39},{8,40},{9,... | collective-permute-start | bytes 460808 | tf_op jit(solution)/shard_map/ppermute | solution.py:141
  76.0 19.6 %collective-permute-start.1 = (f32[640]{0:T(1024)S(1)}, f32[640]{0:T(1024)S(1)}, u32[]{:S(2)}, u32[]{:S(2)}) collective-permute-start(f32[640]{0:T(1024)S(1)} %copy-done.7), channel_id=1, source_target_pairs={{0,8},{1,9},{2,10},{3,11},{4,12},{5,13},{6,14},{7,15},{8,32},{9,33... | collective-permute-start | bytes 7688 | tf_op jit(solution)/shard_map/ppermute | solution.py:141
  99.1 12.1 %collective-permute-start.5 = (bf16[24,3200]{1,0:T(8,128)(2,1)S(1)}, bf16[24,3200]{1,0:T(8,128)(2,1)S(1)}, u32[]{:S(2)}, u32[]{:S(2)}) collective-permute-start(bf16[24,3200]{1,0:T(8,128)(2,1)S(1)} %fusion.16), channel_id=1, source_target_pairs={{0,46},{1,47},{2,0},{3,1},{4,2},{5,3},{6,4},{7,5},{8,6},{9,7},{10,... | collective-permute-start | bytes 460808 | tf_op jit(solution)/shard_map/ppermute | solution.py:141
  101.0 11.2 %collective-permute-start.2 = (bf16[24,3200]{1,0:T(8,128)(2,1)S(1)}, bf16[24,3200]{1,0:T(8,128)(2,1)S(1)}, u32[]{:S(2)}, u32[]{:S(2)}) collective-permute-start(bf16[24,3200]{1,0:T(8,128)(2,1)S(1)} %fusion.16), channel_id=1, source_target_pairs={{0,2},{1,3},{2,4},{3,5},{4,6},{5,7},{6,8},{7,9},{8,10},{9,11},{10,... | collective-permute-start | bytes 460808 | tf_op jit(solution)/shard_map/ppermute | solution.py:141
  112.3 10.5 %collective-permute-start.3 = (bf16[48,3200]{1,0:T(8,128)(2,1)S(1)}, bf16[48,3200]{1,0:T(8,128)(2,1)S(1)}, u32[]{:S(2)}, u32[]{:S(2)}) collective-permute-start(bf16[48,3200]{1,0:T(8,128)(2,1)S(1)} %get-tuple-element.34), channel_id=1, source_target_pairs={{0,1},{1,2},{2,3},{3,4},{4,5},{5,6},{6,7},{7,8},{8,9},{9,10},{10,1... | collective-permute-start | bytes 921608 | tf_op jit(solution)/shard_map/ppermute | solution.py:141
  115.7 22.4 %collective-permute-start.6 = (bf16[48,3200]{1,0:T(8,128)(2,1)S(1)}, bf16[48,3200]{1,0:T(8,128)(2,1)S(1)}, u32[]{:S(2)}, u32[]{:S(2)}) collective-permute-start(bf16[48,3200]{1,0:T(8,128)(2,1)S(1)} %get-tuple-element.33), channel_id=1, source_target_pairs={{0,47},{1,0},{2,1},{3,2},{4,3},{5,4},{6,5},{7,6},{8,7},{9,8},{10,9... | collective-permute-start | bytes 921608 | tf_op jit(solution)/shard_map/ppermute | solution.py:141
  118.8 18.7 %collective-permute-start.4 = (bf16[24,3200]{1,0:T(8,128)(2,1)S(1)}, bf16[24,3200]{1,0:T(8,128)(2,1)S(1)}, u32[]{:S(2)}, u32[]{:S(2)}) collective-permute-start(bf16[24,3200]{1,0:T(8,128)(2,1)S(1)} %collective-permute-done.2), channel_id=1, source_target_pairs={{0,2},{1,3},{2,4},{3,5},{4,6},{5,7},{6,8},{7,9},{8,10},{9,11},{10,... | collective-permute-start | bytes 460808 | tf_op jit(solution)/shard_map/ppermute | solution.py:141
  154.4 35.8 %copy-start.5 = (f32[3200]{0:T(1024)S(1)}, f32[3200]{0:T(1024)}, u32[]{:S(2)}) copy-start(f32[3200]{0:T(1024)} %param.18) | copy-start | bytes 38404
  154.4 35.8 %copy-start.6 = (f32[3200]{0:T(1024)S(1)}, f32[3200]{0:T(1024)}, u32[]{:S(2)}) copy-start(f32[3200]{0:T(1024)} %param.19) | copy-start | bytes 38404
  154.4 14.5 %collective-permute-start.8 = (bf16[48,3200]{1,0:T(8,128)(2,1)S(1)}, bf16[48,3200]{1,0:T(8,128)(2,1)S(1)}, u32[]{:S(2)}, u32[]{:S(2)}) collective-permute-start(bf16[48,3200]{1,0:T(8,128)(2,1)S(1)} %get-tuple-element.31), channel_id=1, source_target_pairs={{0,47},{1,0},{2,1},{3,2},{4,3},{5,4},{6,5},{7,6},{8,7},{9,8},{10,9... | collective-permute-start | bytes 921608 | tf_op jit(solution)/shard_map/ppermute | solution.py:141
  157.5 11.4 %collective-permute-start.11 = (bf16[48,3200]{1,0:T(8,128)(2,1)S(1)}, bf16[48,3200]{1,0:T(8,128)(2,1)S(1)}, u32[]{:S(2)}, u32[]{:S(2)}) collective-permute-start(bf16[48,3200]{1,0:T(8,128)(2,1)S(1)} %get-tuple-element.32), channel_id=1, source_target_pairs={{0,1},{1,2},{2,3},{3,4},{4,5},{5,6},{6,7},{7,8},{8,9},{9,10},{10,1... | collective-permute-start | bytes 921608 | tf_op jit(solution)/shard_map/ppermute | solution.py:141
  159.8 9.2 %collective-permute-start.9 = (bf16[24,3200]{1,0:T(8,128)(2,1)S(1)}, bf16[24,3200]{1,0:T(8,128)(2,1)S(1)}, u32[]{:S(2)}, u32[]{:S(2)}) collective-permute-start(bf16[24,3200]{1,0:T(8,128)(2,1)S(1)} %slice.47), channel_id=1, source_target_pairs={{0,46},{1,47},{2,0},{3,1},{4,2},{5,3},{6,4},{7,5},{8,6},{9,7},{10,... | collective-permute-start | bytes 460808 | tf_op jit(solution)/shard_map/ppermute | solution.py:141
  169.0 14.6 %collective-permute-start.10 = (bf16[24,3200]{1,0:T(8,128)(2,1)S(1)}, bf16[24,3200]{1,0:T(8,128)(2,1)S(1)}, u32[]{:S(2)}, u32[]{:S(2)}) collective-permute-start(bf16[24,3200]{1,0:T(8,128)(2,1)S(1)} %get-tuple-element.29), channel_id=1, source_target_pairs={{0,46},{1,47},{2,0},{3,1},{4,2},{5,3},{6,4},{7,5},{8,6},{9,7},{10,... | collective-permute-start | bytes 460808 | tf_op jit(solution)/shard_map/ppermute | solution.py:141
  178.2 12.0 %collective-permute-start.12 = (bf16[24,3200]{1,0:T(8,128)(2,1)S(1)}, bf16[24,3200]{1,0:T(8,128)(2,1)S(1)}, u32[]{:S(2)}, u32[]{:S(2)}) collective-permute-start(bf16[24,3200]{1,0:T(8,128)(2,1)S(1)} %get-tuple-element.30), channel_id=1, source_target_pairs={{0,2},{1,3},{2,4},{3,5},{4,6},{5,7},{6,8},{7,9},{8,10},{9,11},{10,... | collective-permute-start | bytes 460808 | tf_op jit(solution)/shard_map/ppermute | solution.py:141
Sparse Core Ops, SparseCore 0:
  57.1 86.2 all-gather.1

commit v9 on v8

--- a/solution.py
+++ b/solution.py
@@ -83,15 +83,70 @@
     )(mine[None], live, order, patches)
 
 
+def piece_kernel(mine_ref, fc1_ref, fc2_ref, out_ref, window, rows, sem):
+    depth = out_ref.shape[0]
+    units = fc1_ref.shape[1]
+    mine = mine_ref[0]
+    member = (mine >> 2) * 2 + (mine & 1)
+    pieces = units // depth
+    first = (member & (pieces - 1)) * depth
+
+    def cut(source, held, start):
+        copy = pltpu.make_async_copy(source, held, sem)
+        copy.start()
+        copy.wait()
+        shape = (depth, held.shape[1] if held is window else held.shape[0])
+        unit = first - start + lax.broadcasted_iota(jnp.int32, shape, 0)
+        chosen = unit == lax.broadcasted_iota(jnp.int32, shape, 1)
+        return jnp.where(chosen, 1.0, 0.0).astype(jnp.bfloat16)
+
+    @pl.when(member < pieces)
+    def _():
+        start = pl.multiple_of(jnp.minimum((first >> 7) << 7, units - window.shape[1]), 128)
+        chosen = cut(fc1_ref.at[:, pl.ds(start, window.shape[1])], window, start)
+        out_ref[...] = lax.dot_general(
+            chosen, window[...], (((1,), (1,)), ((), ())), preferred_element_type=jnp.float32
+        ).astype(jnp.bfloat16)
+
+    @pl.when(member >= pieces)
+    def _():
+        start = pl.multiple_of(jnp.minimum((first >> 4) << 4, units - rows.shape[0]), 16)
+        chosen = cut(fc2_ref.at[pl.ds(start, rows.shape[0])], rows, start)
+        out_ref[...] = jnp.dot(
+            chosen, rows[...], preferred_element_type=jnp.float32
+        ).astype(jnp.bfloat16)
+
+
+def cut_piece(mine, fc1_weight, fc2_weight, depth):
+    units, width = fc2_weight.shape
+    anywhere = pl.BlockSpec(memory_space=pl.ANY)
+    return pl.pallas_call(
+        piece_kernel,
+        out_shape=jax.ShapeDtypeStruct((depth, width), jnp.bfloat16),
+        in_specs=[pl.BlockSpec(memory_space=pltpu.SMEM), anywhere, anywhere],
+        out_specs=pl.BlockSpec(memory_space=pltpu.VMEM),
+        scratch_shapes=[
+            pltpu.VMEM((width, 256), jnp.bfloat16),
+            pltpu.VMEM((64, width), jnp.bfloat16),
+            pltpu.SemaphoreType.DMA,
+        ],
+        compiler_params=pltpu.CompilerParams(vmem_limit_bytes=50 * 1024 * 1024),
+    )(mine[None], fc1_weight, fc2_weight)
+
+
 def away_kernel(rows_ref, part_ref, bias_ref, fetched_ref, out_ref, w1, w2, hidden, sems):
     units, width = w1.shape
-    first = pltpu.make_async_copy(fetched_ref.at[pl.ds(0, units)], w1, sems.at[0])
-    second = pltpu.make_async_copy(fetched_ref.at[pl.ds(units, units)], w2, sems.at[1])
-    first.start()
-    second.start()
-    first.wait()
-    for at in range(0, units, 256):
-        span = pl.ds(at, min(256, units - at))
+    spans = [(at, min(256, units - at)) for at in range(0, units, 256)]
+    copies = [
+        pltpu.make_async_copy(fetched_ref.at[pl.ds(at, size)], w1.at[pl.ds(at, size)], sems.at[i])
+        for i, (at, size) in enumerate(spans)
+    ]
+    second = pltpu.make_async_copy(fetched_ref.at[pl.ds(units, units)], w2, sems.at[len(spans)])
+    for copy in copies + [second]:
+        copy.start()
+    for copy, (at, size) in zip(copies, spans):
+        copy.wait()
+        span = pl.ds(at, size)
         pre = lax.dot_general(
             rows_ref[...], w1[span], (((1,), (1,)), ((), ())), preferred_element_type=jnp.float32
         ) + bias_ref[:, span]
@@ -116,7 +171,7 @@
             pltpu.VMEM((units, width), jnp.bfloat16),
             pltpu.VMEM((units, width), jnp.bfloat16),
             pltpu.VMEM((count, units), jnp.bfloat16),
-            pltpu.SemaphoreType.DMA((2,)),
+            pltpu.SemaphoreType.DMA((1 + -(-units // 256),)),
         ],
         compiler_params=pltpu.CompilerParams(vmem_limit_bytes=46 * 1024 * 1024),
     )(rows, part, bias[None], fetched)
@@ -142,16 +197,7 @@
 
     pieces = sections // 4
     depth = units // pieces
-    member = (mine >> 2) * 2 + (mine & 1)
-    first = (member & (pieces - 1)) * depth
-    upper = member < pieces
-    chosen = first + lax.broadcasted_iota(jnp.int32, (depth, units), 0)
-    chosen = (chosen == lax.broadcasted_iota(jnp.int32, (depth, units), 1)).astype(jnp.bfloat16)
-    piece1 = lax.dot_general(
-        chosen, fc1_weight, (((1,), (1,)), ((), ())), preferred_element_type=f32
-    ).astype(jnp.bfloat16)
-    piece2 = lax.dynamic_slice_in_dim(fc2_weight, first, depth, axis=0)
-    piece = jnp.where(upper, piece1, piece2)
+    piece = cut_piece(mine, fc1_weight, fc2_weight, depth)
     piece, live = lax.optimization_barrier((piece, live))
     rows, pick_far, pick_near = plan(patches[0], live, rounds, mine, keep)
     piece = lax.ppermute(piece, AXES, opposite_pairs(sections, dps, dps // 2))

time: 198 us -> 195 us (0.985)
  the two profiles are of different devices: /device:TPU:1 before, /device:TPU:12 now
where the time goes in v9:
time: 195 us
  starting transfers between devices  93.6 us (48%)
  waiting for transfers between devices  43.2 us (22%)
  blocking collectives  20.3 us (10%)
  between operations  13.7 us (7%)
  Pallas kernels  9.71 us (5%)
  matrix products  7.5 us (4%)
  local copies, waits for them, and re-layouts  4.64 us (2%)
  other arithmetic  2.26 us (1%)
    ppermute x12, starting transfers between devices, send(): return lax.ppermute(value, AXES, shift_pairs(sections, dps, hops))  77.8 us
    ppermute x12, waiting for transfers between devices, send(): return lax.ppermute(value, AXES, shift_pairs(sections, dps, hops))  43.1 us
    all_to_all x1, blocking collectives, per_device(): lax.all_to_all(rows, 'section', split_axis=0, concat_axis=0, axis_index_g...  20.3 us
    ppermute x1, starting transfers between devices, per_device(): piece = lax.ppermute(piece, AXES, opposite_pairs(sections, dps, dps // 2))  15.7 us
    pallas_call x1, Pallas kernels, add_away(): pl.pallas_call(away_kernel, out_shape=jax.ShapeDtypeStruct((count, width)...  7.26 us
    dot_general x1, matrix products, per_device(): part = jnp.dot(hidden, fc2_weight, preferred_element_type=f32)  7.14 us
    unnamed x21, local copies, waits for them, and re-layouts  4.27 us
  transfers between devices with their start and end apart: 14, of which 8 were waited for; matrix products, arithmetic and copies ran while one was open for 6% of the time, Pallas kernels for 0%

profile of v9, /device:TPU:12, one launch (start us, length us, event | category | flops | bytes accessed | tf_op | source)
XLA Modules:
  0.0 194.9 jit_solution(17705852135319278444)
XLA Ops:
  6.5 0.0 all-gather.2.cloned.1.call-start
  6.5 0.0 copy-start.1
  6.5 2.1 %shard_map.91 = bf16[40,3200]{1,0:T(8,128)(2,1)S(1)} custom-call(s32[1]{0:T(128)} %bitcast.mine_ref, bf16[3200,640]{1,0:T(8,128)(2,1)} %fc1_ref.1, bf16[640,3200]{1,0:T(8,128)(2,1)} %fc2_ref.1), custom_call_target="tpu_custom_call" | custom-call | tf_op jit(solution)/shard_map/pallas_call | solution.py:123
  8.7 15.7 %collective-permute-start.7 = (bf16[40,3200]{1,0:T(8,128)(2,1)S(1)}, bf16[40,3200]{1,0:T(8,128)(2,1)S(1)}, u32[]{:S(2)}, u32[]{:S(2)}) collective-permute-start(bf16[40,3200]{1,0:T(8,128)(2,1)S(1)} %shard_map.91), channel_id=1, source_target_pairs={{0,8},{1,9},{2,10},{3,11},{4,12},{5,13},{6,14},{7,15},{8,32},{9,33... | collective-permute-start | bytes 768008 | tf_op jit(solution)/shard_map/ppermute | solution.py:203
  24.4 0.0 copy-done.1
  24.4 0.0 copy-done
  24.5 0.0 copy-done.2
  24.5 0.3 shard_map.92
  24.8 0.0 copy-start.7
  24.8 20.6 %conditional.1 = (bf16[64,3200]{1,0:T(8,128)(2,1)S(1)}) conditional(s32[]{:T(128)} %bitcast.2, () %tuple.16, bf16[64,3200]{1,0:T(8,128)(2,1)S(1)} %get-tuple-element.20), branch_computations={%region_0.0_spmd, %region_1.0_spmd} | conditional | bytes 2457608 | solution.py:204
  24.8 0.2 all_to_all.2
  25.0 20.3 %all_to_all.9 = bf16[32,2,3200]{2,1,0:T(2,128)(2,1)S(1)} all-to-all(bf16[32,2,3200]{2,1,0:T(2,128)(2,1)S(1)} %all_to_all.2), channel_id=1, replica_groups={{0,16,64,80,128,144,192,208,256,272,320,336,384,400,448,464,512,528,576..., dimensions={0} | all-to-all | bytes 819200 | tf_op jit(solution)/shard_map/cond/branch_1_fun/all_to_all | solution.py:206
  45.3 0.2 all_to_all.7
  45.4 0.0 copy-start.4
  45.5 0.0 collective-permute-done.7
  45.5 0.0 copy-start.3
  45.5 0.7 copy-done.3
  46.2 0.0 all-gather.2.cloned.1.call-update
  46.2 0.2 convolution_convert_fusion
  46.4 27.5 %collective-permute-start = (bf16[24,3200]{1,0:T(8,128)(2,1)S(1)}, bf16[24,3200]{1,0:T(8,128)(2,1)S(1)}, u32[]{:S(2)}, u32[]{:S(2)}) collective-permute-start(bf16[24,3200]{1,0:T(8,128)(2,1)S(1)} %convolution_convert_fusion), channel_id=1, source_target_pairs={{0,32},{1,33},{2,34},{3,35},{4,36},{5,37},{6,38},{7,39},{8,40},{9,... | collective-permute-start | bytes 460808 | tf_op jit(solution)/shard_map/ppermute | solution.py:196
  73.8 0.0 copy-done.7
  73.9 7.0 %collective-permute-start.1 = (f32[640]{0:T(1024)S(1)}, f32[640]{0:T(1024)S(1)}, u32[]{:S(2)}, u32[]{:S(2)}) collective-permute-start(f32[640]{0:T(1024)S(1)} %copy-done.7), channel_id=1, source_target_pairs={{0,8},{1,9},{2,10},{3,11},{4,12},{5,13},{6,14},{7,15},{8,32},{9,33... | collective-permute-start | bytes 7688 | tf_op jit(solution)/shard_map/ppermute | solution.py:196
  80.9 0.2 convolution_convert_fusion.1
  81.1 8.4 %collective-permute-done.1 = f32[640]{0:T(1024)S(1)} collective-permute-done((f32[640]{0:T(1024)S(1)}, f32[640]{0:T(1024)S(1)}, u32[]{:S(2)}, u32[]{:S(2)}) %collective-permute-start.1) | collective-permute-done | bytes 2592 | tf_op jit(solution)/shard_map/ppermute | solution.py:196
  89.4 0.0 collective-permute-done
  89.4 0.2 convert_reduce_fusion
  89.6 0.2 fusion.13
  89.8 0.0 copy-done.4
  89.8 0.1 fusion.15
  90.0 6.3 %collective-permute-start.5 = (bf16[24,3200]{1,0:T(8,128)(2,1)S(1)}, bf16[24,3200]{1,0:T(8,128)(2,1)S(1)}, u32[]{:S(2)}, u32[]{:S(2)}) collective-permute-start(bf16[24,3200]{1,0:T(8,128)(2,1)S(1)} %fusion.15), channel_id=1, source_target_pairs={{0,46},{1,47},{2,0},{3,1},{4,2},{5,3},{6,4},{7,5},{8,6},{9,7},{10,... | collective-permute-start | bytes 460808 | tf_op jit(solution)/shard_map/ppermute | solution.py:196
  96.3 2.0 %collective-permute-start.2 = (bf16[24,3200]{1,0:T(8,128)(2,1)S(1)}, bf16[24,3200]{1,0:T(8,128)(2,1)S(1)}, u32[]{:S(2)}, u32[]{:S(2)}) collective-permute-start(bf16[24,3200]{1,0:T(8,128)(2,1)S(1)} %fusion.15), channel_id=1, source_target_pairs={{0,2},{1,3},{2,4},{3,5},{4,6},{5,7},{6,8},{7,9},{8,10},{9,11},{10,... | collective-permute-start | bytes 460808 | tf_op jit(solution)/shard_map/ppermute | solution.py:196
  98.3 4.5 %collective-permute-done.5 = bf16[24,3200]{1,0:T(8,128)(2,1)S(1)} collective-permute-done((bf16[24,3200]{1,0:T(8,128)(2,1)S(1)}, bf16[24,3200]{1,0:T(8,128)(2,1)S(1)}, u32[]{:S(2)}, u32[]{:S(2)}) %collective-permute-start.5) | collective-permute-done | bytes 153632 | tf_op jit(solution)/shard_map/ppermute | solution.py:196
  102.9 3.8 %collective-permute-done.2 = bf16[24,3200]{1,0:T(8,128)(2,1)S(1)} collective-permute-done((bf16[24,3200]{1,0:T(8,128)(2,1)S(1)}, bf16[24,3200]{1,0:T(8,128)(2,1)S(1)}, u32[]{:S(2)}, u32[]{:S(2)}) %collective-permute-start.2) | collective-permute-done | bytes 153632 | tf_op jit(solution)/shard_map/ppermute | solution.py:196
  106.7 7.6 %collective-permute-start.3 = (bf16[48,3200]{1,0:T(8,128)(2,1)S(1)}, bf16[48,3200]{1,0:T(8,128)(2,1)S(1)}, u32[]{:S(2)}, u32[]{:S(2)}) collective-permute-start(bf16[48,3200]{1,0:T(8,128)(2,1)S(1)} %get-tuple-element.34), channel_id=1, source_target_pairs={{0,1},{1,2},{2,3},{3,4},{4,5},{5,6},{6,7},{7,8},{8,9},{9,10},{10,1... | collective-permute-start | bytes 921608 | tf_op jit(solution)/shard_map/ppermute | solution.py:196
  114.3 2.6 %collective-permute-start.6 = (bf16[48,3200]{1,0:T(8,128)(2,1)S(1)}, bf16[48,3200]{1,0:T(8,128)(2,1)S(1)}, u32[]{:S(2)}, u32[]{:S(2)}) collective-permute-start(bf16[48,3200]{1,0:T(8,128)(2,1)S(1)} %get-tuple-element.33), channel_id=1, source_target_pairs={{0,47},{1,0},{2,1},{3,2},{4,3},{5,4},{6,5},{7,6},{8,7},{9,8},{10,9... | collective-permute-start | bytes 921608 | tf_op jit(solution)/shard_map/ppermute | solution.py:196
  116.9 2.7 %collective-permute-start.4 = (bf16[24,3200]{1,0:T(8,128)(2,1)S(1)}, bf16[24,3200]{1,0:T(8,128)(2,1)S(1)}, u32[]{:S(2)}, u32[]{:S(2)}) collective-permute-start(bf16[24,3200]{1,0:T(8,128)(2,1)S(1)} %collective-permute-done.2), channel_id=1, source_target_pairs={{0,2},{1,3},{2,4},{3,5},{4,6},{5,7},{6,8},{7,9},{8,10},{9,11},{10,... | collective-permute-start | bytes 460808 | tf_op jit(solution)/shard_map/ppermute | solution.py:196
  119.6 0.7 collective-permute-done.3
  120.3 0.8 constant_dynamic-update-slice_fusion.5
  121.0 0.7 constant_dynamic-update-slice_fusion.4
  121.7 9.3 %collective-permute-done.4 = bf16[24,3200]{1,0:T(8,128)(2,1)S(1)} collective-permute-done((bf16[24,3200]{1,0:T(8,128)(2,1)S(1)}, bf16[24,3200]{1,0:T(8,128)(2,1)S(1)}, u32[]{:S(2)}, u32[]{:S(2)}) %collective-permute-start.4) | collective-permute-done | bytes 153632 | tf_op jit(solution)/shard_map/ppermute | solution.py:196
  131.0 0.7 constant_dynamic-update-slice_fusion.3
  131.7 0.0 collective-permute-done.6
  131.7 0.8 constant_dynamic-update-slice_fusion.2
  132.4 0.7 constant_dynamic-update-slice_fusion.1
  133.1 0.8 constant_dynamic-update-slice_fusion.rows_ref
  133.9 7.1 %fusion.10.part_ref = f32[192,3200]{1,0:T(8,128)S(1)} fusion(bf16[640,3200]{1,0:T(8,128)(2,1)} %fc2_ref.1, bf16[192,3200]{1,0:T(8,128)(2,1)} %constant_dynamic-update-slice_fusion.rows_ref, bf16[3200,640]{1,0:T(8,128)(2,1)} %fc1_ref.1, f32[640]{0:T(1024)S(1)} %copy-done.7), kind=kOutput, calls=%fused_computation.22 | convolution fusion | flops 1580974080 | bytes 11880960 | tf_op jit(solution)/shard_map/dot_general | solution.py:234
  141.0 0.0 all-gather.2.cloned.1.call-done.fetched_ref
  141.0 7.3 %shard_map.93 = bf16[192,3200]{1,0:T(8,128)(2,1)S(1)} custom-call(bf16[192,3200]{1,0:T(8,128)(2,1)} %constant_dynamic-update-slice_fusion.rows_ref, f32[192,3200]{1,0:T(8,128)S(1)} %fusion.10.part_ref, f32[1,640]{1,0:T(1,128)S(1)} %broadcast_in_dim.7.bias_ref, bf16[1280,3200]{1,0:T(8,128)(2,1)} %all-gather.2.cloned.1.call-done.fetched_ref), custom_call_target="tpu_custom_call" | custom-call | tf_op jit(solution)/shard_map/pallas_call | solution.py:165
  148.3 0.0 copy-start.5
  148.3 0.0 copy-start.6
  148.4 4.7 %collective-permute-start.8 = (bf16[48,3200]{1,0:T(8,128)(2,1)S(1)}, bf16[48,3200]{1,0:T(8,128)(2,1)S(1)}, u32[]{:S(2)}, u32[]{:S(2)}) collective-permute-start(bf16[48,3200]{1,0:T(8,128)(2,1)S(1)} %get-tuple-element.31), channel_id=1, source_target_pairs={{0,47},{1,0},{2,1},{3,2},{4,3},{5,4},{6,5},{7,6},{8,7},{9,8},{10,9... | collective-permute-start | bytes 921608 | tf_op jit(solution)/shard_map/ppermute | solution.py:196
  153.1 1.9 collective-permute-start.11
  155.1 7.1 %collective-permute-start.9 = (bf16[24,3200]{1,0:T(8,128)(2,1)S(1)}, bf16[24,3200]{1,0:T(8,128)(2,1)S(1)}, u32[]{:S(2)}, u32[]{:S(2)}) collective-permute-start(bf16[24,3200]{1,0:T(8,128)(2,1)S(1)} %slice.47), channel_id=1, source_target_pairs={{0,46},{1,47},{2,0},{3,1},{4,2},{5,3},{6,4},{7,5},{8,6},{9,7},{10,... | collective-permute-start | bytes 460808 | tf_op jit(solution)/shard_map/ppermute | solution.py:196
  162.2 6.0 %collective-permute-done.9 = bf16[24,3200]{1,0:T(8,128)(2,1)S(1)} collective-permute-done((bf16[24,3200]{1,0:T(8,128)(2,1)S(1)}, bf16[24,3200]{1,0:T(8,128)(2,1)S(1)}, u32[]{:S(2)}, u32[]{:S(2)}) %collective-permute-start.9) | collective-permute-done | bytes 153632 | tf_op jit(solution)/shard_map/ppermute | solution.py:196
  168.2 0.0 collective-permute-done.8
  168.2 0.0 collective-permute-done.11
  168.2 0.1 add_convert_fusion.1
  168.3 6.5 %collective-permute-start.10 = (bf16[24,3200]{1,0:T(8,128)(2,1)S(1)}, bf16[24,3200]{1,0:T(8,128)(2,1)S(1)}, u32[]{:S(2)}, u32[]{:S(2)}) collective-permute-start(bf16[24,3200]{1,0:T(8,128)(2,1)S(1)} %get-tuple-element.29), channel_id=1, source_target_pairs={{0,46},{1,47},{2,0},{3,1},{4,2},{5,3},{6,4},{7,5},{8,6},{9,7},{10,... | collective-permute-start | bytes 460808 | tf_op jit(solution)/shard_map/ppermute | solution.py:196
  174.8 1.9 collective-permute-start.12
  176.7 3.8 %collective-permute-done.10 = bf16[24,3200]{1,0:T(8,128)(2,1)S(1)} collective-permute-done((bf16[24,3200]{1,0:T(8,128)(2,1)S(1)}, bf16[24,3200]{1,0:T(8,128)(2,1)S(1)}, u32[]{:S(2)}, u32[]{:S(2)}) %collective-permute-start.10) | collective-permute-done | bytes 153632 | tf_op jit(solution)/shard_map/ppermute | solution.py:196
  180.5 6.7 %collective-permute-done.12 = bf16[24,3200]{1,0:T(8,128)(2,1)S(1)} collective-permute-done((bf16[24,3200]{1,0:T(8,128)(2,1)S(1)}, bf16[24,3200]{1,0:T(8,128)(2,1)S(1)}, u32[]{:S(2)}, u32[]{:S(2)}) %collective-permute-start.12) | collective-permute-done | bytes 153632 | tf_op jit(solution)/shard_map/ppermute | solution.py:196
  187.2 0.0 copy-done.5
  187.2 0.0 copy-done.6
  187.2 0.8 fusion.48
  (8 shorter events, 0.1 us)
Async XLA Ops:
  6.5 134.5 %all-gather.2.cloned.1.call-start = ((), (), s32[]{:S(2)}) async-start(), calls=%async_computation.1 | async-start | bytes 8448000 | tf_op jit(solution)/shard_map/all_gather | solution.py:213
  6.5 17.9 %copy-start.1 = (s32[1,64]{1,0:T(1,128)S(1)}, s32[1,64]{1,0:T(1,128)}, u32[]{:S(2)}) copy-start(s32[1,64]{1,0:T(1,128)} %live_ref) | copy-start | bytes 772
  6.5 17.9 %copy-start = (bf16[1,64,3200]{2,1,0:T(8,128)(2,1)S(1)}, bf16[1,64,3200]{2,1,0:T(8,128)(2,1)}, u32[]{:S(2)}) copy-start(bf16[1,64,3200]{2,1,0:T(8,128)(2,1)} %param.11) | copy-start | bytes 1228804
  6.5 17.9 %copy-start.2 = (s32[1,64]{1,0:T(1,128)S(1)}, s32[1,64]{1,0:T(1,128)}, u32[]{:S(2)}) copy-start(s32[1,64]{1,0:T(1,128)} %order_ref.1) | copy-start | bytes 772
  8.7 36.8 %collective-permute-start.7 = (bf16[40,3200]{1,0:T(8,128)(2,1)S(1)}, bf16[40,3200]{1,0:T(8,128)(2,1)S(1)}, u32[]{:S(2)}, u32[]{:S(2)}) collective-permute-start(bf16[40,3200]{1,0:T(8,128)(2,1)S(1)} %shard_map.91), channel_id=1, source_target_pairs={{0,8},{1,9},{2,10},{3,11},{4,12},{5,13},{6,14},{7,15},{8,32},{9,33... | collective-permute-start | bytes 768008 | tf_op jit(solution)/shard_map/ppermute | solution.py:203
  24.8 49.0 %copy-start.7 = (f32[640]{0:T(1024)S(1)}, f32[640]{0:T(1024)}, u32[]{:S(2)}) copy-start(f32[640]{0:T(1024)} %param.16) | copy-start | bytes 7684
  45.4 44.4 %copy-start.4 = (f32[3200]{0:T(1024)S(1)}, f32[3200]{0:T(1024)}, u32[]{:S(2)}) copy-start(f32[3200]{0:T(1024)} %param.14) | copy-start | bytes 38404
  45.5 0.7 copy-start.3
  46.4 43.1 %collective-permute-start = (bf16[24,3200]{1,0:T(8,128)(2,1)S(1)}, bf16[24,3200]{1,0:T(8,128)(2,1)S(1)}, u32[]{:S(2)}, u32[]{:S(2)}) collective-permute-start(bf16[24,3200]{1,0:T(8,128)(2,1)S(1)} %convolution_convert_fusion), channel_id=1, source_target_pairs={{0,32},{1,33},{2,34},{3,35},{4,36},{5,37},{6,38},{7,39},{8,40},{9,... | collective-permute-start | bytes 460808 | tf_op jit(solution)/shard_map/ppermute | solution.py:196
  73.9 15.6 %collective-permute-start.1 = (f32[640]{0:T(1024)S(1)}, f32[640]{0:T(1024)S(1)}, u32[]{:S(2)}, u32[]{:S(2)}) collective-permute-start(f32[640]{0:T(1024)S(1)} %copy-done.7), channel_id=1, source_target_pairs={{0,8},{1,9},{2,10},{3,11},{4,12},{5,13},{6,14},{7,15},{8,32},{9,33... | collective-permute-start | bytes 7688 | tf_op jit(solution)/shard_map/ppermute | solution.py:196
  90.0 12.9 %collective-permute-start.5 = (bf16[24,3200]{1,0:T(8,128)(2,1)S(1)}, bf16[24,3200]{1,0:T(8,128)(2,1)S(1)}, u32[]{:S(2)}, u32[]{:S(2)}) collective-permute-start(bf16[24,3200]{1,0:T(8,128)(2,1)S(1)} %fusion.15), channel_id=1, source_target_pairs={{0,46},{1,47},{2,0},{3,1},{4,2},{5,3},{6,4},{7,5},{8,6},{9,7},{10,... | collective-permute-start | bytes 460808 | tf_op jit(solution)/shard_map/ppermute | solution.py:196
  96.3 10.3 %collective-permute-start.2 = (bf16[24,3200]{1,0:T(8,128)(2,1)S(1)}, bf16[24,3200]{1,0:T(8,128)(2,1)S(1)}, u32[]{:S(2)}, u32[]{:S(2)}) collective-permute-start(bf16[24,3200]{1,0:T(8,128)(2,1)S(1)} %fusion.15), channel_id=1, source_target_pairs={{0,2},{1,3},{2,4},{3,5},{4,6},{5,7},{6,8},{7,9},{8,10},{9,11},{10,... | collective-permute-start | bytes 460808 | tf_op jit(solution)/shard_map/ppermute | solution.py:196
  106.7 13.6 %collective-permute-start.3 = (bf16[48,3200]{1,0:T(8,128)(2,1)S(1)}, bf16[48,3200]{1,0:T(8,128)(2,1)S(1)}, u32[]{:S(2)}, u32[]{:S(2)}) collective-permute-start(bf16[48,3200]{1,0:T(8,128)(2,1)S(1)} %get-tuple-element.34), channel_id=1, source_target_pairs={{0,1},{1,2},{2,3},{3,4},{4,5},{5,6},{6,7},{7,8},{8,9},{9,10},{10,1... | collective-permute-start | bytes 921608 | tf_op jit(solution)/shard_map/ppermute | solution.py:196
  114.3 17.4 %collective-permute-start.6 = (bf16[48,3200]{1,0:T(8,128)(2,1)S(1)}, bf16[48,3200]{1,0:T(8,128)(2,1)S(1)}, u32[]{:S(2)}, u32[]{:S(2)}) collective-permute-start(bf16[48,3200]{1,0:T(8,128)(2,1)S(1)} %get-tuple-element.33), channel_id=1, source_target_pairs={{0,47},{1,0},{2,1},{3,2},{4,3},{5,4},{6,5},{7,6},{8,7},{9,8},{10,9... | collective-permute-start | bytes 921608 | tf_op jit(solution)/shard_map/ppermute | solution.py:196
  116.9 14.1 %collective-permute-start.4 = (bf16[24,3200]{1,0:T(8,128)(2,1)S(1)}, bf16[24,3200]{1,0:T(8,128)(2,1)S(1)}, u32[]{:S(2)}, u32[]{:S(2)}) collective-permute-start(bf16[24,3200]{1,0:T(8,128)(2,1)S(1)} %collective-permute-done.2), channel_id=1, source_target_pairs={{0,2},{1,3},{2,4},{3,5},{4,6},{5,7},{6,8},{7,9},{8,10},{9,11},{10,... | collective-permute-start | bytes 460808 | tf_op jit(solution)/shard_map/ppermute | solution.py:196
  148.3 38.9 %copy-start.5 = (f32[3200]{0:T(1024)S(1)}, f32[3200]{0:T(1024)}, u32[]{:S(2)}) copy-start(f32[3200]{0:T(1024)} %param.18) | copy-start | bytes 38404
  148.3 38.9 %copy-start.6 = (f32[3200]{0:T(1024)S(1)}, f32[3200]{0:T(1024)}, u32[]{:S(2)}) copy-start(f32[3200]{0:T(1024)} %param.19) | copy-start | bytes 38404
  148.4 19.9 %collective-permute-start.8 = (bf16[48,3200]{1,0:T(8,128)(2,1)S(1)}, bf16[48,3200]{1,0:T(8,128)(2,1)S(1)}, u32[]{:S(2)}, u32[]{:S(2)}) collective-permute-start(bf16[48,3200]{1,0:T(8,128)(2,1)S(1)} %get-tuple-element.31), channel_id=1, source_target_pairs={{0,47},{1,0},{2,1},{3,2},{4,3},{5,4},{6,5},{7,6},{8,7},{9,8},{10,9... | collective-permute-start | bytes 921608 | tf_op jit(solution)/shard_map/ppermute | solution.py:196
  153.1 15.1 %collective-permute-start.11 = (bf16[48,3200]{1,0:T(8,128)(2,1)S(1)}, bf16[48,3200]{1,0:T(8,128)(2,1)S(1)}, u32[]{:S(2)}, u32[]{:S(2)}) collective-permute-start(bf16[48,3200]{1,0:T(8,128)(2,1)S(1)} %get-tuple-element.32), channel_id=1, source_target_pairs={{0,1},{1,2},{2,3},{3,4},{4,5},{5,6},{6,7},{7,8},{8,9},{9,10},{10,1... | collective-permute-start | bytes 921608 | tf_op jit(solution)/shard_map/ppermute | solution.py:196
  155.1 13.1 %collective-permute-start.9 = (bf16[24,3200]{1,0:T(8,128)(2,1)S(1)}, bf16[24,3200]{1,0:T(8,128)(2,1)S(1)}, u32[]{:S(2)}, u32[]{:S(2)}) collective-permute-start(bf16[24,3200]{1,0:T(8,128)(2,1)S(1)} %slice.47), channel_id=1, source_target_pairs={{0,46},{1,47},{2,0},{3,1},{4,2},{5,3},{6,4},{7,5},{8,6},{9,7},{10,... | collective-permute-start | bytes 460808 | tf_op jit(solution)/shard_map/ppermute | solution.py:196
  168.3 12.2 %collective-permute-start.10 = (bf16[24,3200]{1,0:T(8,128)(2,1)S(1)}, bf16[24,3200]{1,0:T(8,128)(2,1)S(1)}, u32[]{:S(2)}, u32[]{:S(2)}) collective-permute-start(bf16[24,3200]{1,0:T(8,128)(2,1)S(1)} %get-tuple-element.29), channel_id=1, source_target_pairs={{0,46},{1,47},{2,0},{3,1},{4,2},{5,3},{6,4},{7,5},{8,6},{9,7},{10,... | collective-permute-start | bytes 460808 | tf_op jit(solution)/shard_map/ppermute | solution.py:196
  174.8 12.4 %collective-permute-start.12 = (bf16[24,3200]{1,0:T(8,128)(2,1)S(1)}, bf16[24,3200]{1,0:T(8,128)(2,1)S(1)}, u32[]{:S(2)}, u32[]{:S(2)}) collective-permute-start(bf16[24,3200]{1,0:T(8,128)(2,1)S(1)} %get-tuple-element.30), channel_id=1, source_target_pairs={{0,2},{1,3},{2,4},{3,5},{4,6},{5,7},{6,8},{7,9},{8,10},{9,11},{10,... | collective-permute-start | bytes 460808 | tf_op jit(solution)/shard_map/ppermute | solution.py:196
Sparse Core Ops, SparseCore 0:
  46.3 92.0 all-gather.1

commit v10 on v9

--- a/solution.py
+++ b/solution.py
@@ -136,26 +136,31 @@
 
 def away_kernel(rows_ref, part_ref, bias_ref, fetched_ref, out_ref, w1, w2, hidden, sems):
     units, width = w1.shape
-    spans = [(at, min(256, units - at)) for at in range(0, units, 256)]
-    copies = [
-        pltpu.make_async_copy(fetched_ref.at[pl.ds(at, size)], w1.at[pl.ds(at, size)], sems.at[i])
-        for i, (at, size) in enumerate(spans)
-    ]
-    second = pltpu.make_async_copy(fetched_ref.at[pl.ds(units, units)], w2, sems.at[len(spans)])
-    for copy in copies + [second]:
-        copy.start()
-    for copy, (at, size) in zip(copies, spans):
-        copy.wait()
-        span = pl.ds(at, size)
-        pre = lax.dot_general(
-            rows_ref[...], w1[span], (((1,), (1,)), ((), ())), preferred_element_type=jnp.float32
-        ) + bias_ref[:, span]
-        hidden[:, span] = (0.5 * pre * (1.0 + lax.erf(pre * np.float32(0.5**0.5)))).astype(jnp.bfloat16)
-    second.wait()
+    parts = []
+    for at in range(0, units, 256):
+        span = pl.ds(at, min(256, units - at))
+        parts.append((span, fetched_ref.at[span], w1.at[span]))
+    firsts = len(parts)
     for at in range(0, width, 640):
         span = pl.ds(at, min(640, width - at))
-        out = jnp.dot(hidden[...], w2[:, span], preferred_element_type=jnp.float32)
-        out_ref[:, span] = (part_ref[:, span] + out).astype(jnp.bfloat16)
+        parts.append((span, fetched_ref.at[pl.ds(units, units), span], w2.at[:, span]))
+    copies = [
+        pltpu.make_async_copy(source, held, sems.at[i]) for i, (_, source, held) in enumerate(parts)
+    ]
+    copies[0].start()
+    copies[1].start()
+    for i, (span, _, _) in enumerate(parts):
+        copies[i].wait()
+        if i + 2 < len(parts):
+            copies[i + 2].start()
+        if i < firsts:
+            pre = lax.dot_general(
+                rows_ref[...], w1[span], (((1,), (1,)), ((), ())), preferred_element_type=jnp.float32
+            ) + bias_ref[:, span]
+            hidden[:, span] = (0.5 * pre * (1.0 + lax.erf(pre * np.float32(0.5**0.5)))).astype(jnp.bfloat16)
+        else:
+            out = jnp.dot(hidden[...], w2[:, span], preferred_element_type=jnp.float32)
+            out_ref[:, span] = (part_ref[:, span] + out).astype(jnp.bfloat16)
 
 
 def add_away(rows, part, bias, fetched):
@@ -171,7 +176,7 @@
             pltpu.VMEM((units, width), jnp.bfloat16),
             pltpu.VMEM((units, width), jnp.bfloat16),
             pltpu.VMEM((count, units), jnp.bfloat16),
-            pltpu.SemaphoreType.DMA((1 + -(-units // 256),)),
+            pltpu.SemaphoreType.DMA((-(-units // 256) - (-width // 640),)),
         ],
         compiler_params=pltpu.CompilerParams(vmem_limit_bytes=46 * 1024 * 1024),
     )(rows, part, bias[None], fetched)

time: 195 us -> 197 us (1.010)
  no operation moved by 1% of the time
where the time goes in v10:
time: 197 us; the launch traced here: 196 us
  starting transfers between devices  93.6 us (48%)
  waiting for transfers between devices  43.2 us (22%)
  blocking collectives  20.3 us (10%)
  between operations  13.7 us (7%)
  Pallas kernels  10.9 us (6%)
  matrix products  7.5 us (4%)
  local copies, waits for them, and re-layouts  4.64 us (2%)
  other arithmetic  2.26 us (1%)
    ppermute x12, starting transfers between devices, send(): return lax.ppermute(value, AXES, shift_pairs(sections, dps, hops))  77.8 us
    ppermute x12, waiting for transfers between devices, send(): return lax.ppermute(value, AXES, shift_pairs(sections, dps, hops))  43.1 us
    all_to_all x1, blocking collectives, per_device(): lax.all_to_all(rows, 'section', split_axis=0, concat_axis=0, axis_index_g...  20.3 us
    ppermute x1, starting transfers between devices, per_device(): piece = lax.ppermute(piece, AXES, opposite_pairs(sections, dps, dps // 2))  15.7 us
    pallas_call x1, Pallas kernels, add_away(): pl.pallas_call(away_kernel, out_shape=jax.ShapeDtypeStruct((count, width)...  8.48 us
    dot_general x1, matrix products, per_device(): part = jnp.dot(hidden, fc2_weight, preferred_element_type=f32)  7.14 us
    unnamed x21, local copies, waits for them, and re-layouts  4.27 us
  transfers between devices with their start and end apart: 14, of which 8 were waited for; matrix products, arithmetic and copies ran while one was open for 6% of the time, Pallas kernels for 0%

profile of v10, /device:TPU:12, one launch (start us, length us, event | category | flops | bytes accessed | tf_op | source)
XLA Modules:
  0.0 196.1 jit_solution(11169321375501435122)
XLA Ops:
  6.5 0.0 all-gather.2.cloned.1.call-start
  6.5 0.0 copy-start.1
  6.5 2.1 %shard_map.91 = bf16[40,3200]{1,0:T(8,128)(2,1)S(1)} custom-call(s32[1]{0:T(128)} %bitcast.mine_ref, bf16[3200,640]{1,0:T(8,128)(2,1)} %fc1_ref.1, bf16[640,3200]{1,0:T(8,128)(2,1)} %fc2_ref.1), custom_call_target="tpu_custom_call" | custom-call | tf_op jit(solution)/shard_map/pallas_call | solution.py:123
  8.7 15.7 %collective-permute-start.7 = (bf16[40,3200]{1,0:T(8,128)(2,1)S(1)}, bf16[40,3200]{1,0:T(8,128)(2,1)S(1)}, u32[]{:S(2)}, u32[]{:S(2)}) collective-permute-start(bf16[40,3200]{1,0:T(8,128)(2,1)S(1)} %shard_map.91), channel_id=1, source_target_pairs={{0,8},{1,9},{2,10},{3,11},{4,12},{5,13},{6,14},{7,15},{8,32},{9,33... | collective-permute-start | bytes 768008 | tf_op jit(solution)/shard_map/ppermute | solution.py:208
  24.4 0.0 copy-done.1
  24.4 0.0 copy-done
  24.5 0.0 copy-done.2
  24.5 0.3 shard_map.92
  24.8 0.0 copy-start.7
  24.8 20.6 %conditional.1 = (bf16[64,3200]{1,0:T(8,128)(2,1)S(1)}) conditional(s32[]{:T(128)} %bitcast.2, () %tuple.16, bf16[64,3200]{1,0:T(8,128)(2,1)S(1)} %get-tuple-element.20), branch_computations={%region_0.0_spmd, %region_1.0_spmd} | conditional | bytes 2457608 | solution.py:209
  24.8 0.2 all_to_all.2
  25.0 20.3 %all_to_all.9 = bf16[32,2,3200]{2,1,0:T(2,128)(2,1)S(1)} all-to-all(bf16[32,2,3200]{2,1,0:T(2,128)(2,1)S(1)} %all_to_all.2), channel_id=1, replica_groups={{0,16,64,80,128,144,192,208,256,272,320,336,384,400,448,464,512,528,576..., dimensions={0} | all-to-all | bytes 819200 | tf_op jit(solution)/shard_map/cond/branch_1_fun/all_to_all | solution.py:211
  45.3 0.2 all_to_all.7
  45.4 0.0 copy-start.4
  45.5 0.0 collective-permute-done.7
  45.5 0.0 copy-start.3
  45.5 0.7 copy-done.3
  46.2 0.0 all-gather.2.cloned.1.call-update
  46.2 0.2 convolution_convert_fusion
  46.4 27.5 %collective-permute-start = (bf16[24,3200]{1,0:T(8,128)(2,1)S(1)}, bf16[24,3200]{1,0:T(8,128)(2,1)S(1)}, u32[]{:S(2)}, u32[]{:S(2)}) collective-permute-start(bf16[24,3200]{1,0:T(8,128)(2,1)S(1)} %convolution_convert_fusion), channel_id=1, source_target_pairs={{0,32},{1,33},{2,34},{3,35},{4,36},{5,37},{6,38},{7,39},{8,40},{9,... | collective-permute-start | bytes 460808 | tf_op jit(solution)/shard_map/ppermute | solution.py:201
  73.8 0.0 copy-done.7
  73.9 7.0 %collective-permute-start.1 = (f32[640]{0:T(1024)S(1)}, f32[640]{0:T(1024)S(1)}, u32[]{:S(2)}, u32[]{:S(2)}) collective-permute-start(f32[640]{0:T(1024)S(1)} %copy-done.7), channel_id=1, source_target_pairs={{0,8},{1,9},{2,10},{3,11},{4,12},{5,13},{6,14},{7,15},{8,32},{9,33... | collective-permute-start | bytes 7688 | tf_op jit(solution)/shard_map/ppermute | solution.py:201
  80.9 0.2 convolution_convert_fusion.1
  81.1 8.4 %collective-permute-done.1 = f32[640]{0:T(1024)S(1)} collective-permute-done((f32[640]{0:T(1024)S(1)}, f32[640]{0:T(1024)S(1)}, u32[]{:S(2)}, u32[]{:S(2)}) %collective-permute-start.1) | collective-permute-done | bytes 2592 | tf_op jit(solution)/shard_map/ppermute | solution.py:201
  89.4 0.0 collective-permute-done
  89.4 0.2 convert_reduce_fusion
  89.6 0.2 fusion.13
  89.8 0.0 copy-done.4
  89.8 0.1 fusion.15
  90.0 6.3 %collective-permute-start.5 = (bf16[24,3200]{1,0:T(8,128)(2,1)S(1)}, bf16[24,3200]{1,0:T(8,128)(2,1)S(1)}, u32[]{:S(2)}, u32[]{:S(2)}) collective-permute-start(bf16[24,3200]{1,0:T(8,128)(2,1)S(1)} %fusion.15), channel_id=1, source_target_pairs={{0,46},{1,47},{2,0},{3,1},{4,2},{5,3},{6,4},{7,5},{8,6},{9,7},{10,... | collective-permute-start | bytes 460808 | tf_op jit(solution)/shard_map/ppermute | solution.py:201
  96.3 2.0 %collective-permute-start.2 = (bf16[24,3200]{1,0:T(8,128)(2,1)S(1)}, bf16[24,3200]{1,0:T(8,128)(2,1)S(1)}, u32[]{:S(2)}, u32[]{:S(2)}) collective-permute-start(bf16[24,3200]{1,0:T(8,128)(2,1)S(1)} %fusion.15), channel_id=1, source_target_pairs={{0,2},{1,3},{2,4},{3,5},{4,6},{5,7},{6,8},{7,9},{8,10},{9,11},{10,... | collective-permute-start | bytes 460808 | tf_op jit(solution)/shard_map/ppermute | solution.py:201
  98.3 4.5 %collective-permute-done.5 = bf16[24,3200]{1,0:T(8,128)(2,1)S(1)} collective-permute-done((bf16[24,3200]{1,0:T(8,128)(2,1)S(1)}, bf16[24,3200]{1,0:T(8,128)(2,1)S(1)}, u32[]{:S(2)}, u32[]{:S(2)}) %collective-permute-start.5) | collective-permute-done | bytes 153632 | tf_op jit(solution)/shard_map/ppermute | solution.py:201
  102.9 3.8 %collective-permute-done.2 = bf16[24,3200]{1,0:T(8,128)(2,1)S(1)} collective-permute-done((bf16[24,3200]{1,0:T(8,128)(2,1)S(1)}, bf16[24,3200]{1,0:T(8,128)(2,1)S(1)}, u32[]{:S(2)}, u32[]{:S(2)}) %collective-permute-start.2) | collective-permute-done | bytes 153632 | tf_op jit(solution)/shard_map/ppermute | solution.py:201
  106.7 7.6 %collective-permute-start.3 = (bf16[48,3200]{1,0:T(8,128)(2,1)S(1)}, bf16[48,3200]{1,0:T(8,128)(2,1)S(1)}, u32[]{:S(2)}, u32[]{:S(2)}) collective-permute-start(bf16[48,3200]{1,0:T(8,128)(2,1)S(1)} %get-tuple-element.34), channel_id=1, source_target_pairs={{0,1},{1,2},{2,3},{3,4},{4,5},{5,6},{6,7},{7,8},{8,9},{9,10},{10,1... | collective-permute-start | bytes 921608 | tf_op jit(solution)/shard_map/ppermute | solution.py:201
  114.3 2.6 %collective-permute-start.6 = (bf16[48,3200]{1,0:T(8,128)(2,1)S(1)}, bf16[48,3200]{1,0:T(8,128)(2,1)S(1)}, u32[]{:S(2)}, u32[]{:S(2)}) collective-permute-start(bf16[48,3200]{1,0:T(8,128)(2,1)S(1)} %get-tuple-element.33), channel_id=1, source_target_pairs={{0,47},{1,0},{2,1},{3,2},{4,3},{5,4},{6,5},{7,6},{8,7},{9,8},{10,9... | collective-permute-start | bytes 921608 | tf_op jit(solution)/shard_map/ppermute | solution.py:201
  116.9 2.7 %collective-permute-start.4 = (bf16[24,3200]{1,0:T(8,128)(2,1)S(1)}, bf16[24,3200]{1,0:T(8,128)(2,1)S(1)}, u32[]{:S(2)}, u32[]{:S(2)}) collective-permute-start(bf16[24,3200]{1,0:T(8,128)(2,1)S(1)} %collective-permute-done.2), channel_id=1, source_target_pairs={{0,2},{1,3},{2,4},{3,5},{4,6},{5,7},{6,8},{7,9},{8,10},{9,11},{10,... | collective-permute-start | bytes 460808 | tf_op jit(solution)/shard_map/ppermute | solution.py:201
  119.6 0.7 collective-permute-done.3
  120.3 0.8 constant_dynamic-update-slice_fusion.5
  121.0 0.7 constant_dynamic-update-slice_fusion.4
  121.7 9.3 %collective-permute-done.4 = bf16[24,3200]{1,0:T(8,128)(2,1)S(1)} collective-permute-done((bf16[24,3200]{1,0:T(8,128)(2,1)S(1)}, bf16[24,3200]{1,0:T(8,128)(2,1)S(1)}, u32[]{:S(2)}, u32[]{:S(2)}) %collective-permute-start.4) | collective-permute-done | bytes 153632 | tf_op jit(solution)/shard_map/ppermute | solution.py:201
  131.0 0.7 constant_dynamic-update-slice_fusion.3
  131.7 0.0 collective-permute-done.6
  131.7 0.8 constant_dynamic-update-slice_fusion.2
  132.4 0.7 constant_dynamic-update-slice_fusion.1
  133.1 0.8 constant_dynamic-update-slice_fusion.rows_ref
  133.9 7.1 %fusion.10.part_ref = f32[192,3200]{1,0:T(8,128)S(1)} fusion(bf16[640,3200]{1,0:T(8,128)(2,1)} %fc2_ref.1, bf16[192,3200]{1,0:T(8,128)(2,1)} %constant_dynamic-update-slice_fusion.rows_ref, bf16[3200,640]{1,0:T(8,128)(2,1)} %fc1_ref.1, f32[640]{0:T(1024)S(1)} %copy-done.7), kind=kOutput, calls=%fused_computation.22 | convolution fusion | flops 1580974080 | bytes 11880960 | tf_op jit(solution)/shard_map/dot_general | solution.py:239
  141.0 0.0 all-gather.2.cloned.1.call-done.fetched_ref
  141.0 8.5 %shard_map.93 = bf16[192,3200]{1,0:T(8,128)(2,1)S(1)} custom-call(bf16[192,3200]{1,0:T(8,128)(2,1)} %constant_dynamic-update-slice_fusion.rows_ref, f32[192,3200]{1,0:T(8,128)S(1)} %fusion.10.part_ref, f32[1,640]{1,0:T(1,128)S(1)} %broadcast_in_dim.7.bias_ref, bf16[1280,3200]{1,0:T(8,128)(2,1)} %all-gather.2.cloned.1.call-done.fetched_ref), custom_call_target="tpu_custom_call" | custom-call | tf_op jit(solution)/shard_map/pallas_call | solution.py:170
  149.5 0.0 copy-start.5
  149.5 0.0 copy-start.6
  149.6 4.7 %collective-permute-start.8 = (bf16[48,3200]{1,0:T(8,128)(2,1)S(1)}, bf16[48,3200]{1,0:T(8,128)(2,1)S(1)}, u32[]{:S(2)}, u32[]{:S(2)}) collective-permute-start(bf16[48,3200]{1,0:T(8,128)(2,1)S(1)} %get-tuple-element.31), channel_id=1, source_target_pairs={{0,47},{1,0},{2,1},{3,2},{4,3},{5,4},{6,5},{7,6},{8,7},{9,8},{10,9... | collective-permute-start | bytes 921608 | tf_op jit(solution)/shard_map/ppermute | solution.py:201
  154.4 1.9 collective-permute-start.11
  156.3 7.1 %collective-permute-start.9 = (bf16[24,3200]{1,0:T(8,128)(2,1)S(1)}, bf16[24,3200]{1,0:T(8,128)(2,1)S(1)}, u32[]{:S(2)}, u32[]{:S(2)}) collective-permute-start(bf16[24,3200]{1,0:T(8,128)(2,1)S(1)} %slice.47), channel_id=1, source_target_pairs={{0,46},{1,47},{2,0},{3,1},{4,2},{5,3},{6,4},{7,5},{8,6},{9,7},{10,... | collective-permute-start | bytes 460808 | tf_op jit(solution)/shard_map/ppermute | solution.py:201
  163.4 6.0 %collective-permute-done.9 = bf16[24,3200]{1,0:T(8,128)(2,1)S(1)} collective-permute-done((bf16[24,3200]{1,0:T(8,128)(2,1)S(1)}, bf16[24,3200]{1,0:T(8,128)(2,1)S(1)}, u32[]{:S(2)}, u32[]{:S(2)}) %collective-permute-start.9) | collective-permute-done | bytes 153632 | tf_op jit(solution)/shard_map/ppermute | solution.py:201
  169.5 0.0 collective-permute-done.8
  169.5 0.0 collective-permute-done.11
  169.5 0.1 add_convert_fusion.1
  169.6 6.5 %collective-permute-start.10 = (bf16[24,3200]{1,0:T(8,128)(2,1)S(1)}, bf16[24,3200]{1,0:T(8,128)(2,1)S(1)}, u32[]{:S(2)}, u32[]{:S(2)}) collective-permute-start(bf16[24,3200]{1,0:T(8,128)(2,1)S(1)} %get-tuple-element.29), channel_id=1, source_target_pairs={{0,46},{1,47},{2,0},{3,1},{4,2},{5,3},{6,4},{7,5},{8,6},{9,7},{10,... | collective-permute-start | bytes 460808 | tf_op jit(solution)/shard_map/ppermute | solution.py:201
  176.0 1.9 collective-permute-start.12
  178.0 3.8 %collective-permute-done.10 = bf16[24,3200]{1,0:T(8,128)(2,1)S(1)} collective-permute-done((bf16[24,3200]{1,0:T(8,128)(2,1)S(1)}, bf16[24,3200]{1,0:T(8,128)(2,1)S(1)}, u32[]{:S(2)}, u32[]{:S(2)}) %collective-permute-start.10) | collective-permute-done | bytes 153632 | tf_op jit(solution)/shard_map/ppermute | solution.py:201
  181.7 6.7 %collective-permute-done.12 = bf16[24,3200]{1,0:T(8,128)(2,1)S(1)} collective-permute-done((bf16[24,3200]{1,0:T(8,128)(2,1)S(1)}, bf16[24,3200]{1,0:T(8,128)(2,1)S(1)}, u32[]{:S(2)}, u32[]{:S(2)}) %collective-permute-start.12) | collective-permute-done | bytes 153632 | tf_op jit(solution)/shard_map/ppermute | solution.py:201
  188.4 0.0 copy-done.5
  188.4 0.0 copy-done.6
  188.4 0.8 fusion.48
  (8 shorter events, 0.1 us)
Async XLA Ops:
  6.5 134.5 %all-gather.2.cloned.1.call-start = ((), (), s32[]{:S(2)}) async-start(), calls=%async_computation.1 | async-start | bytes 8448000 | tf_op jit(solution)/shard_map/all_gather | solution.py:218
  6.5 17.9 %copy-start.1 = (s32[1,64]{1,0:T(1,128)S(1)}, s32[1,64]{1,0:T(1,128)}, u32[]{:S(2)}) copy-start(s32[1,64]{1,0:T(1,128)} %live_ref) | copy-start | bytes 772
  6.5 17.9 %copy-start = (bf16[1,64,3200]{2,1,0:T(8,128)(2,1)S(1)}, bf16[1,64,3200]{2,1,0:T(8,128)(2,1)}, u32[]{:S(2)}) copy-start(bf16[1,64,3200]{2,1,0:T(8,128)(2,1)} %param.11) | copy-start | bytes 1228804
  6.5 17.9 %copy-start.2 = (s32[1,64]{1,0:T(1,128)S(1)}, s32[1,64]{1,0:T(1,128)}, u32[]{:S(2)}) copy-start(s32[1,64]{1,0:T(1,128)} %order_ref.1) | copy-start | bytes 772
  8.7 36.8 %collective-permute-start.7 = (bf16[40,3200]{1,0:T(8,128)(2,1)S(1)}, bf16[40,3200]{1,0:T(8,128)(2,1)S(1)}, u32[]{:S(2)}, u32[]{:S(2)}) collective-permute-start(bf16[40,3200]{1,0:T(8,128)(2,1)S(1)} %shard_map.91), channel_id=1, source_target_pairs={{0,8},{1,9},{2,10},{3,11},{4,12},{5,13},{6,14},{7,15},{8,32},{9,33... | collective-permute-start | bytes 768008 | tf_op jit(solution)/shard_map/ppermute | solution.py:208
  24.8 49.0 %copy-start.7 = (f32[640]{0:T(1024)S(1)}, f32[640]{0:T(1024)}, u32[]{:S(2)}) copy-start(f32[640]{0:T(1024)} %param.16) | copy-start | bytes 7684
  45.4 44.4 %copy-start.4 = (f32[3200]{0:T(1024)S(1)}, f32[3200]{0:T(1024)}, u32[]{:S(2)}) copy-start(f32[3200]{0:T(1024)} %param.14) | copy-start | bytes 38404
  45.5 0.7 copy-start.3
  46.4 43.1 %collective-permute-start = (bf16[24,3200]{1,0:T(8,128)(2,1)S(1)}, bf16[24,3200]{1,0:T(8,128)(2,1)S(1)}, u32[]{:S(2)}, u32[]{:S(2)}) collective-permute-start(bf16[24,3200]{1,0:T(8,128)(2,1)S(1)} %convolution_convert_fusion), channel_id=1, source_target_pairs={{0,32},{1,33},{2,34},{3,35},{4,36},{5,37},{6,38},{7,39},{8,40},{9,... | collective-permute-start | bytes 460808 | tf_op jit(solution)/shard_map/ppermute | solution.py:201
  73.9 15.6 %collective-permute-start.1 = (f32[640]{0:T(1024)S(1)}, f32[640]{0:T(1024)S(1)}, u32[]{:S(2)}, u32[]{:S(2)}) collective-permute-start(f32[640]{0:T(1024)S(1)} %copy-done.7), channel_id=1, source_target_pairs={{0,8},{1,9},{2,10},{3,11},{4,12},{5,13},{6,14},{7,15},{8,32},{9,33... | collective-permute-start | bytes 7688 | tf_op jit(solution)/shard_map/ppermute | solution.py:201
  90.0 12.9 %collective-permute-start.5 = (bf16[24,3200]{1,0:T(8,128)(2,1)S(1)}, bf16[24,3200]{1,0:T(8,128)(2,1)S(1)}, u32[]{:S(2)}, u32[]{:S(2)}) collective-permute-start(bf16[24,3200]{1,0:T(8,128)(2,1)S(1)} %fusion.15), channel_id=1, source_target_pairs={{0,46},{1,47},{2,0},{3,1},{4,2},{5,3},{6,4},{7,5},{8,6},{9,7},{10,... | collective-permute-start | bytes 460808 | tf_op jit(solution)/shard_map/ppermute | solution.py:201
  96.3 10.3 %collective-permute-start.2 = (bf16[24,3200]{1,0:T(8,128)(2,1)S(1)}, bf16[24,3200]{1,0:T(8,128)(2,1)S(1)}, u32[]{:S(2)}, u32[]{:S(2)}) collective-permute-start(bf16[24,3200]{1,0:T(8,128)(2,1)S(1)} %fusion.15), channel_id=1, source_target_pairs={{0,2},{1,3},{2,4},{3,5},{4,6},{5,7},{6,8},{7,9},{8,10},{9,11},{10,... | collective-permute-start | bytes 460808 | tf_op jit(solution)/shard_map/ppermute | solution.py:201
  106.7 13.6 %collective-permute-start.3 = (bf16[48,3200]{1,0:T(8,128)(2,1)S(1)}, bf16[48,3200]{1,0:T(8,128)(2,1)S(1)}, u32[]{:S(2)}, u32[]{:S(2)}) collective-permute-start(bf16[48,3200]{1,0:T(8,128)(2,1)S(1)} %get-tuple-element.34), channel_id=1, source_target_pairs={{0,1},{1,2},{2,3},{3,4},{4,5},{5,6},{6,7},{7,8},{8,9},{9,10},{10,1... | collective-permute-start | bytes 921608 | tf_op jit(solution)/shard_map/ppermute | solution.py:201
  114.3 17.4 %collective-permute-start.6 = (bf16[48,3200]{1,0:T(8,128)(2,1)S(1)}, bf16[48,3200]{1,0:T(8,128)(2,1)S(1)}, u32[]{:S(2)}, u32[]{:S(2)}) collective-permute-start(bf16[48,3200]{1,0:T(8,128)(2,1)S(1)} %get-tuple-element.33), channel_id=1, source_target_pairs={{0,47},{1,0},{2,1},{3,2},{4,3},{5,4},{6,5},{7,6},{8,7},{9,8},{10,9... | collective-permute-start | bytes 921608 | tf_op jit(solution)/shard_map/ppermute | solution.py:201
  116.9 14.1 %collective-permute-start.4 = (bf16[24,3200]{1,0:T(8,128)(2,1)S(1)}, bf16[24,3200]{1,0:T(8,128)(2,1)S(1)}, u32[]{:S(2)}, u32[]{:S(2)}) collective-permute-start(bf16[24,3200]{1,0:T(8,128)(2,1)S(1)} %collective-permute-done.2), channel_id=1, source_target_pairs={{0,2},{1,3},{2,4},{3,5},{4,6},{5,7},{6,8},{7,9},{8,10},{9,11},{10,... | collective-permute-start | bytes 460808 | tf_op jit(solution)/shard_map/ppermute | solution.py:201
  149.5 38.9 %copy-start.5 = (f32[3200]{0:T(1024)S(1)}, f32[3200]{0:T(1024)}, u32[]{:S(2)}) copy-start(f32[3200]{0:T(1024)} %param.18) | copy-start | bytes 38404
  149.5 38.9 %copy-start.6 = (f32[3200]{0:T(1024)S(1)}, f32[3200]{0:T(1024)}, u32[]{:S(2)}) copy-start(f32[3200]{0:T(1024)} %param.19) | copy-start | bytes 38404
  149.6 19.9 %collective-permute-start.8 = (bf16[48,3200]{1,0:T(8,128)(2,1)S(1)}, bf16[48,3200]{1,0:T(8,128)(2,1)S(1)}, u32[]{:S(2)}, u32[]{:S(2)}) collective-permute-start(bf16[48,3200]{1,0:T(8,128)(2,1)S(1)} %get-tuple-element.31), channel_id=1, source_target_pairs={{0,47},{1,0},{2,1},{3,2},{4,3},{5,4},{6,5},{7,6},{8,7},{9,8},{10,9... | collective-permute-start | bytes 921608 | tf_op jit(solution)/shard_map/ppermute | solution.py:201
  154.4 15.1 %collective-permute-start.11 = (bf16[48,3200]{1,0:T(8,128)(2,1)S(1)}, bf16[48,3200]{1,0:T(8,128)(2,1)S(1)}, u32[]{:S(2)}, u32[]{:S(2)}) collective-permute-start(bf16[48,3200]{1,0:T(8,128)(2,1)S(1)} %get-tuple-element.32), channel_id=1, source_target_pairs={{0,1},{1,2},{2,3},{3,4},{4,5},{5,6},{6,7},{7,8},{8,9},{9,10},{10,1... | collective-permute-start | bytes 921608 | tf_op jit(solution)/shard_map/ppermute | solution.py:201
  156.3 13.1 %collective-permute-start.9 = (bf16[24,3200]{1,0:T(8,128)(2,1)S(1)}, bf16[24,3200]{1,0:T(8,128)(2,1)S(1)}, u32[]{:S(2)}, u32[]{:S(2)}) collective-permute-start(bf16[24,3200]{1,0:T(8,128)(2,1)S(1)} %slice.47), channel_id=1, source_target_pairs={{0,46},{1,47},{2,0},{3,1},{4,2},{5,3},{6,4},{7,5},{8,6},{9,7},{10,... | collective-permute-start | bytes 460808 | tf_op jit(solution)/shard_map/ppermute | solution.py:201
  169.6 12.2 %collective-permute-start.10 = (bf16[24,3200]{1,0:T(8,128)(2,1)S(1)}, bf16[24,3200]{1,0:T(8,128)(2,1)S(1)}, u32[]{:S(2)}, u32[]{:S(2)}) collective-permute-start(bf16[24,3200]{1,0:T(8,128)(2,1)S(1)} %get-tuple-element.29), channel_id=1, source_target_pairs={{0,46},{1,47},{2,0},{3,1},{4,2},{5,3},{6,4},{7,5},{8,6},{9,7},{10,... | collective-permute-start | bytes 460808 | tf_op jit(solution)/shard_map/ppermute | solution.py:201
  176.0 12.4 %collective-permute-start.12 = (bf16[24,3200]{1,0:T(8,128)(2,1)S(1)}, bf16[24,3200]{1,0:T(8,128)(2,1)S(1)}, u32[]{:S(2)}, u32[]{:S(2)}) collective-permute-start(bf16[24,3200]{1,0:T(8,128)(2,1)S(1)} %get-tuple-element.30), channel_id=1, source_target_pairs={{0,2},{1,3},{2,4},{3,5},{4,6},{5,7},{6,8},{7,9},{8,10},{9,11},{10,... | collective-permute-start | bytes 460808 | tf_op jit(solution)/shard_map/ppermute | solution.py:201
Sparse Core Ops, SparseCore 0:
  46.3 92.0 all-gather.1
